TPU v7x, 256 devices: a whole 4x4x8 slice. The times are simulated.
256 devices in a mesh: blk: 32 (over x_hi, z, core), feat: 8 (over x_lo, y).
Axes of the slice: x: 4 (x_hi: 2, x_lo: 2; x = x_hi * 2 + x_lo), y: 4, z: 8, core: 2. Of those that a mesh axis runs over, the one named last changes fastest.
Arguments:
- pool_embed: bfloat16 [262144, 1536], P('blk', 'feat'), may hold values from -16 to 16
- label_embed: bfloat16 [2048, 1536], P('blk', 'feat'), may hold values from -4 to 4
- label_class: int32 [2048], P('blk'), may hold values from 0 to 999
Outputs:
- log_probs: float32 [262144, 1000], P(('blk', 'feat'))
- entropy: float32 [262144], P(('blk', 'feat'))
All inputs are finite; a program needn't handle non-finite values.
Results may differ from a plain program's by a relative error of at most 0.0009.
Values may be sent and summed in bfloat16 or wider, within the bound.
No kernel may reach another device: no remote copies, remote signals or barrier semaphores. Data moves between devices by JAX's collectives and lax.ppermute only.
A program may use at most 64 MiB of HBM per device.

v0:
```python
import math

import jax
import jax.numpy as jnp
from jax import lax
from jax.sharding import PartitionSpec as P

C = 1000


SMOOTHING = 0.1


def per_device(pool_embed, label_embed, label_class):
    pool_rows = lax.all_to_all(pool_embed, "feat", split_axis=0, concat_axis=1, tiled=True)
    key_rows = lax.all_gather(label_embed, "feat", axis=1, tiled=True)
    width = pool_rows.shape[1]
    scale = 2.0 / math.sqrt(width)
    count = pool_rows.shape[0]
    class_ids = jnp.arange(C, dtype=jnp.int32)
    run_max = jnp.full((count,), -1e30, jnp.float32)
    key_piece = lax.all_gather(key_rows, "blk", axis=0, tiled=True)
    class_piece = lax.all_gather(label_class, "blk", axis=0, tiled=True)
    scores = (
        lax.dot_general(
            pool_rows, key_piece, (((1,), (1,)), ((), ())), preferred_element_type=jnp.float32
        )
        * scale
    )
    new_max = jnp.maximum(run_max, jnp.max(scores, axis=1))
    weights = jnp.exp(scores - new_max[:, None])
    onehot = (class_piece[:, None] == class_ids[None, :]).astype(jnp.bfloat16)
    weight_sum = jnp.sum(weights, axis=1)
    class_mass = jnp.dot(weights.astype(jnp.bfloat16), onehot, preferred_element_type=jnp.float32)
    final = (new_max, weight_sum, class_mass)
    run_max, weight_sum, class_mass = final
    probability = (1.0 - SMOOTHING) * class_mass / weight_sum[:, None] + SMOOTHING / C
    log_probs = jnp.log(probability)
    entropy = -jnp.sum(probability * log_probs, axis=1)
    return (log_probs, entropy)


def solution(mesh):
    placed = (P("blk", "feat"), P("blk", "feat"), P("blk"))
    return jax.shard_map(
        per_device,
        mesh=mesh,
        in_specs=placed,
        out_specs=(P(("blk", "feat"), None), P(("blk", "feat"))),
        check_vma=False,
    )
```

profile of v0, /device:TPU:1, one launch (start us, length us, event | category | flops | bytes accessed | tf_op | source)
XLA Modules:
  0.0 162.0 jit_solution(10843462604677200588)
XLA Ops:
  7.2 0.0 all-gather.3.cloned.1.call-start
  7.2 24.1 %all-gather = bf16[8,192,64]{1,2,0:T(8,128)(2,1)S(1)} all-gather(bf16[1,192,64]{1,2,0:T(8,128)(2,1)} %bitcast.19), channel_id=1, replica_groups=mesh['blk'=32,'feat'=8] {'feat'}, dimensions={0}, use_global_device_ids=true | all-gather | bytes 221184 | tf_op jit(solution)/shard_map/all_gather | solution.py:16
  31.3 0.1 copy.9
  31.4 0.9 reshape.16
  32.3 0.0 all-gather.3.cloned.1.call-update
  32.3 0.0 copy-start.1
  32.4 0.0 copy-start
  32.4 4.0 %copy.12 = bf16[24,8,8,1024]{3,2,0,1:T(8,128)(2,1)} copy(bf16[24,8,8,1024]{3,2,1,0:T(8,128)(2,1)} %bitcast.16) | data formatting | bytes 6291456 | tf_op jit(solution)/shard_map/all_to_all | solution.py:15
  36.4 4.4 %all-to-all-start = ((bf16[8,1024,192]{1,2,0:T(8,128)(2,1)}), bf16[8,1024,192]{1,2,0:T(8,128)(2,1)S(1)}, u32[]{:S(2)}, u32[]{:S(2)}) async-start(bf16[8,1024,192]{1,2,0:T(8,128)(2,1)} %bitcast.15), calls=%async_computation | async-start | bytes 6291456 | tf_op jit(solution)/shard_map/all_to_all | solution.py:15
  40.7 0.0 copy-done.1
  40.7 0.6 dynamic-slice
  42.0 0.0 copy-done
  42.0 0.3 dynamic-update-slice
  42.3 30.7 %all-reduce = s32[2048]{0:T(1024)S(1)} all-reduce(s32[2048]{0:T(1024)S(1)} %dynamic-update-slice), channel_id=1, replica_groups=mesh['blk'=32,'feat'=8] {'blk'}, use_global_device_ids=true, to_apply=%add | all-reduce | flops 2048 | bytes 16384
  73.0 0.4 all-to-all-done
  73.4 62.5 %all-gather.3.cloned.1.call-done = bf16[2048,1536]{1,0:T(8,128)(2,1)} async-done(((bf16[64,1536]{1,0:T(8,128)(2,1)}), bf16[2048,1536]{1,0:T(8,128)(2,1)}) %all-gather.3.cloned.1.call-update) | async-done | bytes 6291472 | tf_op jit(solution)/shard_map/all_gather | solution.py:22
  135.9 9.0 %multiply_reduce_fusion = (f32[1024]{0:T(1024)S(1)}, f32[1024,2048]{1,0:T(8,128)S(1)}) fusion(bf16[1024,1536]{0,1:T(8,128)(2,1)S(1)} %bitcast.17, bf16[2048,1536]{1,0:T(8,128)(2,1)} %all-gather.3.cloned.1.call-done), kind=kOutput, calls=%fused_computation.3 | convolution fusion | flops 6446644224 | bytes 17829888 | tf_op jit(solution)/shard_map/dot_general | solution.py:25
  144.9 1.9 %fusion.1 = f32[1024]{0:T(1024)S(1)} fusion(f32[1024,2048]{1,0:T(8,128)S(1)} %get-tuple-element.5, f32[1024]{0:T(1024)S(1)} %broadcast_maximum_fusion), kind=kLoop, calls=%fused_computation.4 | loop fusion | flops 6290432 | bytes 8396800 | tf_op jit(solution)/shard_map/reduce_sum | solution.py:33
  146.8 7.8 %multiply_reduce_fusion.1 = (f32[1024]{0:T(1024)S(1)}, f32[1024,1000]{0,1:T(8,128)}) fusion(f32[1024]{0:T(1024)S(1)} %fusion.1, s32[2048]{0:T(1024)S(1)} %all-reduce, f32[1024,2048]{1,0:T(8,128)S(1)} %get-tuple-element.5, f32[1024]{0:T(1024)S(1)} %broadcast_maximum_fusion), kind=kOutput, calls=%fused_computation.9 | convolution fusion | flops 4207762432 | bytes 12505088 | tf_op jit(solution)/shard_map/dot_general | solution.py:34
  154.6 0.6 neg.3
  (2 shorter events, 0.0 us)
Async XLA Ops:
  7.2 128.7 %all-gather.3.cloned.1.call-start = ((), (), s32[]{:S(2)}) async-start(), calls=%async_computation.1 | async-start | bytes 6488064 | tf_op jit(solution)/shard_map/all_gather | solution.py:22
  32.3 8.4 %copy-start.1 = (u32[256]{0:T(256)S(1)}, u32[256]{0:T(256)}, u32[]{:S(2)}) copy-start(u32[256]{0:T(256)} %constant.14) | copy-start | bytes 3076
  32.4 9.6 %copy-start = (s32[64]{0:T(128)S(1)}, s32[64]{0:T(128)}, u32[]{:S(2)}) copy-start(s32[64]{0:T(128)} %param.5) | copy-start | bytes 772
  36.4 37.0 %all-to-all-start = ((bf16[8,1024,192]{1,2,0:T(8,128)(2,1)}), bf16[8,1024,192]{1,2,0:T(8,128)(2,1)S(1)}, u32[]{:S(2)}, u32[]{:S(2)}) async-start(bf16[8,1024,192]{1,2,0:T(8,128)(2,1)} %bitcast.15), calls=%async_computation | async-start | bytes 6291456 | tf_op jit(solution)/shard_map/all_to_all | solution.py:15
Sparse Core Ops, SparseCore 0:
  32.5 103.3 all-gather.2
where the time goes:
time: 162 us
  waiting for transfers between devices  62.9 us (39%)
  blocking collectives  54.7 us (34%)
  matrix products  16.7 us (10%)
  between operations  14.7 us (9%)
  local copies, waits for them, and re-layouts  5.93 us (4%)
  starting transfers between devices  4.41 us (3%)
  other arithmetic  2.53 us (2%)
    all_gather x1, waiting for transfers between devices, per_device(): key_piece = lax.all_gather(key_rows, 'blk', axis=0, tiled=True)  62.5 us
    unnamed x1, blocking collectives  30.7 us
    all_gather x1, blocking collectives, per_device(): key_rows = lax.all_gather(label_embed, 'feat', axis=1, tiled=True)  24.1 us
    dot_general x1, matrix products, per_device(): lax.dot_general(pool_rows, key_piece, (((1,), (1,)), ((), ())), preferred...  8.99 us
    dot_general x1, matrix products, per_device(): jnp.dot(weights.astype(jnp.bfloat16), onehot, preferred_element_type=jnp....  7.75 us
    all_to_all x1, starting transfers between devices, per_device(): lax.all_to_all(pool_embed, 'feat', split_axis=0, concat_axis=1, tiled=True)  4.37 us
    all_to_all x1, local copies, waits for them, and re-layouts, per_device(): lax.all_to_all(pool_embed, 'feat', split_axis=0, concat_axis=1, tiled=True)  4 us
  transfers between devices with their start and end apart: 2, of which 2 were waited for; matrix products, arithmetic and copies ran while one was open for 3% of the time, Pallas kernels for 0%

commit v1 on v0

v1 whole, which is shorter than its diff:
```python
import functools
import math

import jax
import jax.numpy as jnp
from jax import lax
from jax.experimental import pallas as pl
from jax.experimental.pallas import tpu as pltpu
from jax.sharding import Mesh, PartitionSpec as P

C = 1000
SMOOTHING = 0.1
AXES = ("xh", "z", "c", "xl", "y")
SIZES = (2, 8, 2, 2, 4)
PLANE = ("xh", "xl", "y")
FEAT = ("xl", "y")
LANES = 128
TAIL = 16


def shift(x, step):
    n = SIZES[1]
    return lax.ppermute(x, "z", [(i, (i + step) % n) for i in range(n)])


def swap(x):
    return lax.ppermute(x, "c", [(0, 1), (1, 0)])


def arrange_kernel(parts_ref, out_ref):
    half = parts_ref.shape[1]
    rows = 2 * half
    for xh in range(2):
        for j in range(4):
            even = parts_ref[xh * 8 + 2 * j]
            odd = parts_ref[xh * 8 + 2 * j + 1]
            blocks = (
                even[:, :128],
                jnp.concatenate([even[:, 128:192], odd[:, :64]], axis=1),
                odd[:, 64:192],
            )
            for k, block in enumerate(blocks):
                at = (3 * j + k) * rows + xh * half
                out_ref[at : at + half, :] = block
    out_ref[12 * rows :, :] = jnp.concatenate(
        [parts_ref[0, :TAIL, 192:], parts_ref[8, :TAIL, 192:]], axis=1
    )


def arrange(parts):
    rows = 12 * 2 * parts.shape[1] + TAIL
    return pl.pallas_call(
        arrange_kernel,
        out_shape=jax.ShapeDtypeStruct((rows, LANES), parts.dtype),
        cost_estimate=pl.CostEstimate(
            flops=0, bytes_accessed=4 * rows * LANES, transcendentals=0
        ),
    )(parts)


def attend_kernel(pieces, first, last, scale, *refs):
    labels = refs[:pieces]
    pool_ref = refs[pieces]
    refs = refs[pieces + 1 :]
    if not first:
        old_mass, old_stat = refs[:2]
        refs = refs[2:]
    out_ref, stat_ref, keys, onehot = refs
    rows = 128

    @pl.when(pl.program_id(0) == 0)
    def _():
        classes = lax.broadcasted_iota(jnp.int32, (C, rows), 0).astype(jnp.float32)
        for p, ref in enumerate(labels):
            for k in range(12):
                keys[p * rows : (p + 1) * rows, k * 128 : (k + 1) * 128] = ref[
                    k * rows : (k + 1) * rows, :
                ]
            tail = ref[12 * rows :, :].astype(jnp.float32)
            own = tail[0:1] * 32.0 + tail[1:2]
            onehot[:, p * rows : (p + 1) * rows] = jnp.where(
                classes == own, 1.0, 0.0
            ).astype(jnp.bfloat16)

    scores = (
        jnp.dot(keys[...], pool_ref[...], preferred_element_type=jnp.float32) * scale
    )
    top = jnp.max(scores, axis=0, keepdims=True)
    if not first:
        top = jnp.maximum(top, old_stat[0:1])
    weights = jnp.exp(scores - top)
    total = jnp.sum(weights, axis=0, keepdims=True)
    mass = jnp.dot(
        onehot[...], weights.astype(jnp.bfloat16), preferred_element_type=jnp.float32
    )
    if not first:
        fade = jnp.exp(old_stat[0:1] - top)
        total = total + fade * old_stat[1:2]
        mass = mass + fade * old_mass[...]
    if last:
        probability = mass * ((1.0 - SMOOTHING) / total) + SMOOTHING / C
        log_probs = jnp.log(probability)
        out_ref[...] = log_probs
        stat_ref[0:1] = -jnp.sum(probability * log_probs, axis=0, keepdims=True)
    else:
        out_ref[...] = mass
        stat_ref[0:1] = top
        stat_ref[1:2] = total


def attend(pool, labels, state, last, tile=256):
    depth, count = pool.shape
    pieces = len(labels)
    first = state is None
    m = pieces * 128
    mass_spec = pl.BlockSpec((C, tile), lambda i: (0, i))
    stat_spec = pl.BlockSpec((8, tile), lambda i: (0, i))
    in_specs = [pl.BlockSpec(labels[0].shape, lambda i: (0, 0))] * pieces
    in_specs.append(pl.BlockSpec((depth, tile), lambda i: (0, i)))
    args = list(labels) + [pool]
    if not first:
        in_specs += [mass_spec, stat_spec]
        args += list(state)
    return pl.pallas_call(
        functools.partial(
            attend_kernel, pieces, first, last, 2.0 / math.sqrt(depth)
        ),
        grid=(count // tile,),
        in_specs=in_specs,
        out_specs=[mass_spec, stat_spec],
        out_shape=[
            jax.ShapeDtypeStruct((C, count), jnp.float32),
            jax.ShapeDtypeStruct((8, count), jnp.float32),
        ],
        scratch_shapes=[
            pltpu.VMEM((m, depth), jnp.bfloat16),
            pltpu.VMEM((C, m), jnp.bfloat16),
        ],
        compiler_params=pltpu.CompilerParams(vmem_limit_bytes=40 * 2**20),
        cost_estimate=pl.CostEstimate(
            flops=2 * m * count * (depth + C),
            bytes_accessed=m * depth * 2 + depth * count * 2 + 4 * C * count,
            transcendentals=m * count,
        ),
    )(*args)


def per_device(pool_embed, label_embed, label_class):
    feats = 8
    width = pool_embed.shape[1]
    count = pool_embed.shape[0] // feats
    rows = label_embed.shape[0]
    codes = jnp.stack([label_class // 32, label_class % 32]).astype(jnp.bfloat16)
    side = jnp.concatenate([codes, jnp.zeros((rows - 2, rows), jnp.bfloat16)], axis=0)
    own = jnp.concatenate([label_embed, side], axis=1)
    parts = lax.all_to_all(
        jnp.broadcast_to(own[None], (16,) + own.shape), PLANE, 0, 0, tiled=True
    )
    queries = pool_embed.T.reshape(width, feats, count).transpose(1, 0, 2)
    pool = lax.all_to_all(queries, FEAT, 0, 0, tiled=True).reshape(
        feats * width, count
    )
    near = arrange(parts)
    got = [near, swap(near)]
    up, down = near, near
    for _ in range(2):
        up, down = shift(up, 1), shift(down, -1)
        got += [up, down, swap(up), swap(down)]
    state = attend(pool, got, None, False)
    up, down = shift(up, 1), shift(down, -1)
    state = attend(pool, [up, down, swap(up), swap(down)], state, False)
    n = SIZES[1]
    far = jnp.where(lax.axis_index("c") == 0, down, up)
    same = [(2 * i, 2 * ((i - 1) % n)) for i in range(n)]
    same += [(2 * i + 1, 2 * ((i + 1) % n) + 1) for i in range(n)]
    cross = [(a, b ^ 1) for a, b in same]
    ends = [lax.ppermute(far, ("z", "c"), pairs) for pairs in (same, cross)]
    log_probs, stat = attend(pool, ends, state, True)
    return (log_probs.T, stat[0])


def solution(mesh):
    fine = Mesh(mesh.devices.reshape(SIZES), AXES)
    blk, feat = ("xh", "z", "c"), FEAT
    return jax.shard_map(
        per_device,
        mesh=fine,
        in_specs=(P(blk, feat), P(blk, feat), P(blk)),
        out_specs=(P(blk + feat, None), P(blk + feat)),
        check_vma=False,
    )
```

time: 162 us -> 114 us (0.70)
  blocking collectives: 54.7 us -> 0 us
  waiting for transfers between devices: 62.9 us -> 21.4 us
  Pallas kernels: 0 us -> 34.6 us
  starting transfers between devices: 4.41 us -> 35.8 us
  matrix products: 16.7 us -> 0 us
  between operations: 14.7 us -> 0.75 us
  local copies, waits for them, and re-layouts: 5.93 us -> 18 us
    all_gather x1 -> x0, waiting for transfers between devices: 62.5 us -> none  [per_device(): key_piece = lax.all_gather(key_rows, 'blk', axis=0, tiled=True)]
    pallas_call x0 -> x4, Pallas kernels: none -> 34.6 us  [the longest x3 32.6 us: attend(): pl.pallas_call(functools.partial(attend_kernel, pieces, first, last, 2.0...]
    unnamed x1 -> x0, blocking collectives: 30.7 us -> none
    ppermute x0 -> x15, starting transfers between devices: none -> 24.6 us  [the longest x6 10.9 us: shift(): return lax.ppermute(x, 'z', [(i, (i + step) % n) for i in range(n)])]
    all_gather x1 -> x0, blocking collectives: 24.1 us -> none  [per_device(): key_rows = lax.all_gather(label_embed, 'feat', axis=1, tiled=True)]
    dot_general x2 -> x0, matrix products: 16.7 us -> none  [the longest x1 8.99 us: per_device(): lax.dot_general(pool_rows, key_piece, (((1,), (1,)), ((), ())), preferred...]
    ppermute x0 -> x15, waiting for transfers between devices: none -> 15.1 us  [the longest x6 15.1 us: shift(): return lax.ppermute(x, 'z', [(i, (i + step) % n) for i in range(n)])]
    unnamed x8 -> x32, local copies, waits for them, and re-layouts: 1.78 us -> 12.6 us
  transfers between devices with their start and end apart: 2 -> 17, of which waited for: 2 -> 4; matrix products, arithmetic and copies ran while one was open for 3% -> 4% of each run, Pallas kernels for 0% -> 25%
where the time goes in v1:
time: 114 us; the launch traced here: 113 us
  starting transfers between devices  35.8 us (31%)
  Pallas kernels  34.6 us (30%)
  waiting for transfers between devices  21.4 us (19%)
  local copies, waits for them, and re-layouts  18 us (16%)
  other arithmetic  2.33 us (2%)
    pallas_call x3, Pallas kernels, attend(): pl.pallas_call(functools.partial(attend_kernel, pieces, first, last, 2.0...  32.6 us
    ppermute x6, waiting for transfers between devices, shift(): return lax.ppermute(x, 'z', [(i, (i + step) % n) for i in range(n)])  15.1 us
    unnamed x32, local copies, waits for them, and re-layouts  12.6 us
    ppermute x6, starting transfers between devices, shift(): return lax.ppermute(x, 'z', [(i, (i + step) % n) for i in range(n)])  10.9 us
    ppermute x7, starting transfers between devices, swap(): return lax.ppermute(x, 'c', [(0, 1), (1, 0)])  10.5 us
    all_to_all x1, starting transfers between devices, per_device(): lax.all_to_all(jnp.broadcast_to(own[None], (16,) + own.shape), PLANE, 0,...  7.58 us
    all_to_all x1, waiting for transfers between devices, per_device(): lax.all_to_all(jnp.broadcast_to(own[None], (16,) + own.shape), PLANE, 0,...  6.31 us
    reshape x1, local copies, waits for them, and re-layouts, per_device(): queries = pool_embed.T.reshape(width, feats, count).transpose(1, 0, 2)  3.99 us
  transfers between devices with their start and end apart: 17, of which 4 were waited for; matrix products, arithmetic and copies ran while one was open for 4% of the time, Pallas kernels for 25%

profile of v1, /device:TPU:1, one launch (start us, length us, event | category | flops | bytes accessed | tf_op | source)
XLA Modules:
  0.0 112.9 jit_solution(17828733144727723969)
XLA Ops:
  3.0 7.6 %all-to-all-start = ((bf16[16,64,256]{2,1,0:T(8,128)(2,1)}), bf16[16,64,256]{2,1,0:T(8,128)(2,1)S(1)}, u32[]{:S(2)}, u32[]{:S(2)}) async-start(bf16[16,64,256]{2,1,0:T(8,128)(2,1)} %broadcast_in_dim.2), calls=%async_computation | async-start | bytes 1048576 | tf_op jit(solution)/shard_map/all_to_all | solution.py:156
  10.6 4.0 %copy.8 = bf16[24,8,8,1024]{3,2,0,1:T(8,128)(2,1)} copy(bf16[24,8,8,1024]{3,2,1,0:T(8,128)(2,1)} %bitcast.19) | data formatting | bytes 6291456 | tf_op jit(solution)/shard_map/reshape | solution.py:159
  14.6 6.3 %all-to-all-done.parts_ref = bf16[16,64,256]{2,1,0:T(8,128)(2,1)S(1)} async-done(((bf16[16,64,256]{2,1,0:T(8,128)(2,1)}), bf16[16,64,256]{2,1,0:T(8,128)(2,1)S(1)}, u32[]{:S(2)}, u32[]{:S(2)}) %all-to-all-start) | async-done | bytes 524320 | tf_op jit(solution)/shard_map/all_to_all | solution.py:156
  21.7 3.7 %all-to-all-start.1 = ((bf16[8,192,1024]{2,1,0:T(8,128)(2,1)}), bf16[8,192,1024]{2,1,0:T(8,128)(2,1)S(1)}, u32[]{:S(2)}, u32[]{:S(2)}) async-start(bf16[8,192,1024]{2,1,0:T(8,128)(2,1)} %bitcast.18), calls=%async_computation.1 | async-start | bytes 6291456 | tf_op jit(solution)/shard_map/all_to_all | solution.py:160
  25.3 2.0 %shard_map.50.refs_0_ = bf16[1552,128]{1,0:T(8,128)(2,1)} custom-call(bf16[16,64,256]{2,1,0:T(8,128)(2,1)} %copy-done.15), custom_call_target="tpu_custom_call" | custom-call | bytes 794624 | tf_op jit(solution)/shard_map/pallas_call | solution.py:52
  27.3 1.6 %collective-permute-start.3 = (bf16[1552,128]{1,0:T(8,128)(2,1)}, bf16[1552,128]{1,0:T(8,128)(2,1)S(1)}, u32[]{:S(2)}, u32[]{:S(2)}) collective-permute-start(bf16[1552,128]{1,0:T(8,128)(2,1)} %shard_map.50.refs_0_), channel_id=1, source_target_pairs={{0,16},{16,32},{32,48},{48,64},{64,80},{80,96},{96,112},{112,0},{1... | collective-permute-start | bytes 1191944 | tf_op jit(solution)/shard_map/ppermute | solution.py:23
  29.0 3.9 %collective-permute-start = (bf16[1552,128]{1,0:T(8,128)(2,1)}, bf16[1552,128]{1,0:T(8,128)(2,1)S(1)}, u32[]{:S(2)}, u32[]{:S(2)}) collective-permute-start(bf16[1552,128]{1,0:T(8,128)(2,1)} %shard_map.50.refs_0_), channel_id=1, source_target_pairs={{0,112},{16,0},{32,16},{48,32},{64,48},{80,64},{96,80},{112,96},{1... | collective-permute-start | bytes 1191944 | tf_op jit(solution)/shard_map/ppermute | solution.py:23
  32.9 7.6 %collective-permute-done.3.refs_2_ = bf16[1552,128]{1,0:T(8,128)(2,1)S(1)} collective-permute-done((bf16[1552,128]{1,0:T(8,128)(2,1)}, bf16[1552,128]{1,0:T(8,128)(2,1)S(1)}, u32[]{:S(2)}, u32[]{:S(2)}) %collective-permute-start.3) | collective-permute-done | bytes 397344 | tf_op jit(solution)/shard_map/ppermute | solution.py:23
  40.5 2.7 %collective-permute-start.1 = (bf16[1552,128]{1,0:T(8,128)(2,1)S(1)}, bf16[1552,128]{1,0:T(8,128)(2,1)}, u32[]{:S(2)}, u32[]{:S(2)}) collective-permute-start(bf16[1552,128]{1,0:T(8,128)(2,1)S(1)} %collective-permute-done.refs_3_), channel_id=1, source_target_pairs={{0,112},{16,0},{32,16},{48,32},{64,48},{80,64},{96,80},{112,96},{1... | collective-permute-start | bytes 1191944 | tf_op jit(solution)/shard_map/ppermute | solution.py:23
  43.2 6.5 %collective-permute-done.4.refs_6_ = bf16[1552,128]{1,0:T(8,128)(2,1)} collective-permute-done((bf16[1552,128]{1,0:T(8,128)(2,1)S(1)}, bf16[1552,128]{1,0:T(8,128)(2,1)}, u32[]{:S(2)}, u32[]{:S(2)}) %collective-permute-start.4) | collective-permute-done | bytes 397344 | tf_op jit(solution)/shard_map/ppermute | solution.py:23
  49.7 2.7 %collective-permute-start.2 = (bf16[1552,128]{1,0:T(8,128)(2,1)}, bf16[1552,128]{1,0:T(8,128)(2,1)}, u32[]{:S(2)}, u32[]{:S(2)}) collective-permute-start(bf16[1552,128]{1,0:T(8,128)(2,1)} %collective-permute-done.1.refs_7_), channel_id=1, source_target_pairs={{0,112},{16,0},{32,16},{48,32},{64,48},{80,64},{96,80},{112,96},{1... | collective-permute-start | bytes 1191944 | tf_op jit(solution)/shard_map/ppermute | solution.py:23
  52.4 4.3 %collective-permute-start.10 = (bf16[1552,128]{1,0:T(8,128)(2,1)}, bf16[1552,128]{1,0:T(8,128)(2,1)S(1)}, u32[]{:S(2)}, u32[]{:S(2)}) collective-permute-start(bf16[1552,128]{1,0:T(8,128)(2,1)} %shard_map.50.refs_0_), channel_id=1, source_target_pairs={{0,8},{8,0},{1,9},{9,1},{2,10},{10,2},{3,11},{11,3},{4,12},{12,4},... | collective-permute-start | bytes 1191944 | tf_op jit(solution)/shard_map/ppermute | solution.py:27
  58.1 4.6 %collective-permute-start.13 = (bf16[1552,128]{1,0:T(8,128)(2,1)}, bf16[1552,128]{1,0:T(8,128)(2,1)S(1)}, u32[]{:S(2)}, u32[]{:S(2)}) collective-permute-start(bf16[1552,128]{1,0:T(8,128)(2,1)} %collective-permute-done.4.refs_6_), channel_id=1, source_target_pairs={{0,8},{8,0},{1,9},{9,1},{2,10},{10,2},{3,11},{11,3},{4,12},{12,4},... | collective-permute-start | bytes 1191944 | tf_op jit(solution)/shard_map/ppermute | solution.py:27
  65.1 3.1 %collective-permute-start.7 = (bf16[1552,128]{1,0:T(8,128)(2,1)}, bf16[1552,128]{1,0:T(8,128)(2,1)}, u32[]{:S(2)}, u32[]{:S(2)}) collective-permute-start(bf16[1552,128]{1,0:T(8,128)(2,1)} %broadcast_select_fusion), channel_id=1, source_target_pairs={{0,120},{16,8},{32,24},{48,40},{64,56},{80,72},{96,88},{112,104},{... | collective-permute-start | bytes 1191944 | tf_op jit(solution)/shard_map/ppermute | solution.py:177
  69.0 1.1 collective-permute-start.8
  71.7 1.0 copy-done
  72.7 1.0 copy-done.2
  73.6 1.0 copy-done.4
  74.6 1.0 copy-done.6
  75.6 1.0 copy-done.8
  76.6 1.0 copy-done.10
  79.6 16.9 %shard_map.51 = (f32[1000,1024]{1,0:T(8,128)S(1)}, f32[8,1024]{1,0:T(8,128)S(1)}) custom-call(bf16[1552,128]{1,0:T(8,128)(2,1)S(1)} %copy-done, bf16[1552,128]{1,0:T(8,128)(2,1)S(1)} %copy-done.6, bf16[1552,128]{1,0:T(8,128)(2,1)S(1)} %copy-done.2, bf16[1552,128]{1,0:T(8,128)(2,1)S(1)} %copy-done.4, bf16[1552,128]{1,0:T(8,128)(2,1)S(1)} %copy-done.8, ...), custom_call_target="tpu_custom_call" | custom-call | flops 6647971840 | bytes 11173888 | tf_op jit(solution)/shard_map/pallas_call | solution.py:124
  96.6 8.9 %shard_map.52 = (f32[1000,1024]{1,0:T(8,128)S(1)}, f32[8,1024]{1,0:T(8,128)S(1)}) custom-call(bf16[1552,128]{1,0:T(8,128)(2,1)S(1)} %collective-permute-done.5.refs_0_, bf16[1552,128]{1,0:T(8,128)(2,1)} %collective-permute-done.2.refs_1_, bf16[1552,128]{1,0:T(8,128)(2,1)} %collective-permute-done.8.refs_2_, ...), custom_call_target="tpu_custom_call" | custom-call | flops 2659188736 | bytes 8814592 | tf_op jit(solution)/shard_map/pallas_call | solution.py:124
  105.5 6.8 %shard_map.53 = (f32[1000,1024]{1,0:T(8,128)}, f32[8,1024]{1,0:T(8,128)S(1)}) custom-call(bf16[1552,128]{1,0:T(8,128)(2,1)} %collective-permute-done.6.refs_0_, bf16[1552,128]{1,0:T(8,128)(2,1)} %collective-permute-done.7.refs_1_, bf16[1536,1024]{1,0:T(8,128)(2,1)S(1)} %bitcast.17, f32[1000,1024]{1,0:T(8,128)S(1)} %get-tuple-element.10.refs_3_, ...), custom_call_target="tpu_custom_call" | custom-call | flops 1329594368 | bytes 8028160 | tf_op jit(solution)/shard_map/pallas_call | solution.py:124
  (53 shorter events, 11.9 us)
Async XLA Ops:
  3.0 17.9 %all-to-all-start = ((bf16[16,64,256]{2,1,0:T(8,128)(2,1)}), bf16[16,64,256]{2,1,0:T(8,128)(2,1)S(1)}, u32[]{:S(2)}, u32[]{:S(2)}) async-start(bf16[16,64,256]{2,1,0:T(8,128)(2,1)} %broadcast_in_dim.2), calls=%async_computation | async-start | bytes 1048576 | tf_op jit(solution)/shard_map/all_to_all | solution.py:156
  21.7 50.0 %all-to-all-start.1 = ((bf16[8,192,1024]{2,1,0:T(8,128)(2,1)}), bf16[8,192,1024]{2,1,0:T(8,128)(2,1)S(1)}, u32[]{:S(2)}, u32[]{:S(2)}) async-start(bf16[8,192,1024]{2,1,0:T(8,128)(2,1)} %bitcast.18), calls=%async_computation.1 | async-start | bytes 6291456 | tf_op jit(solution)/shard_map/all_to_all | solution.py:160
  27.3 13.2 %collective-permute-start.3 = (bf16[1552,128]{1,0:T(8,128)(2,1)}, bf16[1552,128]{1,0:T(8,128)(2,1)S(1)}, u32[]{:S(2)}, u32[]{:S(2)}) collective-permute-start(bf16[1552,128]{1,0:T(8,128)(2,1)} %shard_map.50.refs_0_), channel_id=1, source_target_pairs={{0,16},{16,32},{32,48},{48,64},{64,80},{80,96},{96,112},{112,0},{1... | collective-permute-start | bytes 1191944 | tf_op jit(solution)/shard_map/ppermute | solution.py:23
  29.0 11.5 %collective-permute-start = (bf16[1552,128]{1,0:T(8,128)(2,1)}, bf16[1552,128]{1,0:T(8,128)(2,1)S(1)}, u32[]{:S(2)}, u32[]{:S(2)}) collective-permute-start(bf16[1552,128]{1,0:T(8,128)(2,1)} %shard_map.50.refs_0_), channel_id=1, source_target_pairs={{0,112},{16,0},{32,16},{48,32},{64,48},{80,64},{96,80},{112,96},{1... | collective-permute-start | bytes 1191944 | tf_op jit(solution)/shard_map/ppermute | solution.py:23
  40.5 2.7 %copy-start.1 = (bf16[1552,128]{1,0:T(8,128)(2,1)}, bf16[1552,128]{1,0:T(8,128)(2,1)S(1)}, u32[]{:S(2)}) copy-start(bf16[1552,128]{1,0:T(8,128)(2,1)S(1)} %collective-permute-done.3.refs_2_) | copy-start | bytes 1191940
  40.5 9.2 %collective-permute-start.4 = (bf16[1552,128]{1,0:T(8,128)(2,1)S(1)}, bf16[1552,128]{1,0:T(8,128)(2,1)}, u32[]{:S(2)}, u32[]{:S(2)}) collective-permute-start(bf16[1552,128]{1,0:T(8,128)(2,1)S(1)} %collective-permute-done.3.refs_2_), channel_id=1, source_target_pairs={{0,16},{16,32},{32,48},{48,64},{64,80},{80,96},{96,112},{112,0},{1... | collective-permute-start | bytes 1191944 | tf_op jit(solution)/shard_map/ppermute | solution.py:23
  40.5 9.2 %copy-start.3 = (bf16[1552,128]{1,0:T(8,128)(2,1)}, bf16[1552,128]{1,0:T(8,128)(2,1)S(1)}, u32[]{:S(2)}) copy-start(bf16[1552,128]{1,0:T(8,128)(2,1)S(1)} %collective-permute-done.refs_3_) | copy-start | bytes 1191940
  40.5 9.2 %collective-permute-start.1 = (bf16[1552,128]{1,0:T(8,128)(2,1)S(1)}, bf16[1552,128]{1,0:T(8,128)(2,1)}, u32[]{:S(2)}, u32[]{:S(2)}) collective-permute-start(bf16[1552,128]{1,0:T(8,128)(2,1)S(1)} %collective-permute-done.refs_3_), channel_id=1, source_target_pairs={{0,112},{16,0},{32,16},{48,32},{64,48},{80,64},{96,80},{112,96},{1... | collective-permute-start | bytes 1191944 | tf_op jit(solution)/shard_map/ppermute | solution.py:23
  49.7 8.4 %collective-permute-start.5 = (bf16[1552,128]{1,0:T(8,128)(2,1)}, bf16[1552,128]{1,0:T(8,128)(2,1)S(1)}, u32[]{:S(2)}, u32[]{:S(2)}) collective-permute-start(bf16[1552,128]{1,0:T(8,128)(2,1)} %collective-permute-done.4.refs_6_), channel_id=1, source_target_pairs={{0,16},{16,32},{32,48},{48,64},{64,80},{80,96},{96,112},{112,0},{1... | collective-permute-start | bytes 1191944 | tf_op jit(solution)/shard_map/ppermute | solution.py:23
  49.7 13.0 %collective-permute-start.2 = (bf16[1552,128]{1,0:T(8,128)(2,1)}, bf16[1552,128]{1,0:T(8,128)(2,1)}, u32[]{:S(2)}, u32[]{:S(2)}) collective-permute-start(bf16[1552,128]{1,0:T(8,128)(2,1)} %collective-permute-done.1.refs_7_), channel_id=1, source_target_pairs={{0,112},{16,0},{32,16},{48,32},{64,48},{80,64},{96,80},{112,96},{1... | collective-permute-start | bytes 1191944 | tf_op jit(solution)/shard_map/ppermute | solution.py:23
  52.4 11.2 %collective-permute-start.10 = (bf16[1552,128]{1,0:T(8,128)(2,1)}, bf16[1552,128]{1,0:T(8,128)(2,1)S(1)}, u32[]{:S(2)}, u32[]{:S(2)}) collective-permute-start(bf16[1552,128]{1,0:T(8,128)(2,1)} %shard_map.50.refs_0_), channel_id=1, source_target_pairs={{0,8},{8,0},{1,9},{9,1},{2,10},{10,2},{3,11},{11,3},{4,12},{12,4},... | collective-permute-start | bytes 1191944 | tf_op jit(solution)/shard_map/ppermute | solution.py:27
  56.7 7.7 %collective-permute-start.11 = (bf16[1552,128]{1,0:T(8,128)(2,1)}, bf16[1552,128]{1,0:T(8,128)(2,1)S(1)}, u32[]{:S(2)}, u32[]{:S(2)}) collective-permute-start(bf16[1552,128]{1,0:T(8,128)(2,1)} %copy-done.1), channel_id=1, source_target_pairs={{0,8},{8,0},{1,9},{9,1},{2,10},{10,2},{3,11},{11,3},{4,12},{12,4},... | collective-permute-start | bytes 1191944 | tf_op jit(solution)/shard_map/ppermute | solution.py:27
  56.7 11.6 %collective-permute-start.12 = (bf16[1552,128]{1,0:T(8,128)(2,1)}, bf16[1552,128]{1,0:T(8,128)(2,1)S(1)}, u32[]{:S(2)}, u32[]{:S(2)}) collective-permute-start(bf16[1552,128]{1,0:T(8,128)(2,1)} %copy-done.3), channel_id=1, source_target_pairs={{0,8},{8,0},{1,9},{9,1},{2,10},{10,2},{3,11},{11,3},{4,12},{12,4},... | collective-permute-start | bytes 1191944 | tf_op jit(solution)/shard_map/ppermute | solution.py:27
  58.1 12.0 %collective-permute-start.13 = (bf16[1552,128]{1,0:T(8,128)(2,1)}, bf16[1552,128]{1,0:T(8,128)(2,1)S(1)}, u32[]{:S(2)}, u32[]{:S(2)}) collective-permute-start(bf16[1552,128]{1,0:T(8,128)(2,1)} %collective-permute-done.4.refs_6_), channel_id=1, source_target_pairs={{0,8},{8,0},{1,9},{9,1},{2,10},{10,2},{3,11},{11,3},{4,12},{12,4},... | collective-permute-start | bytes 1191944 | tf_op jit(solution)/shard_map/ppermute | solution.py:27
  62.7 8.2 %collective-permute-start.14 = (bf16[1552,128]{1,0:T(8,128)(2,1)}, bf16[1552,128]{1,0:T(8,128)(2,1)S(1)}, u32[]{:S(2)}, u32[]{:S(2)}) collective-permute-start(bf16[1552,128]{1,0:T(8,128)(2,1)} %collective-permute-done.1.refs_7_), channel_id=1, source_target_pairs={{0,8},{8,0},{1,9},{9,1},{2,10},{10,2},{3,11},{11,3},{4,12},{12,4},... | collective-permute-start | bytes 1191944 | tf_op jit(solution)/shard_map/ppermute | solution.py:27
  64.3 41.1 %collective-permute-start.6 = (bf16[1552,128]{1,0:T(8,128)(2,1)}, bf16[1552,128]{1,0:T(8,128)(2,1)}, u32[]{:S(2)}, u32[]{:S(2)}) collective-permute-start(bf16[1552,128]{1,0:T(8,128)(2,1)} %broadcast_select_fusion), channel_id=1, source_target_pairs={{0,112},{16,0},{32,16},{48,32},{64,48},{80,64},{96,80},{112,96},{8... | collective-permute-start | bytes 1191944 | tf_op jit(solution)/shard_map/ppermute | solution.py:177
  65.1 40.3 %collective-permute-start.7 = (bf16[1552,128]{1,0:T(8,128)(2,1)}, bf16[1552,128]{1,0:T(8,128)(2,1)}, u32[]{:S(2)}, u32[]{:S(2)}) collective-permute-start(bf16[1552,128]{1,0:T(8,128)(2,1)} %broadcast_select_fusion), channel_id=1, source_target_pairs={{0,120},{16,8},{32,24},{48,40},{64,56},{80,72},{96,88},{112,104},{... | collective-permute-start | bytes 1191944 | tf_op jit(solution)/shard_map/ppermute | solution.py:177
  69.0 27.5 %collective-permute-start.8 = (bf16[1552,128]{1,0:T(8,128)(2,1)S(1)}, bf16[1552,128]{1,0:T(8,128)(2,1)}, u32[]{:S(2)}, u32[]{:S(2)}) collective-permute-start(bf16[1552,128]{1,0:T(8,128)(2,1)S(1)} %collective-permute-done.5.refs_0_), channel_id=1, source_target_pairs={{0,8},{8,0},{1,9},{9,1},{2,10},{10,2},{3,11},{11,3},{4,12},{12,4},... | collective-permute-start | bytes 1191944 | tf_op jit(solution)/shard_map/ppermute | solution.py:27
  70.9 25.7 %collective-permute-start.9 = (bf16[1552,128]{1,0:T(8,128)(2,1)}, bf16[1552,128]{1,0:T(8,128)(2,1)}, u32[]{:S(2)}, u32[]{:S(2)}) collective-permute-start(bf16[1552,128]{1,0:T(8,128)(2,1)} %collective-permute-done.2.refs_1_), channel_id=1, source_target_pairs={{0,8},{8,0},{1,9},{9,1},{2,10},{10,2},{3,11},{11,3},{4,12},{12,4},... | collective-permute-start | bytes 1191944 | tf_op jit(solution)/shard_map/ppermute | solution.py:27
  71.6 1.0 copy-start
  72.6 1.0 copy-start.2
  73.6 1.0 copy-start.4
  75.6 1.0 copy-start.8
  76.6 1.0 copy-start.10
  (9 other events, 7.6 us)

commit v2 on v0

v2 whole, which is shorter than its diff:
```python
import functools
import math

import jax
import jax.numpy as jnp
from jax import lax
from jax.experimental import pallas as pl
from jax.experimental.pallas import tpu as pltpu
from jax.sharding import Mesh, PartitionSpec as P

C = 1000
SMOOTHING = 0.1
AXES = ("xh", "z", "c", "xl", "y")
SIZES = (2, 8, 2, 2, 4)
FEAT = ("xl", "y")
LANES = 128
TAIL = 16
VMEM = pl.BlockSpec(memory_space=pltpu.VMEM)
ANY = pl.BlockSpec(memory_space=pl.ANY)


def ring(x, axis, step):
    return lax.ppermute(x, axis, [(i, (i + step) % 4) for i in range(4)])


def along_z(x, step, cross=False):
    n = SIZES[1]
    pairs = []
    for i in range(n):
        pairs.append((2 * i, 2 * ((i + step) % n) + cross))
        pairs.append((2 * i + 1, 2 * ((i - step) % n) + 1 - cross))
    return lax.ppermute(x, ("z", "c"), pairs)


def swap(x):
    return lax.ppermute(x, "c", [(0, 1), (1, 0)])


def move(kernel, shape, args, scratch=()):
    return pl.pallas_call(
        kernel,
        out_shape=jax.ShapeDtypeStruct(shape, jnp.bfloat16),
        in_specs=[VMEM] * len(args),
        out_specs=VMEM,
        scratch_shapes=list(scratch),
        cost_estimate=pl.CostEstimate(
            flops=0, bytes_accessed=4 * math.prod(shape), transcendentals=0
        ),
        compiler_params=pltpu.CompilerParams(vmem_limit_bytes=4 * 2**20),
    )(*args)


def pack_kernel(label_ref, class_ref, out_ref):
    rows, width = label_ref.shape
    out_ref[:, :width] = label_ref[...]
    ids = class_ref[...]
    row = lax.broadcasted_iota(jnp.int32, (rows, rows), 0)
    code = jnp.where(row == 0, ids >> 5, jnp.where(row == 1, ids & 31, 0))
    out_ref[:, width:] = code.astype(jnp.float32).astype(jnp.bfloat16)


def along_y_kernel(own_ref, below_ref, above_ref, far_ref, out_ref, parts):
    y = lax.axis_index("y")
    rows = own_ref.shape[0]
    for step, ref in ((0, own_ref), (3, below_ref), (1, above_ref), (2, far_ref)):
        parts[lax.rem(y + step, 4)] = ref[...]
    for j in range(2):
        even, odd = parts[2 * j], parts[2 * j + 1]
        blocks = (
            even[:, :128],
            jnp.concatenate([even[:, 128:192], odd[:, :64]], axis=1),
            odd[:, 64:192],
        )
        for k, block in enumerate(blocks):
            out_ref[(3 * j + k) * rows : (3 * j + k + 1) * rows, :] = block
    tail = own_ref[:TAIL, 192:]
    out_ref[6 * rows :, :] = jnp.concatenate([tail, tail], axis=1)


def along_x_kernel(own_ref, below_ref, above_ref, far_ref, out_ref):
    x = lax.axis_index("xh") * 2 + lax.axis_index("xl")
    half = 64
    for step, ref in ((0, own_ref), (3, below_ref), (1, above_ref), (2, far_ref)):
        at = lax.rem(x + step, 4)
        high, low = at >> 1, at & 1
        for k in range(6):
            row = pl.multiple_of((low * 6 + k) * 2 * half + high * half, half)
            out_ref[pl.ds(row, half), :] = ref[k * half : (k + 1) * half, :]
    own = own_ref[6 * half :, :].astype(jnp.float32)
    far = far_ref[6 * half :, :].astype(jnp.float32)
    lane_high = (lax.broadcasted_iota(jnp.int32, own.shape, 1) >= half).astype(
        jnp.int32
    )
    tail = jnp.where(lane_high == (x >> 1), own, far)
    out_ref[12 * 2 * half :, :] = tail.astype(jnp.bfloat16)


def attend_kernel(pieces, first, last, scale, *refs):
    given = 1 if first else pieces
    labels = refs[:given]
    pool_ref = refs[given]
    refs = refs[given + 1 :]
    if first:
        out_ref, stat_ref, scores, weights, onehot, held, sems = refs
        fetches = [
            pltpu.make_async_copy(labels[0].at[p], held.at[p], sems.at[p])
            for p in range(pieces)
        ]
        for fetch in fetches:
            fetch.start()
        labels = [held.at[p] for p in range(pieces)]
    elif last:
        old_mass, old_stat, out_ref, stat_ref, scores, weights, onehot, logs, sems = refs
    else:
        old_mass, old_stat, out_ref, stat_ref, scores, weights, onehot = refs
    rows = 128
    classes = lax.broadcasted_iota(jnp.int32, (C, rows), 0).astype(jnp.float32)
    top = None if first else old_stat[0:1]
    for pair in range(pieces // 2):
        two = labels[2 * pair : 2 * pair + 2]
        if first:
            fetches[2 * pair].wait()
            fetches[2 * pair + 1].wait()
        keys = jnp.concatenate(
            [
                jnp.concatenate(
                    [ref[k * rows : (k + 1) * rows, :] for ref in two], axis=0
                )
                for k in range(12)
            ],
            axis=1,
        )
        block = (
            jnp.dot(keys, pool_ref[...], preferred_element_type=jnp.float32) * scale
        )
        scores[pair * 2 * rows : (pair + 1) * 2 * rows, :] = block
        high = jnp.max(block, axis=0, keepdims=True)
        top = high if top is None else jnp.maximum(top, high)
        for p, ref in enumerate(two):
            tail = ref[12 * rows :, :].astype(jnp.float32)
            own = tail[0:1] * 32.0 + tail[1:2]
            at = (2 * pair + p) * rows
            onehot[:, at : at + rows] = jnp.where(classes == own, 1.0, 0.0).astype(
                jnp.bfloat16
            )
    total = None
    for pair in range(pieces // 2):
        at = slice(pair * 2 * rows, (pair + 1) * 2 * rows)
        block = jnp.exp(scores[at, :] - top)
        weights[at, :] = block.astype(jnp.bfloat16)
        part = jnp.sum(block, axis=0, keepdims=True)
        total = part if total is None else total + part
    mass = jnp.dot(onehot[...], weights[...], preferred_element_type=jnp.float32)
    if not first:
        fade = jnp.exp(old_stat[0:1] - top)
        total = total + fade * old_stat[1:2]
        mass = mass + fade * old_mass[...]
    if last:
        gain = (1.0 - SMOOTHING) / total
        entropy = jnp.zeros_like(total)
        step = 200
        copies = []
        for i in range(C // step):
            at = slice(i * step, (i + 1) * step)
            probability = mass[at] * gain + SMOOTHING / C
            log_probs = jnp.log(probability)
            logs[at, :] = log_probs
            copies.append(
                pltpu.make_async_copy(logs.at[at], out_ref.at[at], sems.at[i])
            )
            copies[-1].start()
            entropy = entropy - jnp.sum(probability * log_probs, axis=0, keepdims=True)
        stat_ref[...] = entropy
        for copy in copies:
            copy.wait()
    else:
        out_ref[...] = mass
        stat_ref[0:1] = top
        stat_ref[1:2] = total


def attend(pool, labels, state, last):
    depth, count = pool.shape
    first = state is None
    pieces = labels.shape[0] if first else len(labels)
    m = pieces * 128
    args = ([labels] if first else list(labels)) + [pool]
    args += [] if first else list(state)
    scratch = [
        pltpu.VMEM((m, count), jnp.float32),
        pltpu.VMEM((m, count), jnp.bfloat16),
        pltpu.VMEM((C, m), jnp.bfloat16),
    ]
    need = 6 * m * count + 2 * C * m + 4 * C * count
    if first:
        scratch += [
            pltpu.VMEM(labels.shape, jnp.bfloat16),
            pltpu.SemaphoreType.DMA((pieces,)),
        ]
        need += 2 * m * (depth + TAIL)
    if last:
        scratch += [
            pltpu.VMEM((C, count), jnp.float32),
            pltpu.SemaphoreType.DMA((C // 200,)),
        ]
        need += 4 * C * count
    label_specs = [ANY] if first else [VMEM] * pieces
    return pl.pallas_call(
        functools.partial(attend_kernel, pieces, first, last, 2.0 / math.sqrt(depth)),
        in_specs=label_specs + [VMEM] * (len(args) - len(label_specs)),
        out_specs=[ANY if last else VMEM, VMEM],
        out_shape=[
            jax.ShapeDtypeStruct((C, count), jnp.float32),
            jax.ShapeDtypeStruct((1 if last else 2, count), jnp.float32),
        ],
        scratch_shapes=scratch,
        input_output_aliases={}
        if first or last
        else {pieces + 1: 0, pieces + 2: 1},
        compiler_params=pltpu.CompilerParams(vmem_limit_bytes=need + 8 * 2**20),
        cost_estimate=pl.CostEstimate(
            flops=2 * m * count * (depth + C),
            bytes_accessed=4 * C * count,
            transcendentals=m * count,
        ),
    )(*args)


def stash_kernel(count, at, *refs):
    out_ref, sems = refs[-2:]
    copies = [
        pltpu.make_async_copy(refs[i], out_ref.at[at + i], sems.at[i])
        for i in range(count)
    ]
    for copy in copies:
        copy.start()
    for copy in copies:
        copy.wait()


def stash(store, pieces, at, slots):
    shape = (slots,) + pieces[0].shape
    args = list(pieces) + ([] if store is None else [store])
    return pl.pallas_call(
        functools.partial(stash_kernel, len(pieces), at),
        in_specs=[ANY] * len(args),
        out_specs=ANY,
        out_shape=jax.ShapeDtypeStruct(shape, jnp.bfloat16),
        scratch_shapes=[pltpu.SemaphoreType.DMA((len(pieces),))],
        input_output_aliases={} if store is None else {len(pieces): 0},
        cost_estimate=pl.CostEstimate(
            flops=0,
            bytes_accessed=4 * len(pieces) * math.prod(shape[1:]),
            transcendentals=0,
        ),
        compiler_params=pltpu.CompilerParams(vmem_limit_bytes=2**20),
    )(*args)


def split_kernel(in_ref, out_ref, sems):
    parts, _, count = out_ref.shape
    copies = [
        pltpu.make_async_copy(
            in_ref.at[:, p * count : (p + 1) * count], out_ref.at[p], sems.at[p]
        )
        for p in range(parts)
    ]
    for copy in copies:
        copy.start()
    for copy in copies:
        copy.wait()


def split(x, parts):
    width, count = x.shape
    return pl.pallas_call(
        split_kernel,
        in_specs=[ANY],
        out_specs=ANY,
        out_shape=jax.ShapeDtypeStruct((parts, width, count // parts), x.dtype),
        scratch_shapes=[pltpu.SemaphoreType.DMA((parts,))],
        cost_estimate=pl.CostEstimate(
            flops=0, bytes_accessed=4 * width * count, transcendentals=0
        ),
        compiler_params=pltpu.CompilerParams(vmem_limit_bytes=60 * 2**20),
    )(x)


def per_device(pool_embed, label_embed, label_class):
    feats = SIZES[3] * SIZES[4]
    count, width = pool_embed.shape[0] // feats, pool_embed.shape[1]
    rows = label_embed.shape[0]
    own = move(
        pack_kernel, (rows, width + rows), (label_embed, label_class.reshape(1, rows))
    )
    own, pool_embed = lax.optimization_barrier((own, pool_embed))
    pool = lax.all_to_all(split(pool_embed.T, feats), FEAT, 0, 0, tiled=True)
    pool = pool.reshape(feats * width, count)
    near = [own] + [ring(own, "y", step) for step in (1, 3, 2)]
    column = move(
        along_y_kernel,
        (6 * rows + TAIL, LANES),
        near,
        [pltpu.VMEM((4, rows, width + rows), jnp.bfloat16)],
    )
    near = [column] + [ring(column, ("xh", "xl"), step) for step in (1, 3, 2)]
    plane = move(along_x_kernel, (12 * 2 * rows + TAIL, LANES), near)
    other = swap(plane)
    up, down = along_z(plane, 1), along_z(plane, -1)
    store = stash(None, [plane, up, down, other], 0, 10)
    others = [swap(up), swap(down)]
    up, down = along_z(up, 1), along_z(down, -1)
    store = stash(store, others + [up, down], 4, 10)
    store = stash(store, [swap(up), swap(down)], 8, 10)
    state = attend(pool, store, None, False)
    up, down = along_z(up, 1), along_z(down, -1)
    state = attend(pool, [up, down, swap(up), swap(down)], state, False)
    ends = [along_z(up, 1), along_z(up, 1, cross=True)]
    log_probs, entropy = attend(pool, ends, state, True)
    return (log_probs.T, entropy[0])


def solution(mesh):
    fine = Mesh(mesh.devices.reshape(SIZES), AXES)
    blk = ("xh", "z", "c")
    return jax.shard_map(
        per_device,
        mesh=fine,
        in_specs=(P(blk, FEAT), P(blk, FEAT), P(blk)),
        out_specs=(P(blk + FEAT, None), P(blk + FEAT)),
        check_vma=False,
    )
```

time: 162 us -> 223 us (1.38)
  Pallas kernels: 0 us -> 121 us
  blocking collectives: 54.7 us -> 0 us
  starting transfers between devices: 4.41 us -> 50.8 us
  waiting for transfers between devices: 62.9 us -> 45.1 us
  matrix products: 16.7 us -> 0 us
  between operations: 14.7 us -> 0.98 us
  other arithmetic: 2.53 us -> 0 us
    pallas_call x0 -> x10, Pallas kernels: none -> 121 us  [the longest x1 96.5 us: split(): pl.pallas_call(split_kernel, in_specs=[ANY], out_specs=ANY, out_shape=jax...]
    all_gather x1 -> x0, waiting for transfers between devices: 62.5 us -> none  [per_device(): key_piece = lax.all_gather(key_rows, 'blk', axis=0, tiled=True)]
    ppermute x0 -> x21, waiting for transfers between devices: none -> 45.1 us  [the longest x6 38.9 us: ring(): return lax.ppermute(x, axis, [(i, (i + step) % 4) for i in range(4)])]
    ppermute x0 -> x21, starting transfers between devices: none -> 44.9 us  [the longest x7 25.3 us: swap(): return lax.ppermute(x, 'c', [(0, 1), (1, 0)])]
    unnamed x1 -> x0, blocking collectives: 30.7 us -> none
    all_gather x1 -> x0, blocking collectives: 24.1 us -> none  [per_device(): key_rows = lax.all_gather(label_embed, 'feat', axis=1, tiled=True)]
    dot_general x2 -> x0, matrix products: 16.7 us -> none  [the longest x1 8.99 us: per_device(): lax.dot_general(pool_rows, key_piece, (((1,), (1,)), ((), ())), preferred...]
    all_to_all x1 -> x0, local copies, waits for them, and re-layouts: 4 us -> none  [per_device(): lax.all_to_all(pool_embed, 'feat', split_axis=0, concat_axis=1, tiled=True)]
  transfers between devices with their start and end apart: 2 -> 22, of which waited for: 2 -> 4; matrix products, arithmetic and copies ran while one was open for 3% -> 0% of each run, Pallas kernels for 0% -> 8%
where the time goes in v2:
time: 223 us
  Pallas kernels  121 us (54%)
  starting transfers between devices  50.8 us (23%)
  waiting for transfers between devices  45.1 us (20%)
  local copies, waits for them, and re-layouts  5.46 us (2%)
    pallas_call x1, Pallas kernels, split(): pl.pallas_call(split_kernel, in_specs=[ANY], out_specs=ANY, out_shape=jax...  96.5 us
    ppermute x6, waiting for transfers between devices, ring(): return lax.ppermute(x, axis, [(i, (i + step) % 4) for i in range(4)])  38.9 us
    ppermute x7, starting transfers between devices, swap(): return lax.ppermute(x, 'c', [(0, 1), (1, 0)])  25.3 us
    pallas_call x3, Pallas kernels, attend(): pl.pallas_call(functools.partial(attend_kernel, pieces, first, last, 2.0...  21.9 us
    ppermute x8, starting transfers between devices, along_z(): return lax.ppermute(x, ('z', 'c'), pairs)  11.2 us
    ppermute x6, starting transfers between devices, ring(): return lax.ppermute(x, axis, [(i, (i + step) % 4) for i in range(4)])  8.42 us
    ppermute x8, waiting for transfers between devices, along_z(): return lax.ppermute(x, ('z', 'c'), pairs)  6.26 us
    all_to_all x1, starting transfers between devices, per_device(): pool = lax.all_to_all(split(pool_embed.T, feats), FEAT, 0, 0, tiled=True)  5.96 us
  transfers between devices with their start and end apart: 22, of which 4 were waited for; matrix products, arithmetic and copies ran while one was open for 0% of the time, Pallas kernels for 8%

profile of v2, /device:TPU:1, one launch (start us, length us, event | category | flops | bytes accessed | tf_op | source)
XLA Modules:
  0.0 223.0 jit_solution(3475596683586710195)
XLA Ops:
  2.1 96.5 %shard_map.53 = bf16[8,192,1024]{2,1,0:T(8,128)(2,1)} custom-call(bf16[192,8192]{1,0:T(8,128)(2,1)} %bitcast.9), custom_call_target="tpu_custom_call" | custom-call | bytes 6291456 | tf_op jit(solution)/shard_map/pallas_call | solution.py:276
  98.6 6.0 %all-to-all-start = ((bf16[8,192,1024]{2,1,0:T(8,128)(2,1)}), bf16[8,192,1024]{2,1,0:T(8,128)(2,1)S(1)}, u32[]{:S(2)}, u32[]{:S(2)}) async-start(bf16[8,192,1024]{2,1,0:T(8,128)(2,1)} %shard_map.53), calls=%async_computation | async-start | bytes 6291456 | tf_op jit(solution)/shard_map/all_to_all | solution.py:297
  104.6 1.5 collective-permute-start
  106.0 1.2 collective-permute-start.1
  107.3 1.7 collective-permute-start.2
  109.0 34.0 %collective-permute-done.below_ref = bf16[64,256]{1,0:T(8,128)(2,1)S(1)} collective-permute-done((bf16[64,256]{1,0:T(8,128)(2,1)S(1)}, bf16[64,256]{1,0:T(8,128)(2,1)S(1)}, u32[]{:S(2)}, u32[]{:S(2)}) %collective-permute-start) | collective-permute-done | bytes 32800 | tf_op jit(solution)/shard_map/ppermute | solution.py:23
  143.1 1.3 collective-permute-start.3
  144.4 1.5 collective-permute-start.4
  145.9 1.2 collective-permute-start.5
  147.9 4.0 %collective-permute-done.5.far_ref = bf16[400,128]{1,0:T(8,128)(2,1)S(1)} collective-permute-done((bf16[400,128]{1,0:T(8,128)(2,1)S(1)}, bf16[400,128]{1,0:T(8,128)(2,1)S(1)}, u32[]{:S(2)}, u32[]{:S(2)}) %collective-permute-start.5) | collective-permute-done | bytes 102432 | tf_op jit(solution)/shard_map/ppermute | solution.py:23
  152.0 5.7 %collective-permute-start.6 = (bf16[1552,128]{1,0:T(8,128)(2,1)S(1)}, bf16[1552,128]{1,0:T(8,128)(2,1)S(1)}, u32[]{:S(2)}, u32[]{:S(2)}) collective-permute-start(bf16[1552,128]{1,0:T(8,128)(2,1)S(1)} %shard_map.52.refs_0_), channel_id=1, source_target_pairs={{0,16},{8,120},{16,32},{24,8},{32,48},{40,24},{48,64},{56,40},{64,... | collective-permute-start | bytes 1191944 | tf_op jit(solution)/shard_map/ppermute | solution.py:32
  157.7 6.2 %collective-permute-done.6.refs_1_ = bf16[1552,128]{1,0:T(8,128)(2,1)S(1)} collective-permute-done((bf16[1552,128]{1,0:T(8,128)(2,1)S(1)}, bf16[1552,128]{1,0:T(8,128)(2,1)S(1)}, u32[]{:S(2)}, u32[]{:S(2)}) %collective-permute-start.6) | collective-permute-done | bytes 397344 | tf_op jit(solution)/shard_map/ppermute | solution.py:32
  163.9 3.4 %collective-permute-start.7 = (bf16[1552,128]{1,0:T(8,128)(2,1)S(1)}, bf16[1552,128]{1,0:T(8,128)(2,1)S(1)}, u32[]{:S(2)}, u32[]{:S(2)}) collective-permute-start(bf16[1552,128]{1,0:T(8,128)(2,1)S(1)} %collective-permute-done.6.refs_1_), channel_id=1, source_target_pairs={{0,16},{8,120},{16,32},{24,8},{32,48},{40,24},{48,64},{56,40},{64,... | collective-permute-start | bytes 1191944 | tf_op jit(solution)/shard_map/ppermute | solution.py:32
  167.3 2.5 %collective-permute-start.20 = (bf16[1552,128]{1,0:T(8,128)(2,1)S(1)}, bf16[1552,128]{1,0:T(8,128)(2,1)S(1)}, u32[]{:S(2)}, u32[]{:S(2)}) collective-permute-start(bf16[1552,128]{1,0:T(8,128)(2,1)S(1)} %shard_map.52.refs_0_), channel_id=1, source_target_pairs={{0,8},{8,0},{1,9},{9,1},{2,10},{10,2},{3,11},{11,3},{4,12},{12,4},... | collective-permute-start | bytes 1191944 | tf_op jit(solution)/shard_map/ppermute | solution.py:36
  169.8 3.2 %collective-permute-start.18 = (bf16[1552,128]{1,0:T(8,128)(2,1)S(1)}, bf16[1552,128]{1,0:T(8,128)(2,1)S(1)}, u32[]{:S(2)}, u32[]{:S(2)}) collective-permute-start(bf16[1552,128]{1,0:T(8,128)(2,1)S(1)} %collective-permute-done.6.refs_1_), channel_id=1, source_target_pairs={{0,8},{8,0},{1,9},{9,1},{2,10},{10,2},{3,11},{11,3},{4,12},{12,4},... | collective-permute-start | bytes 1191944 | tf_op jit(solution)/shard_map/ppermute | solution.py:36
  173.1 2.1 collective-permute-start.8
  175.2 7.8 %collective-permute-start.16 = (bf16[1552,128]{1,0:T(8,128)(2,1)S(1)}, bf16[1552,128]{1,0:T(8,128)(2,1)S(1)}, u32[]{:S(2)}, u32[]{:S(2)}) collective-permute-start(bf16[1552,128]{1,0:T(8,128)(2,1)S(1)} %collective-permute-done.7.refs_2_), channel_id=1, source_target_pairs={{0,8},{8,0},{1,9},{9,1},{2,10},{10,2},{3,11},{11,3},{4,12},{12,4},... | collective-permute-start | bytes 1191944 | tf_op jit(solution)/shard_map/ppermute | solution.py:36
  183.0 3.3 %collective-permute-start.17 = (bf16[1552,128]{1,0:T(8,128)(2,1)S(1)}, bf16[1552,128]{1,0:T(8,128)(2,1)S(1)}, u32[]{:S(2)}, u32[]{:S(2)}) collective-permute-start(bf16[1552,128]{1,0:T(8,128)(2,1)S(1)} %collective-permute-done.12.refs_3_), channel_id=1, source_target_pairs={{0,8},{8,0},{1,9},{9,1},{2,10},{10,2},{3,11},{11,3},{4,12},{12,4},... | collective-permute-start | bytes 1191944 | tf_op jit(solution)/shard_map/ppermute | solution.py:36
  187.9 8.2 %collective-permute-start.14 = (bf16[1552,128]{1,0:T(8,128)(2,1)}, bf16[1552,128]{1,0:T(8,128)(2,1)}, u32[]{:S(2)}, u32[]{:S(2)}) collective-permute-start(bf16[1552,128]{1,0:T(8,128)(2,1)} %collective-permute-done.8.refs_0_), channel_id=1, source_target_pairs={{0,8},{8,0},{1,9},{9,1},{2,10},{10,2},{3,11},{11,3},{4,12},{12,4},... | collective-permute-start | bytes 1191944 | tf_op jit(solution)/shard_map/ppermute | solution.py:36
  196.8 1.9 copy-done
  198.7 2.1 copy-done.1
  200.9 10.7 %shard_map.57 = (f32[1000,1024]{1,0:T(8,128)S(1)}, f32[2,1024]{1,0:T(2,128)S(1)}) custom-call(bf16[10,1552,128]{2,1,0:T(8,128)(2,1)S(1)} %copy-done.1, bf16[1536,1024]{1,0:T(8,128)(2,1)S(1)} %bitcast.5), custom_call_target="tpu_custom_call" | custom-call | flops 6647971840 | bytes 4096000 | tf_op jit(solution)/shard_map/pallas_call | solution.py:208
  211.6 5.3 %shard_map.58 = (f32[1000,1024]{1,0:T(8,128)S(1)}, f32[2,1024]{1,0:T(2,128)S(1)}) custom-call(bf16[1552,128]{1,0:T(8,128)(2,1)} %collective-permute-done.8.refs_0_, bf16[1552,128]{1,0:T(8,128)(2,1)} %collective-permute-done.13.refs_1_, bf16[1552,128]{1,0:T(8,128)(2,1)} %collective-permute-done.14.refs_2_, ...), custom_call_target="tpu_custom_call", output_to_operand_aliasing={{0}: (5, {}), {1}: (6, {})} | custom-call | flops 2659188736 | bytes 4096000 | tf_op jit(solution)/shard_map/pallas_call | solution.py:208
  216.9 5.9 %shard_map.59 = (f32[1000,1024]{1,0:T(8,128)}, f32[1,1024]{1,0:T(1,128)}) custom-call(bf16[1552,128]{1,0:T(8,128)(2,1)} %collective-permute-done.9.refs_0_, bf16[1552,128]{1,0:T(8,128)(2,1)S(1)} %collective-permute-done.10.refs_1_, bf16[1536,1024]{1,0:T(8,128)(2,1)S(1)} %bitcast.7, f32[1000,1024]{1,0:T(8,128)S(1)} %get-tuple-element.14.refs_3_, ...), custom_call_target="tpu_custom_call" | custom-call | flops 1329594368 | bytes 4096000 | tf_op jit(solution)/shard_map/pallas_call | solution.py:208
  (38 shorter events, 4.7 us)
Async XLA Ops:
  98.6 100.1 %all-to-all-start = ((bf16[8,192,1024]{2,1,0:T(8,128)(2,1)}), bf16[8,192,1024]{2,1,0:T(8,128)(2,1)S(1)}, u32[]{:S(2)}, u32[]{:S(2)}) async-start(bf16[8,192,1024]{2,1,0:T(8,128)(2,1)} %shard_map.53), calls=%async_computation | async-start | bytes 6291456 | tf_op jit(solution)/shard_map/all_to_all | solution.py:297
  104.6 38.4 %collective-permute-start = (bf16[64,256]{1,0:T(8,128)(2,1)S(1)}, bf16[64,256]{1,0:T(8,128)(2,1)S(1)}, u32[]{:S(2)}, u32[]{:S(2)}) collective-permute-start(bf16[64,256]{1,0:T(8,128)(2,1)S(1)} %shard_map.50.own_ref), channel_id=1, source_target_pairs={{0,1},{1,2},{2,3},{3,0},{4,5},{5,6},{6,7},{7,4},{8,9},{9,10},{10,1... | collective-permute-start | bytes 98312 | tf_op jit(solution)/shard_map/ppermute | solution.py:23
  106.0 37.0 %collective-permute-start.1 = (bf16[64,256]{1,0:T(8,128)(2,1)S(1)}, bf16[64,256]{1,0:T(8,128)(2,1)S(1)}, u32[]{:S(2)}, u32[]{:S(2)}) collective-permute-start(bf16[64,256]{1,0:T(8,128)(2,1)S(1)} %shard_map.50.own_ref), channel_id=1, source_target_pairs={{0,3},{1,0},{2,1},{3,2},{4,7},{5,4},{6,5},{7,6},{8,11},{9,8},{10,9... | collective-permute-start | bytes 98312 | tf_op jit(solution)/shard_map/ppermute | solution.py:23
  107.3 35.7 %collective-permute-start.2 = (bf16[64,256]{1,0:T(8,128)(2,1)S(1)}, bf16[64,256]{1,0:T(8,128)(2,1)S(1)}, u32[]{:S(2)}, u32[]{:S(2)}) collective-permute-start(bf16[64,256]{1,0:T(8,128)(2,1)S(1)} %shard_map.50.own_ref), channel_id=1, source_target_pairs={{0,2},{1,3},{2,0},{3,1},{4,6},{5,7},{6,4},{7,5},{8,10},{9,11},{10,... | collective-permute-start | bytes 98312 | tf_op jit(solution)/shard_map/ppermute | solution.py:23
  143.1 4.8 %collective-permute-start.3 = (bf16[400,128]{1,0:T(8,128)(2,1)S(1)}, bf16[400,128]{1,0:T(8,128)(2,1)S(1)}, u32[]{:S(2)}, u32[]{:S(2)}) collective-permute-start(bf16[400,128]{1,0:T(8,128)(2,1)S(1)} %shard_map.51.own_ref), channel_id=1, source_target_pairs={{0,4},{4,128},{128,132},{132,0},{1,5},{5,129},{129,133},{133,1},{2... | collective-permute-start | bytes 307208 | tf_op jit(solution)/shard_map/ppermute | solution.py:23
  144.4 3.5 %collective-permute-start.4 = (bf16[400,128]{1,0:T(8,128)(2,1)S(1)}, bf16[400,128]{1,0:T(8,128)(2,1)S(1)}, u32[]{:S(2)}, u32[]{:S(2)}) collective-permute-start(bf16[400,128]{1,0:T(8,128)(2,1)S(1)} %shard_map.51.own_ref), channel_id=1, source_target_pairs={{0,132},{4,0},{128,4},{132,128},{1,133},{5,1},{129,5},{133,129},{2... | collective-permute-start | bytes 307208 | tf_op jit(solution)/shard_map/ppermute | solution.py:23
  145.9 6.1 %collective-permute-start.5 = (bf16[400,128]{1,0:T(8,128)(2,1)S(1)}, bf16[400,128]{1,0:T(8,128)(2,1)S(1)}, u32[]{:S(2)}, u32[]{:S(2)}) collective-permute-start(bf16[400,128]{1,0:T(8,128)(2,1)S(1)} %shard_map.51.own_ref), channel_id=1, source_target_pairs={{0,128},{4,132},{128,0},{132,4},{1,129},{5,133},{129,1},{133,5},{2... | collective-permute-start | bytes 307208 | tf_op jit(solution)/shard_map/ppermute | solution.py:23
  152.0 11.9 %collective-permute-start.6 = (bf16[1552,128]{1,0:T(8,128)(2,1)S(1)}, bf16[1552,128]{1,0:T(8,128)(2,1)S(1)}, u32[]{:S(2)}, u32[]{:S(2)}) collective-permute-start(bf16[1552,128]{1,0:T(8,128)(2,1)S(1)} %shard_map.52.refs_0_), channel_id=1, source_target_pairs={{0,16},{8,120},{16,32},{24,8},{32,48},{40,24},{48,64},{56,40},{64,... | collective-permute-start | bytes 1191944 | tf_op jit(solution)/shard_map/ppermute | solution.py:32
  157.7 12.2 %collective-permute-start.11 = (bf16[1552,128]{1,0:T(8,128)(2,1)S(1)}, bf16[1552,128]{1,0:T(8,128)(2,1)S(1)}, u32[]{:S(2)}, u32[]{:S(2)}) collective-permute-start(bf16[1552,128]{1,0:T(8,128)(2,1)S(1)} %shard_map.52.refs_0_), channel_id=1, source_target_pairs={{0,112},{8,24},{16,0},{24,40},{32,16},{40,56},{48,32},{56,72},{64,... | collective-permute-start | bytes 1191944 | tf_op jit(solution)/shard_map/ppermute | solution.py:32
  163.9 9.2 %collective-permute-start.7 = (bf16[1552,128]{1,0:T(8,128)(2,1)S(1)}, bf16[1552,128]{1,0:T(8,128)(2,1)S(1)}, u32[]{:S(2)}, u32[]{:S(2)}) collective-permute-start(bf16[1552,128]{1,0:T(8,128)(2,1)S(1)} %collective-permute-done.6.refs_1_), channel_id=1, source_target_pairs={{0,16},{8,120},{16,32},{24,8},{32,48},{40,24},{48,64},{56,40},{64,... | collective-permute-start | bytes 1191944 | tf_op jit(solution)/shard_map/ppermute | solution.py:32
  167.3 7.9 %collective-permute-start.20 = (bf16[1552,128]{1,0:T(8,128)(2,1)S(1)}, bf16[1552,128]{1,0:T(8,128)(2,1)S(1)}, u32[]{:S(2)}, u32[]{:S(2)}) collective-permute-start(bf16[1552,128]{1,0:T(8,128)(2,1)S(1)} %shard_map.52.refs_0_), channel_id=1, source_target_pairs={{0,8},{8,0},{1,9},{9,1},{2,10},{10,2},{3,11},{11,3},{4,12},{12,4},... | collective-permute-start | bytes 1191944 | tf_op jit(solution)/shard_map/ppermute | solution.py:36
  169.8 13.1 %collective-permute-start.12 = (bf16[1552,128]{1,0:T(8,128)(2,1)S(1)}, bf16[1552,128]{1,0:T(8,128)(2,1)S(1)}, u32[]{:S(2)}, u32[]{:S(2)}) collective-permute-start(bf16[1552,128]{1,0:T(8,128)(2,1)S(1)} %collective-permute-done.11.refs_2_), channel_id=1, source_target_pairs={{0,112},{8,24},{16,0},{24,40},{32,16},{40,56},{48,32},{56,72},{64,... | collective-permute-start | bytes 1191944 | tf_op jit(solution)/shard_map/ppermute | solution.py:32
  169.8 13.1 %collective-permute-start.18 = (bf16[1552,128]{1,0:T(8,128)(2,1)S(1)}, bf16[1552,128]{1,0:T(8,128)(2,1)S(1)}, u32[]{:S(2)}, u32[]{:S(2)}) collective-permute-start(bf16[1552,128]{1,0:T(8,128)(2,1)S(1)} %collective-permute-done.6.refs_1_), channel_id=1, source_target_pairs={{0,8},{8,0},{1,9},{9,1},{2,10},{10,2},{3,11},{11,3},{4,12},{12,4},... | collective-permute-start | bytes 1191944 | tf_op jit(solution)/shard_map/ppermute | solution.py:36
  173.1 14.0 %collective-permute-start.19 = (bf16[1552,128]{1,0:T(8,128)(2,1)S(1)}, bf16[1552,128]{1,0:T(8,128)(2,1)S(1)}, u32[]{:S(2)}, u32[]{:S(2)}) collective-permute-start(bf16[1552,128]{1,0:T(8,128)(2,1)S(1)} %collective-permute-done.11.refs_2_), channel_id=1, source_target_pairs={{0,8},{8,0},{1,9},{9,1},{2,10},{10,2},{3,11},{11,3},{4,12},{12,4},... | collective-permute-start | bytes 1191944 | tf_op jit(solution)/shard_map/ppermute | solution.py:36
  173.1 14.8 %collective-permute-start.8 = (bf16[1552,128]{1,0:T(8,128)(2,1)S(1)}, bf16[1552,128]{1,0:T(8,128)(2,1)}, u32[]{:S(2)}, u32[]{:S(2)}) collective-permute-start(bf16[1552,128]{1,0:T(8,128)(2,1)S(1)} %collective-permute-done.7.refs_2_), channel_id=1, source_target_pairs={{0,16},{8,120},{16,32},{24,8},{32,48},{40,24},{48,64},{56,40},{64,... | collective-permute-start | bytes 1191944 | tf_op jit(solution)/shard_map/ppermute | solution.py:32
  175.2 21.0 %collective-permute-start.16 = (bf16[1552,128]{1,0:T(8,128)(2,1)S(1)}, bf16[1552,128]{1,0:T(8,128)(2,1)S(1)}, u32[]{:S(2)}, u32[]{:S(2)}) collective-permute-start(bf16[1552,128]{1,0:T(8,128)(2,1)S(1)} %collective-permute-done.7.refs_2_), channel_id=1, source_target_pairs={{0,8},{8,0},{1,9},{9,1},{2,10},{10,2},{3,11},{11,3},{4,12},{12,4},... | collective-permute-start | bytes 1191944 | tf_op jit(solution)/shard_map/ppermute | solution.py:36
  183.0 13.2 %collective-permute-start.13 = (bf16[1552,128]{1,0:T(8,128)(2,1)S(1)}, bf16[1552,128]{1,0:T(8,128)(2,1)}, u32[]{:S(2)}, u32[]{:S(2)}) collective-permute-start(bf16[1552,128]{1,0:T(8,128)(2,1)S(1)} %collective-permute-done.12.refs_3_), channel_id=1, source_target_pairs={{0,112},{8,24},{16,0},{24,40},{32,16},{40,56},{48,32},{56,72},{64,... | collective-permute-start | bytes 1191944 | tf_op jit(solution)/shard_map/ppermute | solution.py:32
  183.0 13.4 %collective-permute-start.17 = (bf16[1552,128]{1,0:T(8,128)(2,1)S(1)}, bf16[1552,128]{1,0:T(8,128)(2,1)S(1)}, u32[]{:S(2)}, u32[]{:S(2)}) collective-permute-start(bf16[1552,128]{1,0:T(8,128)(2,1)S(1)} %collective-permute-done.12.refs_3_), channel_id=1, source_target_pairs={{0,8},{8,0},{1,9},{9,1},{2,10},{10,2},{3,11},{11,3},{4,12},{12,4},... | collective-permute-start | bytes 1191944 | tf_op jit(solution)/shard_map/ppermute | solution.py:36
  187.9 23.6 %collective-permute-start.14 = (bf16[1552,128]{1,0:T(8,128)(2,1)}, bf16[1552,128]{1,0:T(8,128)(2,1)}, u32[]{:S(2)}, u32[]{:S(2)}) collective-permute-start(bf16[1552,128]{1,0:T(8,128)(2,1)} %collective-permute-done.8.refs_0_), channel_id=1, source_target_pairs={{0,8},{8,0},{1,9},{9,1},{2,10},{10,2},{3,11},{11,3},{4,12},{12,4},... | collective-permute-start | bytes 1191944 | tf_op jit(solution)/shard_map/ppermute | solution.py:36
  196.2 20.7 %collective-permute-start.10 = (bf16[1552,128]{1,0:T(8,128)(2,1)}, bf16[1552,128]{1,0:T(8,128)(2,1)S(1)}, u32[]{:S(2)}, u32[]{:S(2)}) collective-permute-start(bf16[1552,128]{1,0:T(8,128)(2,1)} %collective-permute-done.8.refs_0_), channel_id=1, source_target_pairs={{0,24},{8,112},{16,40},{24,0},{32,56},{40,16},{48,72},{56,32},{64,... | collective-permute-start | bytes 1191944 | tf_op jit(solution)/shard_map/ppermute | solution.py:32
  196.2 20.7 %collective-permute-start.9 = (bf16[1552,128]{1,0:T(8,128)(2,1)}, bf16[1552,128]{1,0:T(8,128)(2,1)}, u32[]{:S(2)}, u32[]{:S(2)}) collective-permute-start(bf16[1552,128]{1,0:T(8,128)(2,1)} %collective-permute-done.8.refs_0_), channel_id=1, source_target_pairs={{0,16},{8,120},{16,32},{24,8},{32,48},{40,24},{48,64},{56,40},{64,... | collective-permute-start | bytes 1191944 | tf_op jit(solution)/shard_map/ppermute | solution.py:32
  196.2 15.3 %collective-permute-start.15 = (bf16[1552,128]{1,0:T(8,128)(2,1)}, bf16[1552,128]{1,0:T(8,128)(2,1)}, u32[]{:S(2)}, u32[]{:S(2)}) collective-permute-start(bf16[1552,128]{1,0:T(8,128)(2,1)} %collective-permute-done.13.refs_1_), channel_id=1, source_target_pairs={{0,8},{8,0},{1,9},{9,1},{2,10},{10,2},{3,11},{11,3},{4,12},{12,4},... | collective-permute-start | bytes 1191944 | tf_op jit(solution)/shard_map/ppermute | solution.py:36
  196.8 1.9 copy-start
  198.7 2.1 copy-start.1
  (2 other events, 1.4 us)

commit v3 on v2

--- a/solution.py
+++ b/solution.py
@@ -13,22 +13,24 @@
 AXES = ("xh", "z", "c", "xl", "y")
 SIZES = (2, 8, 2, 2, 4)
 FEAT = ("xl", "y")
+PLANE = ("xh", "xl", "y")
 LANES = 128
 TAIL = 16
 VMEM = pl.BlockSpec(memory_space=pltpu.VMEM)
 ANY = pl.BlockSpec(memory_space=pl.ANY)
 
 
-def ring(x, axis, step):
-    return lax.ppermute(x, axis, [(i, (i + step) % 4) for i in range(4)])
-
-
-def along_z(x, step, cross=False):
+def along_z(x, step):
+    n = SIZES[1]
+    return lax.ppermute(x, "z", [(i, (i + step) % n) for i in range(n)])
+
+
+def outward(x, cross):
     n = SIZES[1]
     pairs = []
     for i in range(n):
-        pairs.append((2 * i, 2 * ((i + step) % n) + cross))
-        pairs.append((2 * i + 1, 2 * ((i - step) % n) + 1 - cross))
+        pairs.append((2 * i, 2 * ((i - 1) % n) + cross))
+        pairs.append((2 * i + 1, 2 * ((i + 1) % n) + 1 - cross))
     return lax.ppermute(x, ("z", "c"), pairs)
 
 
@@ -52,47 +54,34 @@
 
 def pack_kernel(label_ref, class_ref, out_ref):
     rows, width = label_ref.shape
-    out_ref[:, :width] = label_ref[...]
     ids = class_ref[...]
     row = lax.broadcasted_iota(jnp.int32, (rows, rows), 0)
     code = jnp.where(row == 0, ids >> 5, jnp.where(row == 1, ids & 31, 0))
-    out_ref[:, width:] = code.astype(jnp.float32).astype(jnp.bfloat16)
-
-
-def along_y_kernel(own_ref, below_ref, above_ref, far_ref, out_ref, parts):
-    y = lax.axis_index("y")
-    rows = own_ref.shape[0]
-    for step, ref in ((0, own_ref), (3, below_ref), (1, above_ref), (2, far_ref)):
-        parts[lax.rem(y + step, 4)] = ref[...]
-    for j in range(2):
-        even, odd = parts[2 * j], parts[2 * j + 1]
-        blocks = (
-            even[:, :128],
-            jnp.concatenate([even[:, 128:192], odd[:, :64]], axis=1),
-            odd[:, 64:192],
-        )
-        for k, block in enumerate(blocks):
-            out_ref[(3 * j + k) * rows : (3 * j + k + 1) * rows, :] = block
-    tail = own_ref[:TAIL, 192:]
-    out_ref[6 * rows :, :] = jnp.concatenate([tail, tail], axis=1)
-
-
-def along_x_kernel(own_ref, below_ref, above_ref, far_ref, out_ref):
-    x = lax.axis_index("xh") * 2 + lax.axis_index("xl")
-    half = 64
-    for step, ref in ((0, own_ref), (3, below_ref), (1, above_ref), (2, far_ref)):
-        at = lax.rem(x + step, 4)
-        high, low = at >> 1, at & 1
-        for k in range(6):
-            row = pl.multiple_of((low * 6 + k) * 2 * half + high * half, half)
-            out_ref[pl.ds(row, half), :] = ref[k * half : (k + 1) * half, :]
-    own = own_ref[6 * half :, :].astype(jnp.float32)
-    far = far_ref[6 * half :, :].astype(jnp.float32)
-    lane_high = (lax.broadcasted_iota(jnp.int32, own.shape, 1) >= half).astype(
-        jnp.int32
+    block = jnp.concatenate(
+        [label_ref[...], code.astype(jnp.float32).astype(jnp.bfloat16)], axis=1
     )
-    tail = jnp.where(lane_high == (x >> 1), own, far)
-    out_ref[12 * 2 * half :, :] = tail.astype(jnp.bfloat16)
+    for i in range(out_ref.shape[0]):
+        out_ref[i] = block
+
+
+def arrange_kernel(parts_ref, out_ref):
+    half = parts_ref.shape[1]
+    rows = 2 * half
+    for xh in range(2):
+        for j in range(4):
+            even = parts_ref[xh * 8 + 2 * j]
+            odd = parts_ref[xh * 8 + 2 * j + 1]
+            blocks = (
+                even[:, :128],
+                jnp.concatenate([even[:, 128:192], odd[:, :64]], axis=1),
+                odd[:, 64:192],
+            )
+            for k, block in enumerate(blocks):
+                at = (3 * j + k) * rows + xh * half
+                out_ref[at : at + half, :] = block
+    out_ref[12 * rows :, :] = jnp.concatenate(
+        [parts_ref[0, :TAIL, 192:], parts_ref[8, :TAIL, 192:]], axis=1
+    )
 
 
 def attend_kernel(pieces, first, last, scale, *refs):
@@ -101,14 +90,8 @@
     pool_ref = refs[given]
     refs = refs[given + 1 :]
     if first:
-        out_ref, stat_ref, scores, weights, onehot, held, sems = refs
-        fetches = [
-            pltpu.make_async_copy(labels[0].at[p], held.at[p], sems.at[p])
-            for p in range(pieces)
-        ]
-        for fetch in fetches:
-            fetch.start()
-        labels = [held.at[p] for p in range(pieces)]
+        out_ref, stat_ref, scores, weights, onehot = refs
+        labels = [labels[0].at[p] for p in range(pieces)]
     elif last:
         old_mass, old_stat, out_ref, stat_ref, scores, weights, onehot, logs, sems = refs
     else:
@@ -118,9 +101,6 @@
     top = None if first else old_stat[0:1]
     for pair in range(pieces // 2):
         two = labels[2 * pair : 2 * pair + 2]
-        if first:
-            fetches[2 * pair].wait()
-            fetches[2 * pair + 1].wait()
         keys = jnp.concatenate(
             [
                 jnp.concatenate(
@@ -192,19 +172,13 @@
         pltpu.VMEM((C, m), jnp.bfloat16),
     ]
     need = 6 * m * count + 2 * C * m + 4 * C * count
-    if first:
-        scratch += [
-            pltpu.VMEM(labels.shape, jnp.bfloat16),
-            pltpu.SemaphoreType.DMA((pieces,)),
-        ]
-        need += 2 * m * (depth + TAIL)
     if last:
         scratch += [
             pltpu.VMEM((C, count), jnp.float32),
             pltpu.SemaphoreType.DMA((C // 200,)),
         ]
         need += 4 * C * count
-    label_specs = [ANY] if first else [VMEM] * pieces
+    label_specs = [VMEM] if first else [VMEM] * pieces
     return pl.pallas_call(
         functools.partial(attend_kernel, pieces, first, last, 2.0 / math.sqrt(depth)),
         in_specs=label_specs + [VMEM] * (len(args) - len(label_specs)),
@@ -253,37 +227,38 @@
             bytes_accessed=4 * len(pieces) * math.prod(shape[1:]),
             transcendentals=0,
         ),
+        compiler_params=pltpu.CompilerParams(vmem_limit_bytes=60 * 2**20),
+    )(*args)
+
+
+def choose_kernel(up_ref, down_ref, out_ref, sem):
+    core = lax.axis_index("c")
+
+    @pl.when(core == 0)
+    def _():
+        copy = pltpu.make_async_copy(down_ref, out_ref, sem)
+        copy.start()
+        copy.wait()
+
+    @pl.when(core != 0)
+    def _():
+        copy = pltpu.make_async_copy(up_ref, out_ref, sem)
+        copy.start()
+        copy.wait()
+
+
+def choose(up, down):
+    return pl.pallas_call(
+        choose_kernel,
+        in_specs=[ANY, ANY],
+        out_specs=ANY,
+        out_shape=jax.ShapeDtypeStruct(up.shape, up.dtype),
+        scratch_shapes=[pltpu.SemaphoreType.DMA],
+        cost_estimate=pl.CostEstimate(
+            flops=0, bytes_accessed=4 * up.size, transcendentals=0
+        ),
         compiler_params=pltpu.CompilerParams(vmem_limit_bytes=2**20),
-    )(*args)
-
-
-def split_kernel(in_ref, out_ref, sems):
-    parts, _, count = out_ref.shape
-    copies = [
-        pltpu.make_async_copy(
-            in_ref.at[:, p * count : (p + 1) * count], out_ref.at[p], sems.at[p]
-        )
-        for p in range(parts)
-    ]
-    for copy in copies:
-        copy.start()
-    for copy in copies:
-        copy.wait()
-
-
-def split(x, parts):
-    width, count = x.shape
-    return pl.pallas_call(
-        split_kernel,
-        in_specs=[ANY],
-        out_specs=ANY,
-        out_shape=jax.ShapeDtypeStruct((parts, width, count // parts), x.dtype),
-        scratch_shapes=[pltpu.SemaphoreType.DMA((parts,))],
-        cost_estimate=pl.CostEstimate(
-            flops=0, bytes_accessed=4 * width * count, transcendentals=0
-        ),
-        compiler_params=pltpu.CompilerParams(vmem_limit_bytes=60 * 2**20),
-    )(x)
+    )(up, down)
 
 
 def per_device(pool_embed, label_embed, label_class):
@@ -291,31 +266,28 @@
     count, width = pool_embed.shape[0] // feats, pool_embed.shape[1]
     rows = label_embed.shape[0]
     own = move(
-        pack_kernel, (rows, width + rows), (label_embed, label_class.reshape(1, rows))
+        pack_kernel,
+        (16, rows, width + rows),
+        (label_embed, label_class.reshape(1, rows)),
     )
+    parts = lax.all_to_all(own, PLANE, 0, 0, tiled=True)
     own, pool_embed = lax.optimization_barrier((own, pool_embed))
-    pool = lax.all_to_all(split(pool_embed.T, feats), FEAT, 0, 0, tiled=True)
+    queries = pool_embed.T.reshape(width, feats, count).transpose(1, 0, 2)
+    pool = lax.all_to_all(queries, FEAT, 0, 0, tiled=True)
     pool = pool.reshape(feats * width, count)
-    near = [own] + [ring(own, "y", step) for step in (1, 3, 2)]
-    column = move(
-        along_y_kernel,
-        (6 * rows + TAIL, LANES),
-        near,
-        [pltpu.VMEM((4, rows, width + rows), jnp.bfloat16)],
-    )
-    near = [column] + [ring(column, ("xh", "xl"), step) for step in (1, 3, 2)]
-    plane = move(along_x_kernel, (12 * 2 * rows + TAIL, LANES), near)
-    other = swap(plane)
+    plane = move(arrange_kernel, (12 * 2 * rows + TAIL, LANES), (parts,))
+    slots = 14
     up, down = along_z(plane, 1), along_z(plane, -1)
-    store = stash(None, [plane, up, down, other], 0, 10)
+    store = stash(None, [plane, swap(plane), up, down], 0, slots)
     others = [swap(up), swap(down)]
     up, down = along_z(up, 1), along_z(down, -1)
-    store = stash(store, others + [up, down], 4, 10)
-    store = stash(store, [swap(up), swap(down)], 8, 10)
+    store = stash(store, others + [up, down], 4, slots)
+    others = [swap(up), swap(down)]
+    up, down = along_z(up, 1), along_z(down, -1)
+    store = stash(store, others + [up, down, swap(up), swap(down)], 8, slots)
+    far = choose(up, down)
+    ends = [outward(far, 0), outward(far, 1)]
     state = attend(pool, store, None, False)
-    up, down = along_z(up, 1), along_z(down, -1)
-    state = attend(pool, [up, down, swap(up), swap(down)], state, False)
-    ends = [along_z(up, 1), along_z(up, 1, cross=True)]
     log_probs, entropy = attend(pool, ends, state, True)
     return (log_probs.T, entropy[0])
 

time: 223 us -> 269 us (1.21)
  Pallas kernels: 121 us -> 190 us
  waiting for transfers between devices: 45.1 us -> 17.8 us
  local copies, waits for them, and re-layouts: 5.46 us -> 9.84 us
    pallas_call x3, Pallas kernels: 2.01 us -> 172 us  [stash(): pl.pallas_call(functools.partial(stash_kernel, len(pieces), at), in_specs...]
    pallas_call x1, Pallas kernels: 96.5 us -> 0.79 us  [choose(): pl.pallas_call(choose_kernel, in_specs=[ANY, ANY], out_specs=ANY, out_sha...]
    ppermute x14 -> x8, waiting for transfers between devices: 45.1 us -> 11.4 us  [the longest x6 11.4 us: along_z(): return lax.ppermute(x, 'z', [(i, (i + step) % n) for i in range(n)])]
    ppermute x7, starting transfers between devices: 25.3 us -> 12.9 us  [swap(): return lax.ppermute(x, 'c', [(0, 1), (1, 0)])]
    all_to_all x1 -> x2, waiting for transfers between devices: 0.01 us -> 6.32 us  [the longest x1 6.31 us: per_device(): parts = lax.all_to_all(own, PLANE, 0, 0, tiled=True)]
    ppermute x14 -> x8, starting transfers between devices: 19.6 us -> 25.6 us  [the longest x2 14.5 us: outward(): return lax.ppermute(x, ('z', 'c'), pairs)]
    pallas_call x3 -> x2, Pallas kernels: 21.9 us -> 16.2 us  [attend(): pl.pallas_call(functools.partial(attend_kernel, pieces, first, last, 2.0...]
    all_to_all x1 -> x2, starting transfers between devices: 5.96 us -> 11.2 us  [the longest x1 7.58 us: per_device(): parts = lax.all_to_all(own, PLANE, 0, 0, tiled=True)]
  transfers between devices with their start and end apart: 22 -> 17, of which waited for: 4 -> 4; matrix products, arithmetic and copies ran while one was open for 0% -> 1% of each run, Pallas kernels for 8% -> 68%
where the time goes in v3:
time: 269 us; the launch traced here: 268 us
  Pallas kernels  190 us (71%)
  starting transfers between devices  49.7 us (18%)
  waiting for transfers between devices  17.8 us (7%)
  local copies, waits for them, and re-layouts  9.84 us (4%)
    pallas_call x3, Pallas kernels, stash(): pl.pallas_call(functools.partial(stash_kernel, len(pieces), at), in_specs...  172 us
    pallas_call x2, Pallas kernels, attend(): pl.pallas_call(functools.partial(attend_kernel, pieces, first, last, 2.0...  16.2 us
    ppermute x2, starting transfers between devices, outward(): return lax.ppermute(x, ('z', 'c'), pairs)  14.5 us
    ppermute x7, starting transfers between devices, swap(): return lax.ppermute(x, 'c', [(0, 1), (1, 0)])  12.9 us
    ppermute x6, waiting for transfers between devices, along_z(): return lax.ppermute(x, 'z', [(i, (i + step) % n) for i in range(n)])  11.4 us
    ppermute x6, starting transfers between devices, along_z(): return lax.ppermute(x, 'z', [(i, (i + step) % n) for i in range(n)])  11.1 us
    all_to_all x1, starting transfers between devices, per_device(): parts = lax.all_to_all(own, PLANE, 0, 0, tiled=True)  7.58 us
    all_to_all x1, waiting for transfers between devices, per_device(): parts = lax.all_to_all(own, PLANE, 0, 0, tiled=True)  6.31 us
  transfers between devices with their start and end apart: 17, of which 4 were waited for; matrix products, arithmetic and copies ran while one was open for 1% of the time, Pallas kernels for 68%

profile of v3, /device:TPU:1, one launch (start us, length us, event | category | flops | bytes accessed | tf_op | source)
XLA Modules:
  0.0 268.4 jit_solution(15530738796959956978)
XLA Ops:
  2.0 0.9 shard_map.50
  3.0 7.6 %all-to-all-start = ((bf16[16,64,256]{2,1,0:T(8,128)(2,1)}), bf16[16,64,256]{2,1,0:T(8,128)(2,1)S(1)}, u32[]{:S(2)}, u32[]{:S(2)}) async-start(bf16[16,64,256]{2,1,0:T(8,128)(2,1)} %shard_map.50), calls=%async_computation | async-start | bytes 1048576 | tf_op jit(solution)/shard_map/all_to_all | solution.py:273
  10.6 4.0 %copy.10 = bf16[24,8,8,1024]{3,2,0,1:T(8,128)(2,1)} copy(bf16[24,8,8,1024]{3,2,1,0:T(8,128)(2,1)} %bitcast.16) | data formatting | bytes 6291456 | tf_op jit(solution)/shard_map/reshape | solution.py:275
  14.6 6.3 %all-to-all-done.parts_ref = bf16[16,64,256]{2,1,0:T(8,128)(2,1)S(1)} async-done(((bf16[16,64,256]{2,1,0:T(8,128)(2,1)}), bf16[16,64,256]{2,1,0:T(8,128)(2,1)S(1)}, u32[]{:S(2)}, u32[]{:S(2)}) %all-to-all-start) | async-done | bytes 524320 | tf_op jit(solution)/shard_map/all_to_all | solution.py:273
  20.9 0.8 copy-done.1
  21.7 3.7 %all-to-all-start.1 = ((bf16[8,192,1024]{2,1,0:T(8,128)(2,1)}), bf16[8,192,1024]{2,1,0:T(8,128)(2,1)S(1)}, u32[]{:S(2)}, u32[]{:S(2)}) async-start(bf16[8,192,1024]{2,1,0:T(8,128)(2,1)} %bitcast.15), calls=%async_computation.1 | async-start | bytes 6291456 | tf_op jit(solution)/shard_map/all_to_all | solution.py:276
  25.4 1.0 copy-done.2
  26.6 1.7 collective-permute-start
  28.3 4.0 %collective-permute-start.3 = (bf16[1552,128]{1,0:T(8,128)(2,1)S(1)}, bf16[1552,128]{1,0:T(8,128)(2,1)}, u32[]{:S(2)}, u32[]{:S(2)}) collective-permute-start(bf16[1552,128]{1,0:T(8,128)(2,1)S(1)} %shard_map.51.refs_0_), channel_id=1, source_target_pairs={{0,112},{16,0},{32,16},{48,32},{64,48},{80,64},{96,80},{112,96},{1... | collective-permute-start | bytes 1191944 | tf_op jit(solution)/shard_map/ppermute | solution.py:25
  32.3 7.3 %collective-permute-done.refs_2_ = bf16[1552,128]{1,0:T(8,128)(2,1)S(1)} collective-permute-done((bf16[1552,128]{1,0:T(8,128)(2,1)S(1)}, bf16[1552,128]{1,0:T(8,128)(2,1)S(1)}, u32[]{:S(2)}, u32[]{:S(2)}) %collective-permute-start) | collective-permute-done | bytes 397344 | tf_op jit(solution)/shard_map/ppermute | solution.py:25
  39.6 2.7 collective-permute-start.4
  42.3 3.3 %collective-permute-start.14 = (bf16[1552,128]{1,0:T(8,128)(2,1)S(1)}, bf16[1552,128]{1,0:T(8,128)(2,1)S(1)}, u32[]{:S(2)}, u32[]{:S(2)}) collective-permute-start(bf16[1552,128]{1,0:T(8,128)(2,1)S(1)} %shard_map.51.refs_0_), channel_id=1, source_target_pairs={{0,8},{8,0},{1,9},{9,1},{2,10},{10,2},{3,11},{11,3},{4,12},{12,4},... | collective-permute-start | bytes 1191944 | tf_op jit(solution)/shard_map/ppermute | solution.py:38
  45.7 3.2 %collective-permute-done.1.refs_2_ = bf16[1552,128]{1,0:T(8,128)(2,1)} collective-permute-done((bf16[1552,128]{1,0:T(8,128)(2,1)S(1)}, bf16[1552,128]{1,0:T(8,128)(2,1)}, u32[]{:S(2)}, u32[]{:S(2)}) %collective-permute-start.1) | collective-permute-done | bytes 397344 | tf_op jit(solution)/shard_map/ppermute | solution.py:25
  48.9 2.7 collective-permute-start.5
  51.5 4.3 %collective-permute-start.13 = (bf16[1552,128]{1,0:T(8,128)(2,1)}, bf16[1552,128]{1,0:T(8,128)(2,1)}, u32[]{:S(2)}, u32[]{:S(2)}) collective-permute-start(bf16[1552,128]{1,0:T(8,128)(2,1)} %collective-permute-done.3.refs_3_), channel_id=1, source_target_pairs={{0,8},{8,0},{1,9},{9,1},{2,10},{10,2},{3,11},{11,3},{4,12},{12,4},... | collective-permute-start | bytes 1191944 | tf_op jit(solution)/shard_map/ppermute | solution.py:38
  56.3 0.9 collective-permute-done.2.up_ref.refs_2_
  57.3 4.6 %collective-permute-start.10 = (bf16[1552,128]{1,0:T(8,128)(2,1)S(1)}, bf16[1552,128]{1,0:T(8,128)(2,1)}, u32[]{:S(2)}, u32[]{:S(2)}) collective-permute-start(bf16[1552,128]{1,0:T(8,128)(2,1)S(1)} %collective-permute-done.2.up_ref.refs_2_), channel_id=1, source_target_pairs={{0,8},{8,0},{1,9},{9,1},{2,10},{10,2},{3,11},{11,3},{4,12},{12,4},... | collective-permute-start | bytes 1191944 | tf_op jit(solution)/shard_map/ppermute | solution.py:38
  62.0 49.3 %shard_map.53.refs_4_ = bf16[14,1552,128]{2,1,0:T(8,128)(2,1)} custom-call(bf16[1552,128]{1,0:T(8,128)(2,1)} %copy-done.3, bf16[1552,128]{1,0:T(8,128)(2,1)} %copy-done.8, bf16[1552,128]{1,0:T(8,128)(2,1)} %copy-done.7, bf16[1552,128]{1,0:T(8,128)(2,1)} %collective-permute-done.3.refs_3_), custom_call_target="tpu_custom_call" | custom-call | bytes 3178496 | tf_op jit(solution)/shard_map/pallas_call | solution.py:218
  111.3 49.3 %shard_map.54.refs_6_ = bf16[14,1552,128]{2,1,0:T(8,128)(2,1)} custom-call(bf16[1552,128]{1,0:T(8,128)(2,1)} %copy-done.9, bf16[1552,128]{1,0:T(8,128)(2,1)} %collective-permute-done.13.refs_1_, bf16[1552,128]{1,0:T(8,128)(2,1)} %collective-permute-done.1.refs_2_, bf16[1552,128]{1,0:T(8,128)(2,1)} %collective-permute-done.4.refs_3_, ...), custom_call_target="tpu_custom_call", output_to_operand_aliasing={{}: (4, {})} | custom-call | bytes 3178496 | tf_op jit(solution)/shard_map/pallas_call | solution.py:218
  161.5 14.5 %collective-permute-start.7 = (bf16[1552,128]{1,0:T(8,128)(2,1)}, bf16[1552,128]{1,0:T(8,128)(2,1)}, u32[]{:S(2)}, u32[]{:S(2)}) collective-permute-start(bf16[1552,128]{1,0:T(8,128)(2,1)} %shard_map.52), channel_id=1, source_target_pairs={{0,120},{8,16},{16,8},{24,32},{32,24},{40,48},{48,40},{56,64},{64,... | collective-permute-start | bytes 1191944 | tf_op jit(solution)/shard_map/ppermute | solution.py:34
  176.0 73.4 %shard_map.55.refs_0_ = bf16[14,1552,128]{2,1,0:T(8,128)(2,1)} custom-call(bf16[1552,128]{1,0:T(8,128)(2,1)} %collective-permute-done.8.refs_0_, bf16[1552,128]{1,0:T(8,128)(2,1)} %collective-permute-done.9.refs_1_, bf16[1552,128]{1,0:T(8,128)(2,1)} %copy-done.4, ...), custom_call_target="tpu_custom_call", output_to_operand_aliasing={{}: (6, {})} | custom-call | bytes 4767744 | tf_op jit(solution)/shard_map/pallas_call | solution.py:218
  249.4 2.6 copy-done
  252.0 10.2 %shard_map.56 = (f32[1000,1024]{1,0:T(8,128)S(1)}, f32[2,1024]{1,0:T(2,128)S(1)}) custom-call(bf16[14,1552,128]{2,1,0:T(8,128)(2,1)S(1)} %copy-done, bf16[1536,1024]{1,0:T(8,128)(2,1)S(1)} %bitcast.12), custom_call_target="tpu_custom_call" | custom-call | flops 9307160576 | bytes 4096000 | tf_op jit(solution)/shard_map/pallas_call | solution.py:182
  262.2 6.0 %shard_map.57 = (f32[1000,1024]{1,0:T(8,128)}, f32[1,1024]{1,0:T(1,128)}) custom-call(bf16[1552,128]{1,0:T(8,128)(2,1)} %collective-permute-done.6.refs_0_, bf16[1552,128]{1,0:T(8,128)(2,1)} %collective-permute-done.7.refs_1_, bf16[1536,1024]{1,0:T(8,128)(2,1)S(1)} %bitcast.13, f32[1000,1024]{1,0:T(8,128)S(1)} %get-tuple-element.8.refs_3_, ...), custom_call_target="tpu_custom_call" | custom-call | flops 1329594368 | bytes 4096000 | tf_op jit(solution)/shard_map/pallas_call | solution.py:182
  (39 shorter events, 3.1 us)
Async XLA Ops:
  3.0 17.9 %all-to-all-start = ((bf16[16,64,256]{2,1,0:T(8,128)(2,1)}), bf16[16,64,256]{2,1,0:T(8,128)(2,1)S(1)}, u32[]{:S(2)}, u32[]{:S(2)}) async-start(bf16[16,64,256]{2,1,0:T(8,128)(2,1)} %shard_map.50), calls=%async_computation | async-start | bytes 1048576 | tf_op jit(solution)/shard_map/all_to_all | solution.py:273
  21.7 227.7 %all-to-all-start.1 = ((bf16[8,192,1024]{2,1,0:T(8,128)(2,1)}), bf16[8,192,1024]{2,1,0:T(8,128)(2,1)S(1)}, u32[]{:S(2)}, u32[]{:S(2)}) async-start(bf16[8,192,1024]{2,1,0:T(8,128)(2,1)} %bitcast.15), calls=%async_computation.1 | async-start | bytes 6291456 | tf_op jit(solution)/shard_map/all_to_all | solution.py:276
  25.4 1.0 copy-start.2
  26.6 35.4 %copy-start.3 = (bf16[1552,128]{1,0:T(8,128)(2,1)}, bf16[1552,128]{1,0:T(8,128)(2,1)S(1)}, u32[]{:S(2)}) copy-start(bf16[1552,128]{1,0:T(8,128)(2,1)S(1)} %shard_map.51.refs_0_) | copy-start | bytes 1191940
  26.6 13.0 %collective-permute-start = (bf16[1552,128]{1,0:T(8,128)(2,1)S(1)}, bf16[1552,128]{1,0:T(8,128)(2,1)S(1)}, u32[]{:S(2)}, u32[]{:S(2)}) collective-permute-start(bf16[1552,128]{1,0:T(8,128)(2,1)S(1)} %shard_map.51.refs_0_), channel_id=1, source_target_pairs={{0,16},{16,32},{32,48},{48,64},{64,80},{80,96},{96,112},{112,0},{1... | collective-permute-start | bytes 1191944 | tf_op jit(solution)/shard_map/ppermute | solution.py:25
  28.3 11.3 %collective-permute-start.3 = (bf16[1552,128]{1,0:T(8,128)(2,1)S(1)}, bf16[1552,128]{1,0:T(8,128)(2,1)}, u32[]{:S(2)}, u32[]{:S(2)}) collective-permute-start(bf16[1552,128]{1,0:T(8,128)(2,1)S(1)} %shard_map.51.refs_0_), channel_id=1, source_target_pairs={{0,112},{16,0},{32,16},{48,32},{64,48},{80,64},{96,80},{112,96},{1... | collective-permute-start | bytes 1191944 | tf_op jit(solution)/shard_map/ppermute | solution.py:25
  39.6 17.6 %copy-start.7 = (bf16[1552,128]{1,0:T(8,128)(2,1)}, bf16[1552,128]{1,0:T(8,128)(2,1)S(1)}, u32[]{:S(2)}) copy-start(bf16[1552,128]{1,0:T(8,128)(2,1)S(1)} %collective-permute-done.refs_2_) | copy-start | bytes 1191940
  39.6 9.2 %collective-permute-start.1 = (bf16[1552,128]{1,0:T(8,128)(2,1)S(1)}, bf16[1552,128]{1,0:T(8,128)(2,1)}, u32[]{:S(2)}, u32[]{:S(2)}) collective-permute-start(bf16[1552,128]{1,0:T(8,128)(2,1)S(1)} %collective-permute-done.refs_2_), channel_id=1, source_target_pairs={{0,16},{16,32},{32,48},{48,64},{64,80},{80,96},{96,112},{112,0},{1... | collective-permute-start | bytes 1191944 | tf_op jit(solution)/shard_map/ppermute | solution.py:25
  39.6 9.2 %collective-permute-start.4 = (bf16[1552,128]{1,0:T(8,128)(2,1)}, bf16[1552,128]{1,0:T(8,128)(2,1)}, u32[]{:S(2)}, u32[]{:S(2)}) collective-permute-start(bf16[1552,128]{1,0:T(8,128)(2,1)} %collective-permute-done.3.refs_3_), channel_id=1, source_target_pairs={{0,112},{16,0},{32,16},{48,32},{64,48},{80,64},{96,80},{112,96},{1... | collective-permute-start | bytes 1191944 | tf_op jit(solution)/shard_map/ppermute | solution.py:25
  42.3 13.5 %collective-permute-start.14 = (bf16[1552,128]{1,0:T(8,128)(2,1)S(1)}, bf16[1552,128]{1,0:T(8,128)(2,1)S(1)}, u32[]{:S(2)}, u32[]{:S(2)}) collective-permute-start(bf16[1552,128]{1,0:T(8,128)(2,1)S(1)} %shard_map.51.refs_0_), channel_id=1, source_target_pairs={{0,8},{8,0},{1,9},{9,1},{2,10},{10,2},{3,11},{11,3},{4,12},{12,4},... | collective-permute-start | bytes 1191944 | tf_op jit(solution)/shard_map/ppermute | solution.py:38
  45.6 10.2 %collective-permute-start.12 = (bf16[1552,128]{1,0:T(8,128)(2,1)S(1)}, bf16[1552,128]{1,0:T(8,128)(2,1)S(1)}, u32[]{:S(2)}, u32[]{:S(2)}) collective-permute-start(bf16[1552,128]{1,0:T(8,128)(2,1)S(1)} %collective-permute-done.refs_2_), channel_id=1, source_target_pairs={{0,8},{8,0},{1,9},{9,1},{2,10},{10,2},{3,11},{11,3},{4,12},{12,4},... | collective-permute-start | bytes 1191944 | tf_op jit(solution)/shard_map/ppermute | solution.py:38
  48.8 8.4 %collective-permute-start.2 = (bf16[1552,128]{1,0:T(8,128)(2,1)}, bf16[1552,128]{1,0:T(8,128)(2,1)S(1)}, u32[]{:S(2)}, u32[]{:S(2)}) collective-permute-start(bf16[1552,128]{1,0:T(8,128)(2,1)} %collective-permute-done.1.refs_2_), channel_id=1, source_target_pairs={{0,16},{16,32},{32,48},{48,64},{64,80},{80,96},{96,112},{112,0},{1... | collective-permute-start | bytes 1191944 | tf_op jit(solution)/shard_map/ppermute | solution.py:25
  48.9 13.0 %collective-permute-start.5 = (bf16[1552,128]{1,0:T(8,128)(2,1)}, bf16[1552,128]{1,0:T(8,128)(2,1)}, u32[]{:S(2)}, u32[]{:S(2)}) collective-permute-start(bf16[1552,128]{1,0:T(8,128)(2,1)} %collective-permute-done.4.refs_3_), channel_id=1, source_target_pairs={{0,112},{16,0},{32,16},{48,32},{64,48},{80,64},{96,80},{112,96},{1... | collective-permute-start | bytes 1191944 | tf_op jit(solution)/shard_map/ppermute | solution.py:25
  51.5 59.8 %collective-permute-start.13 = (bf16[1552,128]{1,0:T(8,128)(2,1)}, bf16[1552,128]{1,0:T(8,128)(2,1)}, u32[]{:S(2)}, u32[]{:S(2)}) collective-permute-start(bf16[1552,128]{1,0:T(8,128)(2,1)} %collective-permute-done.3.refs_3_), channel_id=1, source_target_pairs={{0,8},{8,0},{1,9},{9,1},{2,10},{10,2},{3,11},{11,3},{4,12},{12,4},... | collective-permute-start | bytes 1191944 | tf_op jit(solution)/shard_map/ppermute | solution.py:38
  55.8 6.1 %copy-start.8 = (bf16[1552,128]{1,0:T(8,128)(2,1)}, bf16[1552,128]{1,0:T(8,128)(2,1)S(1)}, u32[]{:S(2)}) copy-start(bf16[1552,128]{1,0:T(8,128)(2,1)S(1)} %collective-permute-done.14.refs_1_) | copy-start | bytes 1191940
  55.8 105.7 %collective-permute-start.8 = (bf16[1552,128]{1,0:T(8,128)(2,1)}, bf16[1552,128]{1,0:T(8,128)(2,1)}, u32[]{:S(2)}, u32[]{:S(2)}) collective-permute-start(bf16[1552,128]{1,0:T(8,128)(2,1)} %collective-permute-done.1.refs_2_), channel_id=1, source_target_pairs={{0,8},{8,0},{1,9},{9,1},{2,10},{10,2},{3,11},{11,3},{4,12},{12,4},... | collective-permute-start | bytes 1191944 | tf_op jit(solution)/shard_map/ppermute | solution.py:38
  55.9 6.0 %copy-start.9 = (bf16[1552,128]{1,0:T(8,128)(2,1)}, bf16[1552,128]{1,0:T(8,128)(2,1)S(1)}, u32[]{:S(2)}) copy-start(bf16[1552,128]{1,0:T(8,128)(2,1)S(1)} %collective-permute-done.12.refs_0_) | copy-start | bytes 1191940
  55.9 120.1 %collective-permute-start.9 = (bf16[1552,128]{1,0:T(8,128)(2,1)}, bf16[1552,128]{1,0:T(8,128)(2,1)}, u32[]{:S(2)}, u32[]{:S(2)}) collective-permute-start(bf16[1552,128]{1,0:T(8,128)(2,1)} %collective-permute-done.4.refs_3_), channel_id=1, source_target_pairs={{0,8},{8,0},{1,9},{9,1},{2,10},{10,2},{3,11},{11,3},{4,12},{12,4},... | collective-permute-start | bytes 1191944 | tf_op jit(solution)/shard_map/ppermute | solution.py:38
  57.3 103.3 %copy-start.4 = (bf16[1552,128]{1,0:T(8,128)(2,1)}, bf16[1552,128]{1,0:T(8,128)(2,1)S(1)}, u32[]{:S(2)}) copy-start(bf16[1552,128]{1,0:T(8,128)(2,1)S(1)} %collective-permute-done.2.up_ref.refs_2_) | copy-start | bytes 1191940
  57.3 118.7 %collective-permute-start.10 = (bf16[1552,128]{1,0:T(8,128)(2,1)S(1)}, bf16[1552,128]{1,0:T(8,128)(2,1)}, u32[]{:S(2)}, u32[]{:S(2)}) collective-permute-start(bf16[1552,128]{1,0:T(8,128)(2,1)S(1)} %collective-permute-done.2.up_ref.refs_2_), channel_id=1, source_target_pairs={{0,8},{8,0},{1,9},{9,1},{2,10},{10,2},{3,11},{11,3},{4,12},{12,4},... | collective-permute-start | bytes 1191944 | tf_op jit(solution)/shard_map/ppermute | solution.py:38
  61.9 114.1 %collective-permute-start.11 = (bf16[1552,128]{1,0:T(8,128)(2,1)}, bf16[1552,128]{1,0:T(8,128)(2,1)}, u32[]{:S(2)}, u32[]{:S(2)}) collective-permute-start(bf16[1552,128]{1,0:T(8,128)(2,1)} %collective-permute-done.5.down_ref.refs_3_), channel_id=1, source_target_pairs={{0,8},{8,0},{1,9},{9,1},{2,10},{10,2},{3,11},{11,3},{4,12},{12,4},... | collective-permute-start | bytes 1191944 | tf_op jit(solution)/shard_map/ppermute | solution.py:38
  161.4 100.8 %collective-permute-start.6 = (bf16[1552,128]{1,0:T(8,128)(2,1)}, bf16[1552,128]{1,0:T(8,128)(2,1)}, u32[]{:S(2)}, u32[]{:S(2)}) collective-permute-start(bf16[1552,128]{1,0:T(8,128)(2,1)} %shard_map.52), channel_id=1, source_target_pairs={{0,112},{8,24},{16,0},{24,40},{32,16},{40,56},{48,32},{56,72},{64,... | collective-permute-start | bytes 1191944 | tf_op jit(solution)/shard_map/ppermute | solution.py:34
  161.5 100.7 %collective-permute-start.7 = (bf16[1552,128]{1,0:T(8,128)(2,1)}, bf16[1552,128]{1,0:T(8,128)(2,1)}, u32[]{:S(2)}, u32[]{:S(2)}) collective-permute-start(bf16[1552,128]{1,0:T(8,128)(2,1)} %shard_map.52), channel_id=1, source_target_pairs={{0,120},{8,16},{16,8},{24,32},{32,24},{40,48},{48,40},{56,64},{64,... | collective-permute-start | bytes 1191944 | tf_op jit(solution)/shard_map/ppermute | solution.py:34
  249.4 2.6 copy-start
  (3 other events, 2.2 us)

commit v4 on v3

--- a/solution.py
+++ b/solution.py
@@ -38,17 +38,16 @@
     return lax.ppermute(x, "c", [(0, 1), (1, 0)])
 
 
-def move(kernel, shape, args, scratch=()):
+def move(kernel, shape, args, vmem=4):
     return pl.pallas_call(
         kernel,
         out_shape=jax.ShapeDtypeStruct(shape, jnp.bfloat16),
         in_specs=[VMEM] * len(args),
         out_specs=VMEM,
-        scratch_shapes=list(scratch),
         cost_estimate=pl.CostEstimate(
             flops=0, bytes_accessed=4 * math.prod(shape), transcendentals=0
         ),
-        compiler_params=pltpu.CompilerParams(vmem_limit_bytes=4 * 2**20),
+        compiler_params=pltpu.CompilerParams(vmem_limit_bytes=vmem * 2**20),
     )(*args)
 
 
@@ -85,13 +84,18 @@
 
 
 def attend_kernel(pieces, first, last, scale, *refs):
-    given = 1 if first else pieces
-    labels = refs[:given]
-    pool_ref = refs[given]
-    refs = refs[given + 1 :]
+    labels = refs[:pieces]
+    pool_ref = refs[pieces]
+    refs = refs[pieces + 1 :]
     if first:
-        out_ref, stat_ref, scores, weights, onehot = refs
-        labels = [labels[0].at[p] for p in range(pieces)]
+        out_ref, stat_ref, scores, weights, onehot, held, sems = refs
+        fetches = [
+            pltpu.make_async_copy(ref, held.at[p], sems.at[p])
+            for p, ref in enumerate(labels)
+        ]
+        for fetch in fetches:
+            fetch.start()
+        labels = [held.at[p] for p in range(pieces)]
     elif last:
         old_mass, old_stat, out_ref, stat_ref, scores, weights, onehot, logs, sems = refs
     else:
@@ -101,6 +105,9 @@
     top = None if first else old_stat[0:1]
     for pair in range(pieces // 2):
         two = labels[2 * pair : 2 * pair + 2]
+        if first:
+            fetches[2 * pair].wait()
+            fetches[2 * pair + 1].wait()
         keys = jnp.concatenate(
             [
                 jnp.concatenate(
@@ -130,19 +137,21 @@
         weights[at, :] = block.astype(jnp.bfloat16)
         part = jnp.sum(block, axis=0, keepdims=True)
         total = part if total is None else total + part
-    mass = jnp.dot(onehot[...], weights[...], preferred_element_type=jnp.float32)
     if not first:
         fade = jnp.exp(old_stat[0:1] - top)
         total = total + fade * old_stat[1:2]
-        mass = mass + fade * old_mass[...]
     if last:
         gain = (1.0 - SMOOTHING) / total
+        kept = fade * gain
         entropy = jnp.zeros_like(total)
         step = 200
         copies = []
         for i in range(C // step):
             at = slice(i * step, (i + 1) * step)
-            probability = mass[at] * gain + SMOOTHING / C
+            mass = jnp.dot(
+                onehot[at, :], weights[...], preferred_element_type=jnp.float32
+            )
+            probability = mass * gain + (old_mass[at, :] * kept + SMOOTHING / C)
             log_probs = jnp.log(probability)
             logs[at, :] = log_probs
             copies.append(
@@ -154,7 +163,8 @@
         for copy in copies:
             copy.wait()
     else:
-        out_ref[...] = mass
+        mass = jnp.dot(onehot[...], weights[...], preferred_element_type=jnp.float32)
+        out_ref[...] = mass if first else mass + fade * old_mass[...]
         stat_ref[0:1] = top
         stat_ref[1:2] = total
 
@@ -162,36 +172,42 @@
 def attend(pool, labels, state, last):
     depth, count = pool.shape
     first = state is None
-    pieces = labels.shape[0] if first else len(labels)
+    pieces = len(labels)
     m = pieces * 128
-    args = ([labels] if first else list(labels)) + [pool]
-    args += [] if first else list(state)
+    pool = pltpu.with_memory_space_constraint(pool, pltpu.VMEM)
+    args = list(labels) + [pool] + ([] if first else list(state))
     scratch = [
         pltpu.VMEM((m, count), jnp.float32),
         pltpu.VMEM((m, count), jnp.bfloat16),
         pltpu.VMEM((C, m), jnp.bfloat16),
     ]
     need = 6 * m * count + 2 * C * m + 4 * C * count
+    if first:
+        scratch += [
+            pltpu.VMEM((pieces,) + labels[0].shape, jnp.bfloat16),
+            pltpu.SemaphoreType.DMA((pieces,)),
+        ]
     if last:
         scratch += [
             pltpu.VMEM((C, count), jnp.float32),
             pltpu.SemaphoreType.DMA((C // 200,)),
         ]
         need += 4 * C * count
-    label_specs = [VMEM] if first else [VMEM] * pieces
+    label_specs = [ANY if first else VMEM] * pieces
+    place = jax.ShapeDtypeStruct if last else pltpu.VMEM
     return pl.pallas_call(
         functools.partial(attend_kernel, pieces, first, last, 2.0 / math.sqrt(depth)),
         in_specs=label_specs + [VMEM] * (len(args) - len(label_specs)),
         out_specs=[ANY if last else VMEM, VMEM],
         out_shape=[
-            jax.ShapeDtypeStruct((C, count), jnp.float32),
-            jax.ShapeDtypeStruct((1 if last else 2, count), jnp.float32),
+            place((C, count), jnp.float32),
+            place((1 if last else 2, count), jnp.float32),
         ],
         scratch_shapes=scratch,
         input_output_aliases={}
         if first or last
         else {pieces + 1: 0, pieces + 2: 1},
-        compiler_params=pltpu.CompilerParams(vmem_limit_bytes=need + 8 * 2**20),
+        compiler_params=pltpu.CompilerParams(vmem_limit_bytes=53 * 2**20 if first else need + 8 * 2**20),
         cost_estimate=pl.CostEstimate(
             flops=2 * m * count * (depth + C),
             bytes_accessed=4 * C * count,
@@ -200,65 +216,16 @@
     )(*args)
 
 
-def stash_kernel(count, at, *refs):
-    out_ref, sems = refs[-2:]
-    copies = [
-        pltpu.make_async_copy(refs[i], out_ref.at[at + i], sems.at[i])
-        for i in range(count)
-    ]
-    for copy in copies:
-        copy.start()
-    for copy in copies:
-        copy.wait()
-
-
-def stash(store, pieces, at, slots):
-    shape = (slots,) + pieces[0].shape
-    args = list(pieces) + ([] if store is None else [store])
-    return pl.pallas_call(
-        functools.partial(stash_kernel, len(pieces), at),
-        in_specs=[ANY] * len(args),
-        out_specs=ANY,
-        out_shape=jax.ShapeDtypeStruct(shape, jnp.bfloat16),
-        scratch_shapes=[pltpu.SemaphoreType.DMA((len(pieces),))],
-        input_output_aliases={} if store is None else {len(pieces): 0},
-        cost_estimate=pl.CostEstimate(
-            flops=0,
-            bytes_accessed=4 * len(pieces) * math.prod(shape[1:]),
-            transcendentals=0,
-        ),
-        compiler_params=pltpu.CompilerParams(vmem_limit_bytes=60 * 2**20),
-    )(*args)
-
-
-def choose_kernel(up_ref, down_ref, out_ref, sem):
+def choose_kernel(up_ref, down_ref, out_ref):
     core = lax.axis_index("c")
 
     @pl.when(core == 0)
     def _():
-        copy = pltpu.make_async_copy(down_ref, out_ref, sem)
-        copy.start()
-        copy.wait()
+        out_ref[...] = down_ref[...]
 
     @pl.when(core != 0)
     def _():
-        copy = pltpu.make_async_copy(up_ref, out_ref, sem)
-        copy.start()
-        copy.wait()
-
-
-def choose(up, down):
-    return pl.pallas_call(
-        choose_kernel,
-        in_specs=[ANY, ANY],
-        out_specs=ANY,
-        out_shape=jax.ShapeDtypeStruct(up.shape, up.dtype),
-        scratch_shapes=[pltpu.SemaphoreType.DMA],
-        cost_estimate=pl.CostEstimate(
-            flops=0, bytes_accessed=4 * up.size, transcendentals=0
-        ),
-        compiler_params=pltpu.CompilerParams(vmem_limit_bytes=2**20),
-    )(up, down)
+        out_ref[...] = up_ref[...]
 
 
 def per_device(pool_embed, label_embed, label_class):
@@ -269,25 +236,23 @@
         pack_kernel,
         (16, rows, width + rows),
         (label_embed, label_class.reshape(1, rows)),
+        60,
     )
     parts = lax.all_to_all(own, PLANE, 0, 0, tiled=True)
     own, pool_embed = lax.optimization_barrier((own, pool_embed))
     queries = pool_embed.T.reshape(width, feats, count).transpose(1, 0, 2)
+    plane = move(arrange_kernel, (12 * 2 * rows + TAIL, LANES), (parts,))
+    plane, queries = lax.optimization_barrier((plane, queries))
     pool = lax.all_to_all(queries, FEAT, 0, 0, tiled=True)
     pool = pool.reshape(feats * width, count)
-    plane = move(arrange_kernel, (12 * 2 * rows + TAIL, LANES), (parts,))
-    slots = 14
-    up, down = along_z(plane, 1), along_z(plane, -1)
-    store = stash(None, [plane, swap(plane), up, down], 0, slots)
-    others = [swap(up), swap(down)]
-    up, down = along_z(up, 1), along_z(down, -1)
-    store = stash(store, others + [up, down], 4, slots)
-    others = [swap(up), swap(down)]
-    up, down = along_z(up, 1), along_z(down, -1)
-    store = stash(store, others + [up, down, swap(up), swap(down)], 8, slots)
-    far = choose(up, down)
+    got = [plane, swap(plane)]
+    up, down = plane, plane
+    for _ in range(3):
+        up, down = along_z(up, 1), along_z(down, -1)
+        got += [up, down, swap(up), swap(down)]
+    far = move(choose_kernel, up.shape, (up, down))
     ends = [outward(far, 0), outward(far, 1)]
-    state = attend(pool, store, None, False)
+    state = attend(pool, got, None, False)
     log_probs, entropy = attend(pool, ends, state, True)
     return (log_probs.T, entropy[0])
 

time: 269 us -> 81.9 us (0.30)
  Pallas kernels: 190 us -> 20.2 us
  starting transfers between devices: 49.7 us -> 37.4 us
  local copies, waits for them, and re-layouts: 9.84 us -> 5.5 us
    pallas_call x4 -> x0, Pallas kernels: 173 us -> none  [the longest x3 172 us: stash(): pl.pallas_call(functools.partial(stash_kernel, len(pieces), at), in_specs...]
    ppermute x2, starting transfers between devices: 14.5 us -> 2.17 us  [outward(): return lax.ppermute(x, ('z', 'c'), pairs)]
    unnamed x20 -> x26, local copies, waits for them, and re-layouts: 5.85 us -> 1.51 us
  transfers between devices with their start and end apart: 17 -> 17, of which waited for: 4 -> 4; matrix products, arithmetic and copies ran while one was open for 1% -> 5% of each run, Pallas kernels for 68% -> 16%
where the time goes in v4:
time: 81.9 us; the launch traced here: 81.5 us
  starting transfers between devices  37.4 us (46%)
  Pallas kernels  20.2 us (25%)
  waiting for transfers between devices  17.4 us (21%)
  local copies, waits for them, and re-layouts  5.5 us (7%)
  between operations  1.01 us (1%)
    pallas_call x2, Pallas kernels, attend(): pl.pallas_call(functools.partial(attend_kernel, pieces, first, last, 2.0...  18.4 us
    ppermute x7, starting transfers between devices, swap(): return lax.ppermute(x, 'c', [(0, 1), (1, 0)])  12.9 us
    ppermute x6, waiting for transfers between devices, along_z(): return lax.ppermute(x, 'z', [(i, (i + step) % n) for i in range(n)])  11.1 us
    ppermute x6, starting transfers between devices, along_z(): return lax.ppermute(x, 'z', [(i, (i + step) % n) for i in range(n)])  11.1 us
    all_to_all x1, starting transfers between devices, per_device(): parts = lax.all_to_all(own, PLANE, 0, 0, tiled=True)  7.58 us
    all_to_all x1, waiting for transfers between devices, per_device(): parts = lax.all_to_all(own, PLANE, 0, 0, tiled=True)  6.31 us
    reshape x1, local copies, waits for them, and re-layouts, per_device(): queries = pool_embed.T.reshape(width, feats, count).transpose(1, 0, 2)  3.99 us
    all_to_all x1, starting transfers between devices, per_device(): pool = lax.all_to_all(queries, FEAT, 0, 0, tiled=True)  3.66 us
  transfers between devices with their start and end apart: 17, of which 4 were waited for; matrix products, arithmetic and copies ran while one was open for 5% of the time, Pallas kernels for 16%

profile of v4, /device:TPU:1, one launch (start us, length us, event | category | flops | bytes accessed | tf_op | source)
XLA Modules:
  0.0 81.5 jit_solution(17731263780912900172)
XLA Ops:
  0.6 1.7 %shard_map.50 = bf16[16,64,256]{2,1,0:T(8,128)(2,1)} custom-call(bf16[64,192]{1,0:T(8,128)(2,1)} %label_ref.1, s32[1,64]{1,0:T(1,128)} %bitcast.16), custom_call_target="tpu_custom_call" | custom-call | bytes 1048576 | tf_op jit(solution)/shard_map/pallas_call | solution.py:42
  2.3 7.6 %all-to-all-start = ((bf16[16,64,256]{2,1,0:T(8,128)(2,1)}), bf16[16,64,256]{2,1,0:T(8,128)(2,1)S(1)}, u32[]{:S(2)}, u32[]{:S(2)}) async-start(bf16[16,64,256]{2,1,0:T(8,128)(2,1)} %shard_map.50), calls=%async_computation | async-start | bytes 1048576 | tf_op jit(solution)/shard_map/all_to_all | solution.py:241
  9.9 4.0 %copy.8 = bf16[24,8,8,1024]{3,2,0,1:T(8,128)(2,1)} copy(bf16[24,8,8,1024]{3,2,1,0:T(8,128)(2,1)} %bitcast.15) | data formatting | bytes 6291456 | tf_op jit(solution)/shard_map/reshape | solution.py:243
  13.9 6.3 %all-to-all-done.parts_ref = bf16[16,64,256]{2,1,0:T(8,128)(2,1)S(1)} async-done(((bf16[16,64,256]{2,1,0:T(8,128)(2,1)}), bf16[16,64,256]{2,1,0:T(8,128)(2,1)S(1)}, u32[]{:S(2)}, u32[]{:S(2)}) %all-to-all-start) | async-done | bytes 524320 | tf_op jit(solution)/shard_map/all_to_all | solution.py:241
  20.2 0.2 shard_map.51.refs_0_
  20.4 3.7 %all-to-all-start.1 = ((bf16[8,192,1024]{2,1,0:T(8,128)(2,1)}), bf16[8,192,1024]{2,1,0:T(8,128)(2,1)S(1)}, u32[]{:S(2)}, u32[]{:S(2)}) async-start(bf16[8,192,1024]{2,1,0:T(8,128)(2,1)} %bitcast.14), calls=%async_computation.1 | async-start | bytes 6291456 | tf_op jit(solution)/shard_map/all_to_all | solution.py:246
  24.1 1.7 %collective-permute-start = (bf16[1552,128]{1,0:T(8,128)(2,1)S(1)}, bf16[1552,128]{1,0:T(8,128)(2,1)S(1)}, u32[]{:S(2)}, u32[]{:S(2)}) collective-permute-start(bf16[1552,128]{1,0:T(8,128)(2,1)S(1)} %shard_map.51.refs_0_), channel_id=1, source_target_pairs={{0,16},{16,32},{32,48},{48,64},{64,80},{80,96},{96,112},{112,0},{1... | collective-permute-start | bytes 1191944 | tf_op jit(solution)/shard_map/ppermute | solution.py:25
  25.8 4.0 %collective-permute-start.3 = (bf16[1552,128]{1,0:T(8,128)(2,1)S(1)}, bf16[1552,128]{1,0:T(8,128)(2,1)S(1)}, u32[]{:S(2)}, u32[]{:S(2)}) collective-permute-start(bf16[1552,128]{1,0:T(8,128)(2,1)S(1)} %shard_map.51.refs_0_), channel_id=1, source_target_pairs={{0,112},{16,0},{32,16},{48,32},{64,48},{80,64},{96,80},{112,96},{1... | collective-permute-start | bytes 1191944 | tf_op jit(solution)/shard_map/ppermute | solution.py:25
  29.8 7.3 %collective-permute-done.refs_2_ = bf16[1552,128]{1,0:T(8,128)(2,1)S(1)} collective-permute-done((bf16[1552,128]{1,0:T(8,128)(2,1)S(1)}, bf16[1552,128]{1,0:T(8,128)(2,1)S(1)}, u32[]{:S(2)}, u32[]{:S(2)}) %collective-permute-start) | collective-permute-done | bytes 397344 | tf_op jit(solution)/shard_map/ppermute | solution.py:25
  37.1 2.7 %collective-permute-start.4 = (bf16[1552,128]{1,0:T(8,128)(2,1)S(1)}, bf16[1552,128]{1,0:T(8,128)(2,1)S(1)}, u32[]{:S(2)}, u32[]{:S(2)}) collective-permute-start(bf16[1552,128]{1,0:T(8,128)(2,1)S(1)} %collective-permute-done.3.refs_3_), channel_id=1, source_target_pairs={{0,112},{16,0},{32,16},{48,32},{64,48},{80,64},{96,80},{112,96},{1... | collective-permute-start | bytes 1191944 | tf_op jit(solution)/shard_map/ppermute | solution.py:25
  39.8 3.3 %collective-permute-start.8 = (bf16[1552,128]{1,0:T(8,128)(2,1)S(1)}, bf16[1552,128]{1,0:T(8,128)(2,1)S(1)}, u32[]{:S(2)}, u32[]{:S(2)}) collective-permute-start(bf16[1552,128]{1,0:T(8,128)(2,1)S(1)} %shard_map.51.refs_0_), channel_id=1, source_target_pairs={{0,8},{8,0},{1,9},{9,1},{2,10},{10,2},{3,11},{11,3},{4,12},{12,4},... | collective-permute-start | bytes 1191944 | tf_op jit(solution)/shard_map/ppermute | solution.py:38
  43.1 3.1 %collective-permute-done.1.refs_6_ = bf16[1552,128]{1,0:T(8,128)(2,1)S(1)} collective-permute-done((bf16[1552,128]{1,0:T(8,128)(2,1)S(1)}, bf16[1552,128]{1,0:T(8,128)(2,1)S(1)}, u32[]{:S(2)}, u32[]{:S(2)}) %collective-permute-start.1) | collective-permute-done | bytes 397344 | tf_op jit(solution)/shard_map/ppermute | solution.py:25
  46.2 2.7 %collective-permute-start.5 = (bf16[1552,128]{1,0:T(8,128)(2,1)S(1)}, bf16[1552,128]{1,0:T(8,128)(2,1)S(1)}, u32[]{:S(2)}, u32[]{:S(2)}) collective-permute-start(bf16[1552,128]{1,0:T(8,128)(2,1)S(1)} %collective-permute-done.4.refs_7_), channel_id=1, source_target_pairs={{0,112},{16,0},{32,16},{48,32},{64,48},{80,64},{96,80},{112,96},{1... | collective-permute-start | bytes 1191944 | tf_op jit(solution)/shard_map/ppermute | solution.py:25
  48.9 4.3 %collective-permute-start.9 = (bf16[1552,128]{1,0:T(8,128)(2,1)S(1)}, bf16[1552,128]{1,0:T(8,128)(2,1)S(1)}, u32[]{:S(2)}, u32[]{:S(2)}) collective-permute-start(bf16[1552,128]{1,0:T(8,128)(2,1)S(1)} %collective-permute-done.refs_2_), channel_id=1, source_target_pairs={{0,8},{8,0},{1,9},{9,1},{2,10},{10,2},{3,11},{11,3},{4,12},{12,4},... | collective-permute-start | bytes 1191944 | tf_op jit(solution)/shard_map/ppermute | solution.py:38
  53.2 0.1 collective-permute-start.11
  53.3 0.4 collective-permute-start.12
  53.7 0.7 collective-permute-done.2.up_ref.refs_10_
  54.4 4.6 %collective-permute-start.13 = (bf16[1552,128]{1,0:T(8,128)(2,1)S(1)}, bf16[1552,128]{1,0:T(8,128)(2,1)S(1)}, u32[]{:S(2)}, u32[]{:S(2)}) collective-permute-start(bf16[1552,128]{1,0:T(8,128)(2,1)S(1)} %collective-permute-done.2.up_ref.refs_10_), channel_id=1, source_target_pairs={{0,8},{8,0},{1,9},{9,1},{2,10},{10,2},{3,11},{11,3},{4,12},{12,4},... | collective-permute-start | bytes 1191944 | tf_op jit(solution)/shard_map/ppermute | solution.py:38
  59.1 0.1 collective-permute-start.14
  59.3 2.1 %collective-permute-start.7 = (bf16[1552,128]{1,0:T(8,128)(2,1)S(1)}, bf16[1552,128]{1,0:T(8,128)(2,1)}, u32[]{:S(2)}, u32[]{:S(2)}) collective-permute-start(bf16[1552,128]{1,0:T(8,128)(2,1)S(1)} %shard_map.52), channel_id=1, source_target_pairs={{0,120},{8,16},{16,8},{24,32},{32,24},{40,48},{48,40},{56,64},{64,... | collective-permute-start | bytes 1191944 | tf_op jit(solution)/shard_map/ppermute | solution.py:34
  61.5 0.7 copy-done.11
  62.2 0.8 copy-done.12
  63.0 13.0 %shard_map.53 = (f32[1000,1024]{1,0:T(8,128)S(1)}, f32[2,1024]{1,0:T(2,128)S(1)}) custom-call(bf16[1552,128]{1,0:T(8,128)(2,1)} %copy-done, bf16[1552,128]{1,0:T(8,128)(2,1)} %copy-done.7, bf16[1552,128]{1,0:T(8,128)(2,1)} %copy-done.3, bf16[1552,128]{1,0:T(8,128)(2,1)} %copy-done.4, bf16[1552,128]{1,0:T(8,128)(2,1)} %copy-done.9, ...), custom_call_target="tpu_custom_call" | custom-call | flops 9307160576 | bytes 4096000 | tf_op jit(solution)/shard_map/pallas_call | solution.py:198
  76.0 5.4 %shard_map.54 = (f32[1000,1024]{1,0:T(8,128)}, f32[1,1024]{1,0:T(1,128)}) custom-call(bf16[1552,128]{1,0:T(8,128)(2,1)} %collective-permute-done.6.refs_0_, bf16[1552,128]{1,0:T(8,128)(2,1)} %collective-permute-done.7.refs_1_, bf16[1536,1024]{1,0:T(8,128)(2,1)S(1)} %bitcast.13, f32[1000,1024]{1,0:T(8,128)S(1)} %get-tuple-element.12.refs_3_, ...), custom_call_target="tpu_custom_call" | custom-call | flops 1329594368 | bytes 4096000 | tf_op jit(solution)/shard_map/pallas_call | solution.py:198
  (42 shorter events, 0.2 us)
Async XLA Ops:
  2.3 17.9 %all-to-all-start = ((bf16[16,64,256]{2,1,0:T(8,128)(2,1)}), bf16[16,64,256]{2,1,0:T(8,128)(2,1)S(1)}, u32[]{:S(2)}, u32[]{:S(2)}) async-start(bf16[16,64,256]{2,1,0:T(8,128)(2,1)} %shard_map.50), calls=%async_computation | async-start | bytes 1048576 | tf_op jit(solution)/shard_map/all_to_all | solution.py:241
  20.4 19.4 %copy-start = (bf16[1552,128]{1,0:T(8,128)(2,1)}, bf16[1552,128]{1,0:T(8,128)(2,1)S(1)}, u32[]{:S(2)}) copy-start(bf16[1552,128]{1,0:T(8,128)(2,1)S(1)} %shard_map.51.refs_0_) | copy-start | bytes 1191940
  20.4 42.6 %all-to-all-start.1 = ((bf16[8,192,1024]{2,1,0:T(8,128)(2,1)}), bf16[8,192,1024]{2,1,0:T(8,128)(2,1)S(1)}, u32[]{:S(2)}, u32[]{:S(2)}) async-start(bf16[8,192,1024]{2,1,0:T(8,128)(2,1)} %bitcast.14), calls=%async_computation.1 | async-start | bytes 6291456 | tf_op jit(solution)/shard_map/all_to_all | solution.py:246
  24.1 13.0 %collective-permute-start = (bf16[1552,128]{1,0:T(8,128)(2,1)S(1)}, bf16[1552,128]{1,0:T(8,128)(2,1)S(1)}, u32[]{:S(2)}, u32[]{:S(2)}) collective-permute-start(bf16[1552,128]{1,0:T(8,128)(2,1)S(1)} %shard_map.51.refs_0_), channel_id=1, source_target_pairs={{0,16},{16,32},{32,48},{48,64},{64,80},{80,96},{96,112},{112,0},{1... | collective-permute-start | bytes 1191944 | tf_op jit(solution)/shard_map/ppermute | solution.py:25
  25.8 11.3 %collective-permute-start.3 = (bf16[1552,128]{1,0:T(8,128)(2,1)S(1)}, bf16[1552,128]{1,0:T(8,128)(2,1)S(1)}, u32[]{:S(2)}, u32[]{:S(2)}) collective-permute-start(bf16[1552,128]{1,0:T(8,128)(2,1)S(1)} %shard_map.51.refs_0_), channel_id=1, source_target_pairs={{0,112},{16,0},{32,16},{48,32},{64,48},{80,64},{96,80},{112,96},{1... | collective-permute-start | bytes 1191944 | tf_op jit(solution)/shard_map/ppermute | solution.py:25
  37.1 24.4 %copy-start.3 = (bf16[1552,128]{1,0:T(8,128)(2,1)}, bf16[1552,128]{1,0:T(8,128)(2,1)S(1)}, u32[]{:S(2)}) copy-start(bf16[1552,128]{1,0:T(8,128)(2,1)S(1)} %collective-permute-done.refs_2_) | copy-start | bytes 1191940
  37.1 9.1 %collective-permute-start.1 = (bf16[1552,128]{1,0:T(8,128)(2,1)S(1)}, bf16[1552,128]{1,0:T(8,128)(2,1)S(1)}, u32[]{:S(2)}, u32[]{:S(2)}) collective-permute-start(bf16[1552,128]{1,0:T(8,128)(2,1)S(1)} %collective-permute-done.refs_2_), channel_id=1, source_target_pairs={{0,16},{16,32},{32,48},{48,64},{64,80},{80,96},{96,112},{112,0},{1... | collective-permute-start | bytes 1191944 | tf_op jit(solution)/shard_map/ppermute | solution.py:25
  37.1 22.0 %copy-start.4 = (bf16[1552,128]{1,0:T(8,128)(2,1)}, bf16[1552,128]{1,0:T(8,128)(2,1)S(1)}, u32[]{:S(2)}) copy-start(bf16[1552,128]{1,0:T(8,128)(2,1)S(1)} %collective-permute-done.3.refs_3_) | copy-start | bytes 1191940
  37.1 9.1 %collective-permute-start.4 = (bf16[1552,128]{1,0:T(8,128)(2,1)S(1)}, bf16[1552,128]{1,0:T(8,128)(2,1)S(1)}, u32[]{:S(2)}, u32[]{:S(2)}) collective-permute-start(bf16[1552,128]{1,0:T(8,128)(2,1)S(1)} %collective-permute-done.3.refs_3_), channel_id=1, source_target_pairs={{0,112},{16,0},{32,16},{48,32},{64,48},{80,64},{96,80},{112,96},{1... | collective-permute-start | bytes 1191944 | tf_op jit(solution)/shard_map/ppermute | solution.py:25
  39.8 13.4 %collective-permute-start.8 = (bf16[1552,128]{1,0:T(8,128)(2,1)S(1)}, bf16[1552,128]{1,0:T(8,128)(2,1)S(1)}, u32[]{:S(2)}, u32[]{:S(2)}) collective-permute-start(bf16[1552,128]{1,0:T(8,128)(2,1)S(1)} %shard_map.51.refs_0_), channel_id=1, source_target_pairs={{0,8},{8,0},{1,9},{9,1},{2,10},{10,2},{3,11},{11,3},{4,12},{12,4},... | collective-permute-start | bytes 1191944 | tf_op jit(solution)/shard_map/ppermute | solution.py:38
  43.1 10.1 %collective-permute-start.10 = (bf16[1552,128]{1,0:T(8,128)(2,1)S(1)}, bf16[1552,128]{1,0:T(8,128)(2,1)S(1)}, u32[]{:S(2)}, u32[]{:S(2)}) collective-permute-start(bf16[1552,128]{1,0:T(8,128)(2,1)S(1)} %collective-permute-done.3.refs_3_), channel_id=1, source_target_pairs={{0,8},{8,0},{1,9},{9,1},{2,10},{10,2},{3,11},{11,3},{4,12},{12,4},... | collective-permute-start | bytes 1191944 | tf_op jit(solution)/shard_map/ppermute | solution.py:38
  46.2 15.3 %copy-start.5 = (bf16[1552,128]{1,0:T(8,128)(2,1)}, bf16[1552,128]{1,0:T(8,128)(2,1)S(1)}, u32[]{:S(2)}) copy-start(bf16[1552,128]{1,0:T(8,128)(2,1)S(1)} %collective-permute-done.1.refs_6_) | copy-start | bytes 1191940
  46.2 8.2 %collective-permute-start.2 = (bf16[1552,128]{1,0:T(8,128)(2,1)S(1)}, bf16[1552,128]{1,0:T(8,128)(2,1)S(1)}, u32[]{:S(2)}, u32[]{:S(2)}) collective-permute-start(bf16[1552,128]{1,0:T(8,128)(2,1)S(1)} %collective-permute-done.1.refs_6_), channel_id=1, source_target_pairs={{0,16},{16,32},{32,48},{48,64},{64,80},{80,96},{96,112},{112,0},{1... | collective-permute-start | bytes 1191944 | tf_op jit(solution)/shard_map/ppermute | solution.py:25
  46.2 15.3 %copy-start.6 = (bf16[1552,128]{1,0:T(8,128)(2,1)}, bf16[1552,128]{1,0:T(8,128)(2,1)S(1)}, u32[]{:S(2)}) copy-start(bf16[1552,128]{1,0:T(8,128)(2,1)S(1)} %collective-permute-done.4.refs_7_) | copy-start | bytes 1191940
  46.2 12.8 %collective-permute-start.5 = (bf16[1552,128]{1,0:T(8,128)(2,1)S(1)}, bf16[1552,128]{1,0:T(8,128)(2,1)S(1)}, u32[]{:S(2)}, u32[]{:S(2)}) collective-permute-start(bf16[1552,128]{1,0:T(8,128)(2,1)S(1)} %collective-permute-done.4.refs_7_), channel_id=1, source_target_pairs={{0,112},{16,0},{32,16},{48,32},{64,48},{80,64},{96,80},{112,96},{1... | collective-permute-start | bytes 1191944 | tf_op jit(solution)/shard_map/ppermute | solution.py:25
  48.9 10.3 %collective-permute-start.9 = (bf16[1552,128]{1,0:T(8,128)(2,1)S(1)}, bf16[1552,128]{1,0:T(8,128)(2,1)S(1)}, u32[]{:S(2)}, u32[]{:S(2)}) collective-permute-start(bf16[1552,128]{1,0:T(8,128)(2,1)S(1)} %collective-permute-done.refs_2_), channel_id=1, source_target_pairs={{0,8},{8,0},{1,9},{9,1},{2,10},{10,2},{3,11},{11,3},{4,12},{12,4},... | collective-permute-start | bytes 1191944 | tf_op jit(solution)/shard_map/ppermute | solution.py:38
  53.2 5.9 %copy-start.7 = (bf16[1552,128]{1,0:T(8,128)(2,1)}, bf16[1552,128]{1,0:T(8,128)(2,1)S(1)}, u32[]{:S(2)}) copy-start(bf16[1552,128]{1,0:T(8,128)(2,1)S(1)} %collective-permute-done.8.refs_1_) | copy-start | bytes 1191940
  53.2 6.2 %collective-permute-start.11 = (bf16[1552,128]{1,0:T(8,128)(2,1)S(1)}, bf16[1552,128]{1,0:T(8,128)(2,1)S(1)}, u32[]{:S(2)}, u32[]{:S(2)}) collective-permute-start(bf16[1552,128]{1,0:T(8,128)(2,1)S(1)} %collective-permute-done.1.refs_6_), channel_id=1, source_target_pairs={{0,8},{8,0},{1,9},{9,1},{2,10},{10,2},{3,11},{11,3},{4,12},{12,4},... | collective-permute-start | bytes 1191944 | tf_op jit(solution)/shard_map/ppermute | solution.py:38
  53.3 8.2 %collective-permute-start.12 = (bf16[1552,128]{1,0:T(8,128)(2,1)S(1)}, bf16[1552,128]{1,0:T(8,128)(2,1)S(1)}, u32[]{:S(2)}, u32[]{:S(2)}) collective-permute-start(bf16[1552,128]{1,0:T(8,128)(2,1)S(1)} %collective-permute-done.4.refs_7_), channel_id=1, source_target_pairs={{0,8},{8,0},{1,9},{9,1},{2,10},{10,2},{3,11},{11,3},{4,12},{12,4},... | collective-permute-start | bytes 1191944 | tf_op jit(solution)/shard_map/ppermute | solution.py:38
  54.4 7.1 %copy-start.1 = (bf16[1552,128]{1,0:T(8,128)(2,1)}, bf16[1552,128]{1,0:T(8,128)(2,1)S(1)}, u32[]{:S(2)}) copy-start(bf16[1552,128]{1,0:T(8,128)(2,1)S(1)} %collective-permute-done.2.up_ref.refs_10_) | copy-start | bytes 1191940
  54.4 7.0 %collective-permute-start.13 = (bf16[1552,128]{1,0:T(8,128)(2,1)S(1)}, bf16[1552,128]{1,0:T(8,128)(2,1)S(1)}, u32[]{:S(2)}, u32[]{:S(2)}) collective-permute-start(bf16[1552,128]{1,0:T(8,128)(2,1)S(1)} %collective-permute-done.2.up_ref.refs_10_), channel_id=1, source_target_pairs={{0,8},{8,0},{1,9},{9,1},{2,10},{10,2},{3,11},{11,3},{4,12},{12,4},... | collective-permute-start | bytes 1191944 | tf_op jit(solution)/shard_map/ppermute | solution.py:38
  59.1 3.9 %collective-permute-start.14 = (bf16[1552,128]{1,0:T(8,128)(2,1)S(1)}, bf16[1552,128]{1,0:T(8,128)(2,1)}, u32[]{:S(2)}, u32[]{:S(2)}) collective-permute-start(bf16[1552,128]{1,0:T(8,128)(2,1)S(1)} %collective-permute-done.5.down_ref.refs_11_), channel_id=1, source_target_pairs={{0,8},{8,0},{1,9},{9,1},{2,10},{10,2},{3,11},{11,3},{4,12},{12,4},... | collective-permute-start | bytes 1191944 | tf_op jit(solution)/shard_map/ppermute | solution.py:38
  59.2 16.7 %collective-permute-start.6 = (bf16[1552,128]{1,0:T(8,128)(2,1)S(1)}, bf16[1552,128]{1,0:T(8,128)(2,1)}, u32[]{:S(2)}, u32[]{:S(2)}) collective-permute-start(bf16[1552,128]{1,0:T(8,128)(2,1)S(1)} %shard_map.52), channel_id=1, source_target_pairs={{0,112},{8,24},{16,0},{24,40},{32,16},{40,56},{48,32},{56,72},{64,... | collective-permute-start | bytes 1191944 | tf_op jit(solution)/shard_map/ppermute | solution.py:34
  59.3 16.6 %collective-permute-start.7 = (bf16[1552,128]{1,0:T(8,128)(2,1)S(1)}, bf16[1552,128]{1,0:T(8,128)(2,1)}, u32[]{:S(2)}, u32[]{:S(2)}) collective-permute-start(bf16[1552,128]{1,0:T(8,128)(2,1)S(1)} %shard_map.52), channel_id=1, source_target_pairs={{0,120},{8,16},{16,8},{24,32},{32,24},{40,48},{48,40},{56,64},{64,... | collective-permute-start | bytes 1191944 | tf_op jit(solution)/shard_map/ppermute | solution.py:34
  (6 other events, 14.2 us)

commit v5 on v4

--- a/solution.py
+++ b/solution.py
@@ -106,8 +106,8 @@
     for pair in range(pieces // 2):
         two = labels[2 * pair : 2 * pair + 2]
         if first:
-            fetches[2 * pair].wait()
-            fetches[2 * pair + 1].wait()
+            for fetch in {0: fetches[:4], 2: fetches[4:]}.get(pair, []):
+                fetch.wait()
         keys = jnp.concatenate(
             [
                 jnp.concatenate(
@@ -207,7 +207,7 @@
         input_output_aliases={}
         if first or last
         else {pieces + 1: 0, pieces + 2: 1},
-        compiler_params=pltpu.CompilerParams(vmem_limit_bytes=53 * 2**20 if first else need + 8 * 2**20),
+        compiler_params=pltpu.CompilerParams(vmem_limit_bytes=52 * 2**20 if first else need + 8 * 2**20),
         cost_estimate=pl.CostEstimate(
             flops=2 * m * count * (depth + C),
             bytes_accessed=4 * C * count,
@@ -251,7 +251,10 @@
         up, down = along_z(up, 1), along_z(down, -1)
         got += [up, down, swap(up), swap(down)]
     far = move(choose_kernel, up.shape, (up, down))
-    ends = [outward(far, 0), outward(far, 1)]
+    ends = [
+        pltpu.with_memory_space_constraint(outward(far, cross), pltpu.VMEM)
+        for cross in (0, 1)
+    ]
     state = attend(pool, got, None, False)
     log_probs, entropy = attend(pool, ends, state, True)
     return (log_probs.T, entropy[0])

time: 81.9 us -> 80.8 us (0.987)
  Pallas kernels: 20.2 us -> 19.2 us
    pallas_call x2, Pallas kernels: 18.4 us -> 17.3 us  [attend(): pl.pallas_call(functools.partial(attend_kernel, pieces, first, last, 2.0...]
  transfers between devices with their start and end apart: 17 -> 17, of which waited for: 4 -> 4; matrix products, arithmetic and copies ran while one was open for 5% -> 5% of each run, Pallas kernels for 16% -> 15%
where the time goes in v5:
time: 80.8 us; the launch traced here: 80.5 us
  starting transfers between devices  37.4 us (46%)
  Pallas kernels  19.2 us (24%)
  waiting for transfers between devices  17.4 us (22%)
  local copies, waits for them, and re-layouts  5.5 us (7%)
  between operations  1.01 us (1%)
    pallas_call x2, Pallas kernels, attend(): pl.pallas_call(functools.partial(attend_kernel, pieces, first, last, 2.0...  17.3 us
    ppermute x7, starting transfers between devices, swap(): return lax.ppermute(x, 'c', [(0, 1), (1, 0)])  12.9 us
    ppermute x6, waiting for transfers between devices, along_z(): return lax.ppermute(x, 'z', [(i, (i + step) % n) for i in range(n)])  11.1 us
    ppermute x6, starting transfers between devices, along_z(): return lax.ppermute(x, 'z', [(i, (i + step) % n) for i in range(n)])  11.1 us
    all_to_all x1, starting transfers between devices, per_device(): parts = lax.all_to_all(own, PLANE, 0, 0, tiled=True)  7.58 us
    all_to_all x1, waiting for transfers between devices, per_device(): parts = lax.all_to_all(own, PLANE, 0, 0, tiled=True)  6.31 us
    reshape x1, local copies, waits for them, and re-layouts, per_device(): queries = pool_embed.T.reshape(width, feats, count).transpose(1, 0, 2)  3.99 us
    all_to_all x1, starting transfers between devices, per_device(): pool = lax.all_to_all(queries, FEAT, 0, 0, tiled=True)  3.66 us
  transfers between devices with their start and end apart: 17, of which 4 were waited for; matrix products, arithmetic and copies ran while one was open for 5% of the time, Pallas kernels for 15%

profile of v5, /device:TPU:1, one launch (start us, length us, event | category | flops | bytes accessed | tf_op | source)
XLA Modules:
  0.0 80.5 jit_solution(11024169002296455144)
XLA Ops:
  0.6 1.7 %shard_map.50 = bf16[16,64,256]{2,1,0:T(8,128)(2,1)} custom-call(bf16[64,192]{1,0:T(8,128)(2,1)} %label_ref.1, s32[1,64]{1,0:T(1,128)} %bitcast.16), custom_call_target="tpu_custom_call" | custom-call | bytes 1048576 | tf_op jit(solution)/shard_map/pallas_call | solution.py:42
  2.3 7.6 %all-to-all-start = ((bf16[16,64,256]{2,1,0:T(8,128)(2,1)}), bf16[16,64,256]{2,1,0:T(8,128)(2,1)S(1)}, u32[]{:S(2)}, u32[]{:S(2)}) async-start(bf16[16,64,256]{2,1,0:T(8,128)(2,1)} %shard_map.50), calls=%async_computation | async-start | bytes 1048576 | tf_op jit(solution)/shard_map/all_to_all | solution.py:241
  9.9 4.0 %copy.8 = bf16[24,8,8,1024]{3,2,0,1:T(8,128)(2,1)} copy(bf16[24,8,8,1024]{3,2,1,0:T(8,128)(2,1)} %bitcast.15) | data formatting | bytes 6291456 | tf_op jit(solution)/shard_map/reshape | solution.py:243
  13.9 6.3 %all-to-all-done.parts_ref = bf16[16,64,256]{2,1,0:T(8,128)(2,1)S(1)} async-done(((bf16[16,64,256]{2,1,0:T(8,128)(2,1)}), bf16[16,64,256]{2,1,0:T(8,128)(2,1)S(1)}, u32[]{:S(2)}, u32[]{:S(2)}) %all-to-all-start) | async-done | bytes 524320 | tf_op jit(solution)/shard_map/all_to_all | solution.py:241
  20.2 0.2 shard_map.51.refs_0_
  20.4 3.7 %all-to-all-start.1 = ((bf16[8,192,1024]{2,1,0:T(8,128)(2,1)}), bf16[8,192,1024]{2,1,0:T(8,128)(2,1)S(1)}, u32[]{:S(2)}, u32[]{:S(2)}) async-start(bf16[8,192,1024]{2,1,0:T(8,128)(2,1)} %bitcast.14), calls=%async_computation.1 | async-start | bytes 6291456 | tf_op jit(solution)/shard_map/all_to_all | solution.py:246
  24.1 1.7 %collective-permute-start = (bf16[1552,128]{1,0:T(8,128)(2,1)S(1)}, bf16[1552,128]{1,0:T(8,128)(2,1)S(1)}, u32[]{:S(2)}, u32[]{:S(2)}) collective-permute-start(bf16[1552,128]{1,0:T(8,128)(2,1)S(1)} %shard_map.51.refs_0_), channel_id=1, source_target_pairs={{0,16},{16,32},{32,48},{48,64},{64,80},{80,96},{96,112},{112,0},{1... | collective-permute-start | bytes 1191944 | tf_op jit(solution)/shard_map/ppermute | solution.py:25
  25.8 4.0 %collective-permute-start.3 = (bf16[1552,128]{1,0:T(8,128)(2,1)S(1)}, bf16[1552,128]{1,0:T(8,128)(2,1)S(1)}, u32[]{:S(2)}, u32[]{:S(2)}) collective-permute-start(bf16[1552,128]{1,0:T(8,128)(2,1)S(1)} %shard_map.51.refs_0_), channel_id=1, source_target_pairs={{0,112},{16,0},{32,16},{48,32},{64,48},{80,64},{96,80},{112,96},{1... | collective-permute-start | bytes 1191944 | tf_op jit(solution)/shard_map/ppermute | solution.py:25
  29.8 7.3 %collective-permute-done.refs_2_ = bf16[1552,128]{1,0:T(8,128)(2,1)S(1)} collective-permute-done((bf16[1552,128]{1,0:T(8,128)(2,1)S(1)}, bf16[1552,128]{1,0:T(8,128)(2,1)S(1)}, u32[]{:S(2)}, u32[]{:S(2)}) %collective-permute-start) | collective-permute-done | bytes 397344 | tf_op jit(solution)/shard_map/ppermute | solution.py:25
  37.1 2.7 %collective-permute-start.4 = (bf16[1552,128]{1,0:T(8,128)(2,1)S(1)}, bf16[1552,128]{1,0:T(8,128)(2,1)S(1)}, u32[]{:S(2)}, u32[]{:S(2)}) collective-permute-start(bf16[1552,128]{1,0:T(8,128)(2,1)S(1)} %collective-permute-done.3.refs_3_), channel_id=1, source_target_pairs={{0,112},{16,0},{32,16},{48,32},{64,48},{80,64},{96,80},{112,96},{1... | collective-permute-start | bytes 1191944 | tf_op jit(solution)/shard_map/ppermute | solution.py:25
  39.8 3.3 %collective-permute-start.8 = (bf16[1552,128]{1,0:T(8,128)(2,1)S(1)}, bf16[1552,128]{1,0:T(8,128)(2,1)S(1)}, u32[]{:S(2)}, u32[]{:S(2)}) collective-permute-start(bf16[1552,128]{1,0:T(8,128)(2,1)S(1)} %shard_map.51.refs_0_), channel_id=1, source_target_pairs={{0,8},{8,0},{1,9},{9,1},{2,10},{10,2},{3,11},{11,3},{4,12},{12,4},... | collective-permute-start | bytes 1191944 | tf_op jit(solution)/shard_map/ppermute | solution.py:38
  43.1 3.1 %collective-permute-done.1.refs_6_ = bf16[1552,128]{1,0:T(8,128)(2,1)S(1)} collective-permute-done((bf16[1552,128]{1,0:T(8,128)(2,1)S(1)}, bf16[1552,128]{1,0:T(8,128)(2,1)S(1)}, u32[]{:S(2)}, u32[]{:S(2)}) %collective-permute-start.1) | collective-permute-done | bytes 397344 | tf_op jit(solution)/shard_map/ppermute | solution.py:25
  46.2 2.7 %collective-permute-start.5 = (bf16[1552,128]{1,0:T(8,128)(2,1)S(1)}, bf16[1552,128]{1,0:T(8,128)(2,1)S(1)}, u32[]{:S(2)}, u32[]{:S(2)}) collective-permute-start(bf16[1552,128]{1,0:T(8,128)(2,1)S(1)} %collective-permute-done.4.refs_7_), channel_id=1, source_target_pairs={{0,112},{16,0},{32,16},{48,32},{64,48},{80,64},{96,80},{112,96},{1... | collective-permute-start | bytes 1191944 | tf_op jit(solution)/shard_map/ppermute | solution.py:25
  48.9 4.3 %collective-permute-start.9 = (bf16[1552,128]{1,0:T(8,128)(2,1)S(1)}, bf16[1552,128]{1,0:T(8,128)(2,1)S(1)}, u32[]{:S(2)}, u32[]{:S(2)}) collective-permute-start(bf16[1552,128]{1,0:T(8,128)(2,1)S(1)} %collective-permute-done.refs_2_), channel_id=1, source_target_pairs={{0,8},{8,0},{1,9},{9,1},{2,10},{10,2},{3,11},{11,3},{4,12},{12,4},... | collective-permute-start | bytes 1191944 | tf_op jit(solution)/shard_map/ppermute | solution.py:38
  53.2 0.1 collective-permute-start.11
  53.3 0.4 collective-permute-start.12
  53.7 0.7 collective-permute-done.2.up_ref.refs_10_
  54.4 4.6 %collective-permute-start.13 = (bf16[1552,128]{1,0:T(8,128)(2,1)S(1)}, bf16[1552,128]{1,0:T(8,128)(2,1)S(1)}, u32[]{:S(2)}, u32[]{:S(2)}) collective-permute-start(bf16[1552,128]{1,0:T(8,128)(2,1)S(1)} %collective-permute-done.2.up_ref.refs_10_), channel_id=1, source_target_pairs={{0,8},{8,0},{1,9},{9,1},{2,10},{10,2},{3,11},{11,3},{4,12},{12,4},... | collective-permute-start | bytes 1191944 | tf_op jit(solution)/shard_map/ppermute | solution.py:38
  59.1 0.1 collective-permute-start.14
  59.3 2.1 %collective-permute-start.7 = (bf16[1552,128]{1,0:T(8,128)(2,1)S(1)}, bf16[1552,128]{1,0:T(8,128)(2,1)}, u32[]{:S(2)}, u32[]{:S(2)}) collective-permute-start(bf16[1552,128]{1,0:T(8,128)(2,1)S(1)} %shard_map.52), channel_id=1, source_target_pairs={{0,120},{8,16},{16,8},{24,32},{32,24},{40,48},{48,40},{56,64},{64,... | collective-permute-start | bytes 1191944 | tf_op jit(solution)/shard_map/ppermute | solution.py:34
  61.5 0.7 copy-done.11
  62.2 0.8 copy-done.12
  63.0 11.9 %shard_map.53 = (f32[1000,1024]{1,0:T(8,128)S(1)}, f32[2,1024]{1,0:T(2,128)S(1)}) custom-call(bf16[1552,128]{1,0:T(8,128)(2,1)} %copy-done, bf16[1552,128]{1,0:T(8,128)(2,1)} %copy-done.7, bf16[1552,128]{1,0:T(8,128)(2,1)} %copy-done.3, bf16[1552,128]{1,0:T(8,128)(2,1)} %copy-done.4, bf16[1552,128]{1,0:T(8,128)(2,1)} %copy-done.9, ...), custom_call_target="tpu_custom_call" | custom-call | flops 9307160576 | bytes 4096000 | tf_op jit(solution)/shard_map/pallas_call | solution.py:198
  74.9 5.4 %shard_map.54 = (f32[1000,1024]{1,0:T(8,128)}, f32[1,1024]{1,0:T(1,128)}) custom-call(bf16[1552,128]{1,0:T(8,128)(2,1)} %collective-permute-done.6.refs_0_, bf16[1552,128]{1,0:T(8,128)(2,1)} %collective-permute-done.7.refs_1_, bf16[1536,1024]{1,0:T(8,128)(2,1)S(1)} %bitcast.13, f32[1000,1024]{1,0:T(8,128)S(1)} %get-tuple-element.12.refs_3_, ...), custom_call_target="tpu_custom_call" | custom-call | flops 1329594368 | bytes 4096000 | tf_op jit(solution)/shard_map/pallas_call | solution.py:198
  (42 shorter events, 0.2 us)
Async XLA Ops:
  2.3 17.9 %all-to-all-start = ((bf16[16,64,256]{2,1,0:T(8,128)(2,1)}), bf16[16,64,256]{2,1,0:T(8,128)(2,1)S(1)}, u32[]{:S(2)}, u32[]{:S(2)}) async-start(bf16[16,64,256]{2,1,0:T(8,128)(2,1)} %shard_map.50), calls=%async_computation | async-start | bytes 1048576 | tf_op jit(solution)/shard_map/all_to_all | solution.py:241
  20.4 19.4 %copy-start = (bf16[1552,128]{1,0:T(8,128)(2,1)}, bf16[1552,128]{1,0:T(8,128)(2,1)S(1)}, u32[]{:S(2)}) copy-start(bf16[1552,128]{1,0:T(8,128)(2,1)S(1)} %shard_map.51.refs_0_) | copy-start | bytes 1191940
  20.4 42.6 %all-to-all-start.1 = ((bf16[8,192,1024]{2,1,0:T(8,128)(2,1)}), bf16[8,192,1024]{2,1,0:T(8,128)(2,1)S(1)}, u32[]{:S(2)}, u32[]{:S(2)}) async-start(bf16[8,192,1024]{2,1,0:T(8,128)(2,1)} %bitcast.14), calls=%async_computation.1 | async-start | bytes 6291456 | tf_op jit(solution)/shard_map/all_to_all | solution.py:246
  24.1 13.0 %collective-permute-start = (bf16[1552,128]{1,0:T(8,128)(2,1)S(1)}, bf16[1552,128]{1,0:T(8,128)(2,1)S(1)}, u32[]{:S(2)}, u32[]{:S(2)}) collective-permute-start(bf16[1552,128]{1,0:T(8,128)(2,1)S(1)} %shard_map.51.refs_0_), channel_id=1, source_target_pairs={{0,16},{16,32},{32,48},{48,64},{64,80},{80,96},{96,112},{112,0},{1... | collective-permute-start | bytes 1191944 | tf_op jit(solution)/shard_map/ppermute | solution.py:25
  25.8 11.3 %collective-permute-start.3 = (bf16[1552,128]{1,0:T(8,128)(2,1)S(1)}, bf16[1552,128]{1,0:T(8,128)(2,1)S(1)}, u32[]{:S(2)}, u32[]{:S(2)}) collective-permute-start(bf16[1552,128]{1,0:T(8,128)(2,1)S(1)} %shard_map.51.refs_0_), channel_id=1, source_target_pairs={{0,112},{16,0},{32,16},{48,32},{64,48},{80,64},{96,80},{112,96},{1... | collective-permute-start | bytes 1191944 | tf_op jit(solution)/shard_map/ppermute | solution.py:25
  37.1 24.4 %copy-start.3 = (bf16[1552,128]{1,0:T(8,128)(2,1)}, bf16[1552,128]{1,0:T(8,128)(2,1)S(1)}, u32[]{:S(2)}) copy-start(bf16[1552,128]{1,0:T(8,128)(2,1)S(1)} %collective-permute-done.refs_2_) | copy-start | bytes 1191940
  37.1 9.1 %collective-permute-start.1 = (bf16[1552,128]{1,0:T(8,128)(2,1)S(1)}, bf16[1552,128]{1,0:T(8,128)(2,1)S(1)}, u32[]{:S(2)}, u32[]{:S(2)}) collective-permute-start(bf16[1552,128]{1,0:T(8,128)(2,1)S(1)} %collective-permute-done.refs_2_), channel_id=1, source_target_pairs={{0,16},{16,32},{32,48},{48,64},{64,80},{80,96},{96,112},{112,0},{1... | collective-permute-start | bytes 1191944 | tf_op jit(solution)/shard_map/ppermute | solution.py:25
  37.1 22.0 %copy-start.4 = (bf16[1552,128]{1,0:T(8,128)(2,1)}, bf16[1552,128]{1,0:T(8,128)(2,1)S(1)}, u32[]{:S(2)}) copy-start(bf16[1552,128]{1,0:T(8,128)(2,1)S(1)} %collective-permute-done.3.refs_3_) | copy-start | bytes 1191940
  37.1 9.1 %collective-permute-start.4 = (bf16[1552,128]{1,0:T(8,128)(2,1)S(1)}, bf16[1552,128]{1,0:T(8,128)(2,1)S(1)}, u32[]{:S(2)}, u32[]{:S(2)}) collective-permute-start(bf16[1552,128]{1,0:T(8,128)(2,1)S(1)} %collective-permute-done.3.refs_3_), channel_id=1, source_target_pairs={{0,112},{16,0},{32,16},{48,32},{64,48},{80,64},{96,80},{112,96},{1... | collective-permute-start | bytes 1191944 | tf_op jit(solution)/shard_map/ppermute | solution.py:25
  39.8 13.4 %collective-permute-start.8 = (bf16[1552,128]{1,0:T(8,128)(2,1)S(1)}, bf16[1552,128]{1,0:T(8,128)(2,1)S(1)}, u32[]{:S(2)}, u32[]{:S(2)}) collective-permute-start(bf16[1552,128]{1,0:T(8,128)(2,1)S(1)} %shard_map.51.refs_0_), channel_id=1, source_target_pairs={{0,8},{8,0},{1,9},{9,1},{2,10},{10,2},{3,11},{11,3},{4,12},{12,4},... | collective-permute-start | bytes 1191944 | tf_op jit(solution)/shard_map/ppermute | solution.py:38
  43.1 10.1 %collective-permute-start.10 = (bf16[1552,128]{1,0:T(8,128)(2,1)S(1)}, bf16[1552,128]{1,0:T(8,128)(2,1)S(1)}, u32[]{:S(2)}, u32[]{:S(2)}) collective-permute-start(bf16[1552,128]{1,0:T(8,128)(2,1)S(1)} %collective-permute-done.3.refs_3_), channel_id=1, source_target_pairs={{0,8},{8,0},{1,9},{9,1},{2,10},{10,2},{3,11},{11,3},{4,12},{12,4},... | collective-permute-start | bytes 1191944 | tf_op jit(solution)/shard_map/ppermute | solution.py:38
  46.2 15.3 %copy-start.5 = (bf16[1552,128]{1,0:T(8,128)(2,1)}, bf16[1552,128]{1,0:T(8,128)(2,1)S(1)}, u32[]{:S(2)}) copy-start(bf16[1552,128]{1,0:T(8,128)(2,1)S(1)} %collective-permute-done.1.refs_6_) | copy-start | bytes 1191940
  46.2 8.2 %collective-permute-start.2 = (bf16[1552,128]{1,0:T(8,128)(2,1)S(1)}, bf16[1552,128]{1,0:T(8,128)(2,1)S(1)}, u32[]{:S(2)}, u32[]{:S(2)}) collective-permute-start(bf16[1552,128]{1,0:T(8,128)(2,1)S(1)} %collective-permute-done.1.refs_6_), channel_id=1, source_target_pairs={{0,16},{16,32},{32,48},{48,64},{64,80},{80,96},{96,112},{112,0},{1... | collective-permute-start | bytes 1191944 | tf_op jit(solution)/shard_map/ppermute | solution.py:25
  46.2 15.3 %copy-start.6 = (bf16[1552,128]{1,0:T(8,128)(2,1)}, bf16[1552,128]{1,0:T(8,128)(2,1)S(1)}, u32[]{:S(2)}) copy-start(bf16[1552,128]{1,0:T(8,128)(2,1)S(1)} %collective-permute-done.4.refs_7_) | copy-start | bytes 1191940
  46.2 12.8 %collective-permute-start.5 = (bf16[1552,128]{1,0:T(8,128)(2,1)S(1)}, bf16[1552,128]{1,0:T(8,128)(2,1)S(1)}, u32[]{:S(2)}, u32[]{:S(2)}) collective-permute-start(bf16[1552,128]{1,0:T(8,128)(2,1)S(1)} %collective-permute-done.4.refs_7_), channel_id=1, source_target_pairs={{0,112},{16,0},{32,16},{48,32},{64,48},{80,64},{96,80},{112,96},{1... | collective-permute-start | bytes 1191944 | tf_op jit(solution)/shard_map/ppermute | solution.py:25
  48.9 10.3 %collective-permute-start.9 = (bf16[1552,128]{1,0:T(8,128)(2,1)S(1)}, bf16[1552,128]{1,0:T(8,128)(2,1)S(1)}, u32[]{:S(2)}, u32[]{:S(2)}) collective-permute-start(bf16[1552,128]{1,0:T(8,128)(2,1)S(1)} %collective-permute-done.refs_2_), channel_id=1, source_target_pairs={{0,8},{8,0},{1,9},{9,1},{2,10},{10,2},{3,11},{11,3},{4,12},{12,4},... | collective-permute-start | bytes 1191944 | tf_op jit(solution)/shard_map/ppermute | solution.py:38
  53.2 5.9 %copy-start.7 = (bf16[1552,128]{1,0:T(8,128)(2,1)}, bf16[1552,128]{1,0:T(8,128)(2,1)S(1)}, u32[]{:S(2)}) copy-start(bf16[1552,128]{1,0:T(8,128)(2,1)S(1)} %collective-permute-done.8.refs_1_) | copy-start | bytes 1191940
  53.2 6.2 %collective-permute-start.11 = (bf16[1552,128]{1,0:T(8,128)(2,1)S(1)}, bf16[1552,128]{1,0:T(8,128)(2,1)S(1)}, u32[]{:S(2)}, u32[]{:S(2)}) collective-permute-start(bf16[1552,128]{1,0:T(8,128)(2,1)S(1)} %collective-permute-done.1.refs_6_), channel_id=1, source_target_pairs={{0,8},{8,0},{1,9},{9,1},{2,10},{10,2},{3,11},{11,3},{4,12},{12,4},... | collective-permute-start | bytes 1191944 | tf_op jit(solution)/shard_map/ppermute | solution.py:38
  53.3 8.2 %collective-permute-start.12 = (bf16[1552,128]{1,0:T(8,128)(2,1)S(1)}, bf16[1552,128]{1,0:T(8,128)(2,1)S(1)}, u32[]{:S(2)}, u32[]{:S(2)}) collective-permute-start(bf16[1552,128]{1,0:T(8,128)(2,1)S(1)} %collective-permute-done.4.refs_7_), channel_id=1, source_target_pairs={{0,8},{8,0},{1,9},{9,1},{2,10},{10,2},{3,11},{11,3},{4,12},{12,4},... | collective-permute-start | bytes 1191944 | tf_op jit(solution)/shard_map/ppermute | solution.py:38
  54.4 7.1 %copy-start.1 = (bf16[1552,128]{1,0:T(8,128)(2,1)}, bf16[1552,128]{1,0:T(8,128)(2,1)S(1)}, u32[]{:S(2)}) copy-start(bf16[1552,128]{1,0:T(8,128)(2,1)S(1)} %collective-permute-done.2.up_ref.refs_10_) | copy-start | bytes 1191940
  54.4 7.0 %collective-permute-start.13 = (bf16[1552,128]{1,0:T(8,128)(2,1)S(1)}, bf16[1552,128]{1,0:T(8,128)(2,1)S(1)}, u32[]{:S(2)}, u32[]{:S(2)}) collective-permute-start(bf16[1552,128]{1,0:T(8,128)(2,1)S(1)} %collective-permute-done.2.up_ref.refs_10_), channel_id=1, source_target_pairs={{0,8},{8,0},{1,9},{9,1},{2,10},{10,2},{3,11},{11,3},{4,12},{12,4},... | collective-permute-start | bytes 1191944 | tf_op jit(solution)/shard_map/ppermute | solution.py:38
  59.1 3.9 %collective-permute-start.14 = (bf16[1552,128]{1,0:T(8,128)(2,1)S(1)}, bf16[1552,128]{1,0:T(8,128)(2,1)}, u32[]{:S(2)}, u32[]{:S(2)}) collective-permute-start(bf16[1552,128]{1,0:T(8,128)(2,1)S(1)} %collective-permute-done.5.down_ref.refs_11_), channel_id=1, source_target_pairs={{0,8},{8,0},{1,9},{9,1},{2,10},{10,2},{3,11},{11,3},{4,12},{12,4},... | collective-permute-start | bytes 1191944 | tf_op jit(solution)/shard_map/ppermute | solution.py:38
  59.2 15.6 %collective-permute-start.6 = (bf16[1552,128]{1,0:T(8,128)(2,1)S(1)}, bf16[1552,128]{1,0:T(8,128)(2,1)}, u32[]{:S(2)}, u32[]{:S(2)}) collective-permute-start(bf16[1552,128]{1,0:T(8,128)(2,1)S(1)} %shard_map.52), channel_id=1, source_target_pairs={{0,112},{8,24},{16,0},{24,40},{32,16},{40,56},{48,32},{56,72},{64,... | collective-permute-start | bytes 1191944 | tf_op jit(solution)/shard_map/ppermute | solution.py:34
  59.3 15.5 %collective-permute-start.7 = (bf16[1552,128]{1,0:T(8,128)(2,1)S(1)}, bf16[1552,128]{1,0:T(8,128)(2,1)}, u32[]{:S(2)}, u32[]{:S(2)}) collective-permute-start(bf16[1552,128]{1,0:T(8,128)(2,1)S(1)} %shard_map.52), channel_id=1, source_target_pairs={{0,120},{8,16},{16,8},{24,32},{32,24},{40,48},{48,40},{56,64},{64,... | collective-permute-start | bytes 1191944 | tf_op jit(solution)/shard_map/ppermute | solution.py:34
  (6 other events, 14.2 us)

commit v6 on v5

--- a/solution.py
+++ b/solution.py
@@ -133,12 +133,12 @@
     total = None
     for pair in range(pieces // 2):
         at = slice(pair * 2 * rows, (pair + 1) * 2 * rows)
-        block = jnp.exp(scores[at, :] - top)
+        block = jnp.exp2(scores[at, :] - top)
         weights[at, :] = block.astype(jnp.bfloat16)
         part = jnp.sum(block, axis=0, keepdims=True)
         total = part if total is None else total + part
     if not first:
-        fade = jnp.exp(old_stat[0:1] - top)
+        fade = jnp.exp2(old_stat[0:1] - top)
         total = total + fade * old_stat[1:2]
     if last:
         gain = (1.0 - SMOOTHING) / total
@@ -196,7 +196,7 @@
     label_specs = [ANY if first else VMEM] * pieces
     place = jax.ShapeDtypeStruct if last else pltpu.VMEM
     return pl.pallas_call(
-        functools.partial(attend_kernel, pieces, first, last, 2.0 / math.sqrt(depth)),
+        functools.partial(attend_kernel, pieces, first, last, 2.0 * math.log2(math.e) / math.sqrt(depth)),
         in_specs=label_specs + [VMEM] * (len(args) - len(label_specs)),
         out_specs=[ANY if last else VMEM, VMEM],
         out_shape=[

time: 80.8 us -> 80.7 us (level)
  no operation moved by 1% of the time
where the time goes in v6:
time: 80.7 us; the launch traced here: 80.3 us
  starting transfers between devices  37.4 us (46%)
  Pallas kernels  19 us (24%)
  waiting for transfers between devices  17.4 us (22%)
  local copies, waits for them, and re-layouts  5.5 us (7%)
  between operations  1.01 us (1%)
    pallas_call x2, Pallas kernels, attend(): pl.pallas_call(functools.partial(attend_kernel, pieces, first, last, 2.0...  17.1 us
    ppermute x7, starting transfers between devices, swap(): return lax.ppermute(x, 'c', [(0, 1), (1, 0)])  12.9 us
    ppermute x6, waiting for transfers between devices, along_z(): return lax.ppermute(x, 'z', [(i, (i + step) % n) for i in range(n)])  11.1 us
    ppermute x6, starting transfers between devices, along_z(): return lax.ppermute(x, 'z', [(i, (i + step) % n) for i in range(n)])  11.1 us
    all_to_all x1, starting transfers between devices, per_device(): parts = lax.all_to_all(own, PLANE, 0, 0, tiled=True)  7.58 us
    all_to_all x1, waiting for transfers between devices, per_device(): parts = lax.all_to_all(own, PLANE, 0, 0, tiled=True)  6.31 us
    reshape x1, local copies, waits for them, and re-layouts, per_device(): queries = pool_embed.T.reshape(width, feats, count).transpose(1, 0, 2)  3.99 us
    all_to_all x1, starting transfers between devices, per_device(): pool = lax.all_to_all(queries, FEAT, 0, 0, tiled=True)  3.66 us
  transfers between devices with their start and end apart: 17, of which 4 were waited for; matrix products, arithmetic and copies ran while one was open for 5% of the time, Pallas kernels for 15%

profile of v6, /device:TPU:1, one launch (start us, length us, event | category | flops | bytes accessed | tf_op | source)
XLA Modules:
  0.0 80.3 jit_solution(14205884535694734261)
XLA Ops:
  0.6 1.7 %shard_map.50 = bf16[16,64,256]{2,1,0:T(8,128)(2,1)} custom-call(bf16[64,192]{1,0:T(8,128)(2,1)} %label_ref.1, s32[1,64]{1,0:T(1,128)} %bitcast.16), custom_call_target="tpu_custom_call" | custom-call | bytes 1048576 | tf_op jit(solution)/shard_map/pallas_call | solution.py:42
  2.3 7.6 %all-to-all-start = ((bf16[16,64,256]{2,1,0:T(8,128)(2,1)}), bf16[16,64,256]{2,1,0:T(8,128)(2,1)S(1)}, u32[]{:S(2)}, u32[]{:S(2)}) async-start(bf16[16,64,256]{2,1,0:T(8,128)(2,1)} %shard_map.50), calls=%async_computation | async-start | bytes 1048576 | tf_op jit(solution)/shard_map/all_to_all | solution.py:241
  9.9 4.0 %copy.8 = bf16[24,8,8,1024]{3,2,0,1:T(8,128)(2,1)} copy(bf16[24,8,8,1024]{3,2,1,0:T(8,128)(2,1)} %bitcast.15) | data formatting | bytes 6291456 | tf_op jit(solution)/shard_map/reshape | solution.py:243
  13.9 6.3 %all-to-all-done.parts_ref = bf16[16,64,256]{2,1,0:T(8,128)(2,1)S(1)} async-done(((bf16[16,64,256]{2,1,0:T(8,128)(2,1)}), bf16[16,64,256]{2,1,0:T(8,128)(2,1)S(1)}, u32[]{:S(2)}, u32[]{:S(2)}) %all-to-all-start) | async-done | bytes 524320 | tf_op jit(solution)/shard_map/all_to_all | solution.py:241
  20.2 0.2 shard_map.51.refs_0_
  20.4 3.7 %all-to-all-start.1 = ((bf16[8,192,1024]{2,1,0:T(8,128)(2,1)}), bf16[8,192,1024]{2,1,0:T(8,128)(2,1)S(1)}, u32[]{:S(2)}, u32[]{:S(2)}) async-start(bf16[8,192,1024]{2,1,0:T(8,128)(2,1)} %bitcast.14), calls=%async_computation.1 | async-start | bytes 6291456 | tf_op jit(solution)/shard_map/all_to_all | solution.py:246
  24.1 1.7 %collective-permute-start = (bf16[1552,128]{1,0:T(8,128)(2,1)S(1)}, bf16[1552,128]{1,0:T(8,128)(2,1)S(1)}, u32[]{:S(2)}, u32[]{:S(2)}) collective-permute-start(bf16[1552,128]{1,0:T(8,128)(2,1)S(1)} %shard_map.51.refs_0_), channel_id=1, source_target_pairs={{0,16},{16,32},{32,48},{48,64},{64,80},{80,96},{96,112},{112,0},{1... | collective-permute-start | bytes 1191944 | tf_op jit(solution)/shard_map/ppermute | solution.py:25
  25.8 4.0 %collective-permute-start.3 = (bf16[1552,128]{1,0:T(8,128)(2,1)S(1)}, bf16[1552,128]{1,0:T(8,128)(2,1)S(1)}, u32[]{:S(2)}, u32[]{:S(2)}) collective-permute-start(bf16[1552,128]{1,0:T(8,128)(2,1)S(1)} %shard_map.51.refs_0_), channel_id=1, source_target_pairs={{0,112},{16,0},{32,16},{48,32},{64,48},{80,64},{96,80},{112,96},{1... | collective-permute-start | bytes 1191944 | tf_op jit(solution)/shard_map/ppermute | solution.py:25
  29.8 7.3 %collective-permute-done.refs_2_ = bf16[1552,128]{1,0:T(8,128)(2,1)S(1)} collective-permute-done((bf16[1552,128]{1,0:T(8,128)(2,1)S(1)}, bf16[1552,128]{1,0:T(8,128)(2,1)S(1)}, u32[]{:S(2)}, u32[]{:S(2)}) %collective-permute-start) | collective-permute-done | bytes 397344 | tf_op jit(solution)/shard_map/ppermute | solution.py:25
  37.1 2.7 %collective-permute-start.4 = (bf16[1552,128]{1,0:T(8,128)(2,1)S(1)}, bf16[1552,128]{1,0:T(8,128)(2,1)S(1)}, u32[]{:S(2)}, u32[]{:S(2)}) collective-permute-start(bf16[1552,128]{1,0:T(8,128)(2,1)S(1)} %collective-permute-done.3.refs_3_), channel_id=1, source_target_pairs={{0,112},{16,0},{32,16},{48,32},{64,48},{80,64},{96,80},{112,96},{1... | collective-permute-start | bytes 1191944 | tf_op jit(solution)/shard_map/ppermute | solution.py:25
  39.8 3.3 %collective-permute-start.8 = (bf16[1552,128]{1,0:T(8,128)(2,1)S(1)}, bf16[1552,128]{1,0:T(8,128)(2,1)S(1)}, u32[]{:S(2)}, u32[]{:S(2)}) collective-permute-start(bf16[1552,128]{1,0:T(8,128)(2,1)S(1)} %shard_map.51.refs_0_), channel_id=1, source_target_pairs={{0,8},{8,0},{1,9},{9,1},{2,10},{10,2},{3,11},{11,3},{4,12},{12,4},... | collective-permute-start | bytes 1191944 | tf_op jit(solution)/shard_map/ppermute | solution.py:38
  43.1 3.1 %collective-permute-done.1.refs_6_ = bf16[1552,128]{1,0:T(8,128)(2,1)S(1)} collective-permute-done((bf16[1552,128]{1,0:T(8,128)(2,1)S(1)}, bf16[1552,128]{1,0:T(8,128)(2,1)S(1)}, u32[]{:S(2)}, u32[]{:S(2)}) %collective-permute-start.1) | collective-permute-done | bytes 397344 | tf_op jit(solution)/shard_map/ppermute | solution.py:25
  46.2 2.7 %collective-permute-start.5 = (bf16[1552,128]{1,0:T(8,128)(2,1)S(1)}, bf16[1552,128]{1,0:T(8,128)(2,1)S(1)}, u32[]{:S(2)}, u32[]{:S(2)}) collective-permute-start(bf16[1552,128]{1,0:T(8,128)(2,1)S(1)} %collective-permute-done.4.refs_7_), channel_id=1, source_target_pairs={{0,112},{16,0},{32,16},{48,32},{64,48},{80,64},{96,80},{112,96},{1... | collective-permute-start | bytes 1191944 | tf_op jit(solution)/shard_map/ppermute | solution.py:25
  48.9 4.3 %collective-permute-start.9 = (bf16[1552,128]{1,0:T(8,128)(2,1)S(1)}, bf16[1552,128]{1,0:T(8,128)(2,1)S(1)}, u32[]{:S(2)}, u32[]{:S(2)}) collective-permute-start(bf16[1552,128]{1,0:T(8,128)(2,1)S(1)} %collective-permute-done.refs_2_), channel_id=1, source_target_pairs={{0,8},{8,0},{1,9},{9,1},{2,10},{10,2},{3,11},{11,3},{4,12},{12,4},... | collective-permute-start | bytes 1191944 | tf_op jit(solution)/shard_map/ppermute | solution.py:38
  53.2 0.1 collective-permute-start.11
  53.3 0.4 collective-permute-start.12
  53.7 0.7 collective-permute-done.2.up_ref.refs_10_
  54.4 4.6 %collective-permute-start.13 = (bf16[1552,128]{1,0:T(8,128)(2,1)S(1)}, bf16[1552,128]{1,0:T(8,128)(2,1)S(1)}, u32[]{:S(2)}, u32[]{:S(2)}) collective-permute-start(bf16[1552,128]{1,0:T(8,128)(2,1)S(1)} %collective-permute-done.2.up_ref.refs_10_), channel_id=1, source_target_pairs={{0,8},{8,0},{1,9},{9,1},{2,10},{10,2},{3,11},{11,3},{4,12},{12,4},... | collective-permute-start | bytes 1191944 | tf_op jit(solution)/shard_map/ppermute | solution.py:38
  59.1 0.1 collective-permute-start.14
  59.3 2.1 %collective-permute-start.7 = (bf16[1552,128]{1,0:T(8,128)(2,1)S(1)}, bf16[1552,128]{1,0:T(8,128)(2,1)}, u32[]{:S(2)}, u32[]{:S(2)}) collective-permute-start(bf16[1552,128]{1,0:T(8,128)(2,1)S(1)} %shard_map.52), channel_id=1, source_target_pairs={{0,120},{8,16},{16,8},{24,32},{32,24},{40,48},{48,40},{56,64},{64,... | collective-permute-start | bytes 1191944 | tf_op jit(solution)/shard_map/ppermute | solution.py:34
  61.5 0.7 copy-done.11
  62.2 0.8 copy-done.12
  63.0 11.7 %shard_map.53 = (f32[1000,1024]{1,0:T(8,128)S(1)}, f32[2,1024]{1,0:T(2,128)S(1)}) custom-call(bf16[1552,128]{1,0:T(8,128)(2,1)} %copy-done, bf16[1552,128]{1,0:T(8,128)(2,1)} %copy-done.7, bf16[1552,128]{1,0:T(8,128)(2,1)} %copy-done.3, bf16[1552,128]{1,0:T(8,128)(2,1)} %copy-done.4, bf16[1552,128]{1,0:T(8,128)(2,1)} %copy-done.9, ...), custom_call_target="tpu_custom_call" | custom-call | flops 9307160576 | bytes 4096000 | tf_op jit(solution)/shard_map/pallas_call | solution.py:198
  74.7 5.4 %shard_map.54 = (f32[1000,1024]{1,0:T(8,128)}, f32[1,1024]{1,0:T(1,128)}) custom-call(bf16[1552,128]{1,0:T(8,128)(2,1)} %collective-permute-done.6.refs_0_, bf16[1552,128]{1,0:T(8,128)(2,1)} %collective-permute-done.7.refs_1_, bf16[1536,1024]{1,0:T(8,128)(2,1)S(1)} %bitcast.13, f32[1000,1024]{1,0:T(8,128)S(1)} %get-tuple-element.12.refs_3_, ...), custom_call_target="tpu_custom_call" | custom-call | flops 1329594368 | bytes 4096000 | tf_op jit(solution)/shard_map/pallas_call | solution.py:198
  (42 shorter events, 0.2 us)
Async XLA Ops:
  2.3 17.9 %all-to-all-start = ((bf16[16,64,256]{2,1,0:T(8,128)(2,1)}), bf16[16,64,256]{2,1,0:T(8,128)(2,1)S(1)}, u32[]{:S(2)}, u32[]{:S(2)}) async-start(bf16[16,64,256]{2,1,0:T(8,128)(2,1)} %shard_map.50), calls=%async_computation | async-start | bytes 1048576 | tf_op jit(solution)/shard_map/all_to_all | solution.py:241
  20.4 19.4 %copy-start = (bf16[1552,128]{1,0:T(8,128)(2,1)}, bf16[1552,128]{1,0:T(8,128)(2,1)S(1)}, u32[]{:S(2)}) copy-start(bf16[1552,128]{1,0:T(8,128)(2,1)S(1)} %shard_map.51.refs_0_) | copy-start | bytes 1191940
  20.4 42.6 %all-to-all-start.1 = ((bf16[8,192,1024]{2,1,0:T(8,128)(2,1)}), bf16[8,192,1024]{2,1,0:T(8,128)(2,1)S(1)}, u32[]{:S(2)}, u32[]{:S(2)}) async-start(bf16[8,192,1024]{2,1,0:T(8,128)(2,1)} %bitcast.14), calls=%async_computation.1 | async-start | bytes 6291456 | tf_op jit(solution)/shard_map/all_to_all | solution.py:246
  24.1 13.0 %collective-permute-start = (bf16[1552,128]{1,0:T(8,128)(2,1)S(1)}, bf16[1552,128]{1,0:T(8,128)(2,1)S(1)}, u32[]{:S(2)}, u32[]{:S(2)}) collective-permute-start(bf16[1552,128]{1,0:T(8,128)(2,1)S(1)} %shard_map.51.refs_0_), channel_id=1, source_target_pairs={{0,16},{16,32},{32,48},{48,64},{64,80},{80,96},{96,112},{112,0},{1... | collective-permute-start | bytes 1191944 | tf_op jit(solution)/shard_map/ppermute | solution.py:25
  25.8 11.3 %collective-permute-start.3 = (bf16[1552,128]{1,0:T(8,128)(2,1)S(1)}, bf16[1552,128]{1,0:T(8,128)(2,1)S(1)}, u32[]{:S(2)}, u32[]{:S(2)}) collective-permute-start(bf16[1552,128]{1,0:T(8,128)(2,1)S(1)} %shard_map.51.refs_0_), channel_id=1, source_target_pairs={{0,112},{16,0},{32,16},{48,32},{64,48},{80,64},{96,80},{112,96},{1... | collective-permute-start | bytes 1191944 | tf_op jit(solution)/shard_map/ppermute | solution.py:25
  37.1 24.4 %copy-start.3 = (bf16[1552,128]{1,0:T(8,128)(2,1)}, bf16[1552,128]{1,0:T(8,128)(2,1)S(1)}, u32[]{:S(2)}) copy-start(bf16[1552,128]{1,0:T(8,128)(2,1)S(1)} %collective-permute-done.refs_2_) | copy-start | bytes 1191940
  37.1 9.1 %collective-permute-start.1 = (bf16[1552,128]{1,0:T(8,128)(2,1)S(1)}, bf16[1552,128]{1,0:T(8,128)(2,1)S(1)}, u32[]{:S(2)}, u32[]{:S(2)}) collective-permute-start(bf16[1552,128]{1,0:T(8,128)(2,1)S(1)} %collective-permute-done.refs_2_), channel_id=1, source_target_pairs={{0,16},{16,32},{32,48},{48,64},{64,80},{80,96},{96,112},{112,0},{1... | collective-permute-start | bytes 1191944 | tf_op jit(solution)/shard_map/ppermute | solution.py:25
  37.1 22.0 %copy-start.4 = (bf16[1552,128]{1,0:T(8,128)(2,1)}, bf16[1552,128]{1,0:T(8,128)(2,1)S(1)}, u32[]{:S(2)}) copy-start(bf16[1552,128]{1,0:T(8,128)(2,1)S(1)} %collective-permute-done.3.refs_3_) | copy-start | bytes 1191940
  37.1 9.1 %collective-permute-start.4 = (bf16[1552,128]{1,0:T(8,128)(2,1)S(1)}, bf16[1552,128]{1,0:T(8,128)(2,1)S(1)}, u32[]{:S(2)}, u32[]{:S(2)}) collective-permute-start(bf16[1552,128]{1,0:T(8,128)(2,1)S(1)} %collective-permute-done.3.refs_3_), channel_id=1, source_target_pairs={{0,112},{16,0},{32,16},{48,32},{64,48},{80,64},{96,80},{112,96},{1... | collective-permute-start | bytes 1191944 | tf_op jit(solution)/shard_map/ppermute | solution.py:25
  39.8 13.4 %collective-permute-start.8 = (bf16[1552,128]{1,0:T(8,128)(2,1)S(1)}, bf16[1552,128]{1,0:T(8,128)(2,1)S(1)}, u32[]{:S(2)}, u32[]{:S(2)}) collective-permute-start(bf16[1552,128]{1,0:T(8,128)(2,1)S(1)} %shard_map.51.refs_0_), channel_id=1, source_target_pairs={{0,8},{8,0},{1,9},{9,1},{2,10},{10,2},{3,11},{11,3},{4,12},{12,4},... | collective-permute-start | bytes 1191944 | tf_op jit(solution)/shard_map/ppermute | solution.py:38
  43.1 10.1 %collective-permute-start.10 = (bf16[1552,128]{1,0:T(8,128)(2,1)S(1)}, bf16[1552,128]{1,0:T(8,128)(2,1)S(1)}, u32[]{:S(2)}, u32[]{:S(2)}) collective-permute-start(bf16[1552,128]{1,0:T(8,128)(2,1)S(1)} %collective-permute-done.3.refs_3_), channel_id=1, source_target_pairs={{0,8},{8,0},{1,9},{9,1},{2,10},{10,2},{3,11},{11,3},{4,12},{12,4},... | collective-permute-start | bytes 1191944 | tf_op jit(solution)/shard_map/ppermute | solution.py:38
  46.2 15.3 %copy-start.5 = (bf16[1552,128]{1,0:T(8,128)(2,1)}, bf16[1552,128]{1,0:T(8,128)(2,1)S(1)}, u32[]{:S(2)}) copy-start(bf16[1552,128]{1,0:T(8,128)(2,1)S(1)} %collective-permute-done.1.refs_6_) | copy-start | bytes 1191940
  46.2 8.2 %collective-permute-start.2 = (bf16[1552,128]{1,0:T(8,128)(2,1)S(1)}, bf16[1552,128]{1,0:T(8,128)(2,1)S(1)}, u32[]{:S(2)}, u32[]{:S(2)}) collective-permute-start(bf16[1552,128]{1,0:T(8,128)(2,1)S(1)} %collective-permute-done.1.refs_6_), channel_id=1, source_target_pairs={{0,16},{16,32},{32,48},{48,64},{64,80},{80,96},{96,112},{112,0},{1... | collective-permute-start | bytes 1191944 | tf_op jit(solution)/shard_map/ppermute | solution.py:25
  46.2 15.3 %copy-start.6 = (bf16[1552,128]{1,0:T(8,128)(2,1)}, bf16[1552,128]{1,0:T(8,128)(2,1)S(1)}, u32[]{:S(2)}) copy-start(bf16[1552,128]{1,0:T(8,128)(2,1)S(1)} %collective-permute-done.4.refs_7_) | copy-start | bytes 1191940
  46.2 12.8 %collective-permute-start.5 = (bf16[1552,128]{1,0:T(8,128)(2,1)S(1)}, bf16[1552,128]{1,0:T(8,128)(2,1)S(1)}, u32[]{:S(2)}, u32[]{:S(2)}) collective-permute-start(bf16[1552,128]{1,0:T(8,128)(2,1)S(1)} %collective-permute-done.4.refs_7_), channel_id=1, source_target_pairs={{0,112},{16,0},{32,16},{48,32},{64,48},{80,64},{96,80},{112,96},{1... | collective-permute-start | bytes 1191944 | tf_op jit(solution)/shard_map/ppermute | solution.py:25
  48.9 10.3 %collective-permute-start.9 = (bf16[1552,128]{1,0:T(8,128)(2,1)S(1)}, bf16[1552,128]{1,0:T(8,128)(2,1)S(1)}, u32[]{:S(2)}, u32[]{:S(2)}) collective-permute-start(bf16[1552,128]{1,0:T(8,128)(2,1)S(1)} %collective-permute-done.refs_2_), channel_id=1, source_target_pairs={{0,8},{8,0},{1,9},{9,1},{2,10},{10,2},{3,11},{11,3},{4,12},{12,4},... | collective-permute-start | bytes 1191944 | tf_op jit(solution)/shard_map/ppermute | solution.py:38
  53.2 5.9 %copy-start.7 = (bf16[1552,128]{1,0:T(8,128)(2,1)}, bf16[1552,128]{1,0:T(8,128)(2,1)S(1)}, u32[]{:S(2)}) copy-start(bf16[1552,128]{1,0:T(8,128)(2,1)S(1)} %collective-permute-done.8.refs_1_) | copy-start | bytes 1191940
  53.2 6.2 %collective-permute-start.11 = (bf16[1552,128]{1,0:T(8,128)(2,1)S(1)}, bf16[1552,128]{1,0:T(8,128)(2,1)S(1)}, u32[]{:S(2)}, u32[]{:S(2)}) collective-permute-start(bf16[1552,128]{1,0:T(8,128)(2,1)S(1)} %collective-permute-done.1.refs_6_), channel_id=1, source_target_pairs={{0,8},{8,0},{1,9},{9,1},{2,10},{10,2},{3,11},{11,3},{4,12},{12,4},... | collective-permute-start | bytes 1191944 | tf_op jit(solution)/shard_map/ppermute | solution.py:38
  53.3 8.2 %collective-permute-start.12 = (bf16[1552,128]{1,0:T(8,128)(2,1)S(1)}, bf16[1552,128]{1,0:T(8,128)(2,1)S(1)}, u32[]{:S(2)}, u32[]{:S(2)}) collective-permute-start(bf16[1552,128]{1,0:T(8,128)(2,1)S(1)} %collective-permute-done.4.refs_7_), channel_id=1, source_target_pairs={{0,8},{8,0},{1,9},{9,1},{2,10},{10,2},{3,11},{11,3},{4,12},{12,4},... | collective-permute-start | bytes 1191944 | tf_op jit(solution)/shard_map/ppermute | solution.py:38
  54.4 7.1 %copy-start.1 = (bf16[1552,128]{1,0:T(8,128)(2,1)}, bf16[1552,128]{1,0:T(8,128)(2,1)S(1)}, u32[]{:S(2)}) copy-start(bf16[1552,128]{1,0:T(8,128)(2,1)S(1)} %collective-permute-done.2.up_ref.refs_10_) | copy-start | bytes 1191940
  54.4 7.0 %collective-permute-start.13 = (bf16[1552,128]{1,0:T(8,128)(2,1)S(1)}, bf16[1552,128]{1,0:T(8,128)(2,1)S(1)}, u32[]{:S(2)}, u32[]{:S(2)}) collective-permute-start(bf16[1552,128]{1,0:T(8,128)(2,1)S(1)} %collective-permute-done.2.up_ref.refs_10_), channel_id=1, source_target_pairs={{0,8},{8,0},{1,9},{9,1},{2,10},{10,2},{3,11},{11,3},{4,12},{12,4},... | collective-permute-start | bytes 1191944 | tf_op jit(solution)/shard_map/ppermute | solution.py:38
  59.1 3.9 %collective-permute-start.14 = (bf16[1552,128]{1,0:T(8,128)(2,1)S(1)}, bf16[1552,128]{1,0:T(8,128)(2,1)}, u32[]{:S(2)}, u32[]{:S(2)}) collective-permute-start(bf16[1552,128]{1,0:T(8,128)(2,1)S(1)} %collective-permute-done.5.down_ref.refs_11_), channel_id=1, source_target_pairs={{0,8},{8,0},{1,9},{9,1},{2,10},{10,2},{3,11},{11,3},{4,12},{12,4},... | collective-permute-start | bytes 1191944 | tf_op jit(solution)/shard_map/ppermute | solution.py:38
  59.2 15.5 %collective-permute-start.6 = (bf16[1552,128]{1,0:T(8,128)(2,1)S(1)}, bf16[1552,128]{1,0:T(8,128)(2,1)}, u32[]{:S(2)}, u32[]{:S(2)}) collective-permute-start(bf16[1552,128]{1,0:T(8,128)(2,1)S(1)} %shard_map.52), channel_id=1, source_target_pairs={{0,112},{8,24},{16,0},{24,40},{32,16},{40,56},{48,32},{56,72},{64,... | collective-permute-start | bytes 1191944 | tf_op jit(solution)/shard_map/ppermute | solution.py:34
  59.3 15.4 %collective-permute-start.7 = (bf16[1552,128]{1,0:T(8,128)(2,1)S(1)}, bf16[1552,128]{1,0:T(8,128)(2,1)}, u32[]{:S(2)}, u32[]{:S(2)}) collective-permute-start(bf16[1552,128]{1,0:T(8,128)(2,1)S(1)} %shard_map.52), channel_id=1, source_target_pairs={{0,120},{8,16},{16,8},{24,32},{32,24},{40,48},{48,40},{56,64},{64,... | collective-permute-start | bytes 1191944 | tf_op jit(solution)/shard_map/ppermute | solution.py:34
  (6 other events, 14.2 us)
